TPU v7x, 512 devices: a whole 4x4x16 slice. The times are simulated.
512 devices in a mesh: band: 32 (over z_hi, y, x), sector: 16 (over z_lo, core).
Axes of the slice: x: 4, y: 4, z: 16 (z_hi: 2, z_lo: 8; z = z_hi * 8 + z_lo), core: 2. Of those that a mesh axis runs over, the one named last changes fastest.
Arguments:
- feats: bfloat16 [96, 64, 2048], P(None, 'band', 'sector'), may hold values from -6 to 6
- counts: int32 [64, 2048], P('band', 'sector'), may hold values from 0 to 15
- occupancy: int32 [64, 16], P('band', 'sector'), may hold values from 0 to 1, as said below
- window_ids: int32 [2048, 64], P('sector', 'band'), may hold values from 0 to 3, never falling along the last dimension, each value on 1 to 32 neighbouring positions
- w_qkv: bfloat16 [288, 96], replicated, may hold values from -1.1 to 1.15
- w_out: bfloat16 [96, 96], replicated, may hold values from -0.625 to 0.625
- conv_weight: bfloat16 [27, 96, 96], replicated, may hold values from -0.125 to 0.125
- cotangent: bfloat16 [96, 64, 2048], P(None, 'band', 'sector'), may hold values from -6 to 6
Outputs:
- section_out: bfloat16 [96, 64, 2048], P(None, 'band', 'sector')
- grad_weight: float32 [27, 96, 96], replicated
- grad_mid: bfloat16 [96, 64, 2048], P(None, 'band', 'sector')
Inputs may be any that keep to these rules, and one draw needn't show every extreme that they name: `window_ids`: window numbers never fall along a ray; each window holds 1 to 32 cells. `occupancy`: tiles near the sensor are occupied more often.
All inputs are finite; a program needn't handle non-finite values.
Results may differ from a plain program's by a relative error of at most 0.008.
Values may be sent and summed in bfloat16 or wider, within the bound.
No kernel may reach another device: no remote copies, remote signals or barrier semaphores. Data moves between devices by JAX's collectives and lax.ppermute only.
A program may use at most 64 MiB of HBM per device.

v0:
```python
import jax
import jax.numpy as jnp
from jax import lax
from jax.sharding import PartitionSpec as P

HEAD_DIM = 16
INC = 32


def extended(cells, sides, width, closed):
    for axis, dim in sides:
        count = lax.axis_size(axis)
        ends = count if closed else count - 1
        head = lax.slice_in_dim(cells, 0, width, axis=dim)
        tail = lax.slice_in_dim(cells, cells.shape[dim] - width, cells.shape[dim], axis=dim)
        cells = jnp.concatenate(
            [
                lax.ppermute(tail, axis, [(i, (i + 1) % count) for i in range(ends)]),
                cells,
                lax.ppermute(head, axis, [((i + 1) % count, i) for i in range(ends)]),
            ],
            axis=dim,
        )
    return cells


def ray_attention(query, key, value, allowed):

    def one_head(items):
        head_query, head_key, head_value = items
        score = (
            jnp.einsum("crd,ckd->crk", head_query, head_key, preferred_element_type=jnp.float32)
            * 0.25
        )
        score = jnp.where(allowed, score, -jnp.inf)
        top = jnp.max(score, axis=2, keepdims=True)
        weight = jnp.exp(score - top)
        total = jnp.sum(weight, axis=2)
        summed = jnp.einsum("crk,ckd->crd", weight, head_value.astype(jnp.float32))
        return (summed / total[..., None]).astype(jnp.bfloat16)

    return lax.map(one_head, (query, key, value))


def shards(feats, counts, occupancy, window_ids, w_qkv, w_out, conv_weight, cotangent):
    chans, rows, cells = feats.shape
    heads = chans // HEAD_DIM
    scale = jnp.log(2.0 + counts.astype(jnp.float32))
    scaled = feats.astype(jnp.float32) * scale[None]
    normed = (scaled * lax.rsqrt(jnp.mean(scaled * scaled, axis=0, keepdims=True) + 1e-05)).astype(
        jnp.bfloat16
    )
    ids = window_ids.T
    occ_cells = jnp.repeat(occupancy, 128, axis=1)
    tags = jnp.where(occ_cells == 1, ids, -1)
    rays = lax.all_to_all(normed, "band", split_axis=2, concat_axis=1, tiled=True)
    meta = lax.all_to_all(jnp.stack([ids, tags]), "band", split_axis=2, concat_axis=1, tiled=True)
    full_rows, narrow = (rays.shape[1], rays.shape[2])
    qkv = jnp.dot(w_qkv, rays.reshape(chans, -1), preferred_element_type=jnp.float32).astype(
        jnp.bfloat16
    )
    qkv = qkv.reshape(3, heads, HEAD_DIM, full_rows, narrow).transpose(0, 1, 4, 3, 2)
    ray_ids = meta[0].T
    ray_tags = meta[1].T
    positions = jnp.arange(full_rows, dtype=jnp.int32)
    allowed = (ray_tags[:, None, :] == ray_ids[:, :, None]) | (
        positions[:, None] == positions[None, :]
    )[None]
    ray_out = ray_attention(qkv[0], qkv[1], qkv[2], allowed)
    ray_out = ray_out.transpose(0, 3, 2, 1).reshape(chans, full_rows, narrow)
    attn = lax.all_to_all(ray_out, "band", split_axis=1, concat_axis=2, tiled=True).reshape(
        chans, -1
    )
    mid = (
        scaled.reshape(chans, -1) + jnp.dot(w_out, attn, preferred_element_type=jnp.float32)
    ).astype(jnp.bfloat16)
    azimuths = cells // INC
    both = jnp.stack(
        [mid.reshape(chans, rows, azimuths, INC), cotangent.reshape(chans, rows, azimuths, INC)]
    )
    both = extended(both, (("sector", 3),), 1, True)
    both = extended(both, (("band", 2),), 1, False)
    both = jnp.pad(both, ((0, 0), (0, 0), (0, 0), (0, 0), (1, 1)))
    mid_pad = both[0]
    cot_pad = both[1]
    cot_flat = cotangent.reshape(chans, -1)
    out = jnp.zeros((chans, rows * cells), jnp.float32)
    back = jnp.zeros((chans, rows * cells), jnp.float32)
    grads = []
    for tap in range(27):
        dr, da, di = (tap // 9, tap // 3 % 3, tap % 3)
        patch = mid_pad[:, dr : dr + rows, da : da + azimuths, di : di + INC].reshape(chans, -1)
        out = out + jnp.dot(conv_weight[tap], patch, preferred_element_type=jnp.float32)
        grads.append(
            lax.dot_general(
                cot_flat, patch, (((1,), (1,)), ((), ())), preferred_element_type=jnp.float32
            )
        )
        cpatch = cot_pad[
            :, 2 - dr : 2 - dr + rows, 2 - da : 2 - da + azimuths, 2 - di : 2 - di + INC
        ].reshape(chans, -1)
        back = back + jnp.dot(conv_weight[tap].T, cpatch, preferred_element_type=jnp.float32)
    grad_weight = lax.psum(jnp.stack(grads), ("band", "sector"))
    section_out = out.astype(jnp.bfloat16).reshape(chans, rows, cells)
    grad_mid = back.astype(jnp.bfloat16).reshape(chans, rows, cells)
    return (section_out, grad_weight, grad_mid)


def solution(mesh):
    in_specs = (
        P(None, "band", "sector"),
        P("band", "sector"),
        P("band", "sector"),
        P("sector", "band"),
        P(),
        P(),
        P(),
        P(None, "band", "sector"),
    )
    out_specs = (P(None, "band", "sector"), P(), P(None, "band", "sector"))
    return jax.shard_map(shards, mesh=mesh, in_specs=in_specs, out_specs=out_specs, check_vma=False)
```

profile of v0, /device:TPU:1, one launch (start us, length us, event | category | flops | bytes accessed | tf_op | source)
XLA Modules:
  0.0 638.3 jit_solution(7138135910772922258)
XLA Ops:
  7.2 0.7 compare_bitcast_fusion
  7.9 0.7 fusion.216
  8.6 0.7 pad_add_fusion
  9.3 0.8 copy.126
  10.1 21.1 %all-to-all-start.1 = ((s32[2,2,128]{1,0,2:T(2,128)}), s32[2,2,128]{1,0,2:T(2,128)S(1)}, u32[]{:S(2)}, u32[]{:S(2)}) async-start(s32[2,2,128]{1,0,2:T(2,128)} %copy.126), calls=%async_computation.1 | async-start | bytes 262144 | tf_op jit(solution)/shard_map/all_to_all | solution.py:57
  31.2 0.7 add_log_fusion
  31.9 0.8 multiply_reduce_fusion
  32.8 0.8 fusion.78
  33.6 0.7 copy.122
  34.4 13.0 %all-to-all-done.1 = s32[2,2,128]{1,0,2:T(2,128)S(1)} async-done(((s32[2,2,128]{1,0,2:T(2,128)}), s32[2,2,128]{1,0,2:T(2,128)S(1)}, u32[]{:S(2)}, u32[]{:S(2)}) %all-to-all-start.1) | async-done | bytes 2080 | tf_op jit(solution)/shard_map/all_to_all | solution.py:57
  47.4 3.9 all-to-all-start
  51.2 0.5 copy.143
  52.0 15.2 %all-to-all-done = bf16[96,2,128]{0,1,2:T(2,128)(2,1)S(1)} async-done(((bf16[96,2,128]{0,1,2:T(2,128)(2,1)}), bf16[96,2,128]{0,1,2:T(2,128)(2,1)S(1)}, u32[]{:S(2)}, u32[]{:S(2)}) %all-to-all-start) | async-done | bytes 49184 | tf_op jit(solution)/shard_map/all_to_all | solution.py:56
  67.5 0.9 reshape.231
  68.7 0.5 copy.132
  69.2 0.5 copy.131
  69.6 0.5 copy.130
  70.1 2.8 while.11
  72.9 0.7 copy.136
  73.6 3.9 all-to-all-start.2
  77.7 15.8 %all-to-all-done.2 = bf16[96,64,4]{0,2,1:T(4,128)(2,1)S(1)} async-done(((bf16[96,64,4]{0,2,1:T(4,128)(2,1)}), bf16[96,64,4]{0,2,1:T(4,128)(2,1)S(1)}, u32[]{:S(2)}, u32[]{:S(2)}) %all-to-all-start.2) | async-done | bytes 49184 | tf_op jit(solution)/shard_map/all_to_all | solution.py:71
  93.9 10.5 %collective-permute-start = (bf16[2,96,2,1,32]{1,4,3,2,0:T(8,128)(2,1)S(1)}, bf16[2,96,2,1,32]{1,4,3,2,0:T(8,128)(2,1)S(1)}, u32[]{:S(2)}, u32[]{:S(2)}) collective-permute-start(bf16[2,96,2,1,32]{1,4,3,2,0:T(8,128)(2,1)S(1)} %get-tuple-element.205), channel_id=1, source_target_pairs={{0,1},{1,2},{2,3},{3,4},{4,5},{5,6},{6,7},{7,8},{8,9},{9,10},{10,1... | collective-permute-start | bytes 73736 | tf_op jit(solution)/shard_map/ppermute | solution.py:18
  104.4 1.9 collective-permute-start.1
  106.4 3.4 collective-permute-done.1
  109.9 2.2 collective-permute-start.2
  112.1 1.3 collective-permute-start.3
  113.4 0.3 collective-permute-done.2
  113.7 3.7 collective-permute-done.3
  117.9 0.9 fusion.246
  118.8 0.7 fusion.245
  119.5 0.4 copy-done.2
  120.8 0.9 convolution_add_fusion.30
  121.9 0.9 convolution_add_fusion.29
  123.0 0.9 convolution_add_fusion.28
  124.1 0.9 convolution_add_fusion.27
  125.2 0.9 convolution_add_fusion.26
  126.3 0.9 convolution_add_fusion.25
  127.4 0.9 convolution_add_fusion.24
  128.4 0.9 convolution_add_fusion.23
  129.5 0.9 convolution_add_fusion.22
  130.6 0.9 convolution_add_fusion.21
  131.7 0.9 convolution_add_fusion.20
  132.8 0.9 convolution_add_fusion.19
  133.9 0.9 convolution_add_fusion.18
  135.0 0.9 convolution_add_fusion.17
  136.4 0.9 fusion.37
  137.5 0.9 fusion.36
  138.6 0.9 fusion.35
  139.7 0.9 fusion.34
  140.8 0.9 fusion.33
  141.9 0.9 fusion.32
  143.0 0.9 fusion.31
  144.1 0.9 fusion.30
  145.2 0.9 fusion.29
  146.5 1.1 copy-done.3
  147.6 1.1 convolution_add_fusion.15
  148.7 1.0 convolution_add_fusion.14
  149.7 1.0 convolution_add_fusion.13
  150.8 1.0 convolution_add_fusion.12
  151.8 1.0 convolution_add_fusion.11
  157.2 0.6 reshape.262
  158.2 0.6 reshape.291
  158.9 469.7 %all-reduce.3.cloned.1.call-done = f32[27,96,96]{1,2,0:T(8,128)} async-done(((f32[27,96,96]{1,2,0:T(8,128)}), f32[27,96,96]{1,2,0:T(8,128)}) %all-reduce.3.cloned.1.call-update) | async-done | bytes 995344 | tf_op jit(solution)/shard_map/psum | solution.py:103
  628.6 2.8 copy.141
  (113 shorter events, 14.7 us)
Async XLA Ops:
  7.2 60.0 %copy-start = (bf16[288,96]{1,0:T(8,128)(2,1)S(1)}, bf16[288,96]{1,0:T(8,128)(2,1)}, u32[]{:S(2)}) copy-start(bf16[288,96]{1,0:T(8,128)(2,1)} %param.14) | copy-start | bytes 165892
  10.1 37.2 %all-to-all-start.1 = ((s32[2,2,128]{1,0,2:T(2,128)}), s32[2,2,128]{1,0,2:T(2,128)S(1)}, u32[]{:S(2)}, u32[]{:S(2)}) async-start(s32[2,2,128]{1,0,2:T(2,128)} %copy.126), calls=%async_computation.1 | async-start | bytes 262144 | tf_op jit(solution)/shard_map/all_to_all | solution.py:57
  47.4 19.8 %all-to-all-start = ((bf16[96,2,128]{0,1,2:T(2,128)(2,1)}), bf16[96,2,128]{0,1,2:T(2,128)(2,1)S(1)}, u32[]{:S(2)}, u32[]{:S(2)}) async-start(bf16[96,2,128]{0,1,2:T(2,128)(2,1)} %copy.122), calls=%async_computation | async-start | bytes 131072 | tf_op jit(solution)/shard_map/all_to_all | solution.py:56
  70.1 7.4 %copy-start.1 = (bf16[96,2,128]{2,1,0:T(2,128)(2,1)S(1)}, bf16[96,2,128]{2,1,0:T(2,128)(2,1)}, u32[]{:S(2)}) copy-start(bf16[96,2,128]{2,1,0:T(2,128)(2,1)} %param.17) | copy-start | bytes 147460
  70.1 23.5 %copy-start.7 = (bf16[96,96]{1,0:T(8,128)(2,1)S(1)}, bf16[96,96]{1,0:T(8,128)(2,1)}, u32[]{:S(2)}) copy-start(bf16[96,96]{1,0:T(8,128)(2,1)} %param.15) | copy-start | bytes 55300
  73.6 19.9 %all-to-all-start.2 = ((bf16[96,64,4]{0,2,1:T(4,128)(2,1)}), bf16[96,64,4]{0,2,1:T(4,128)(2,1)S(1)}, u32[]{:S(2)}, u32[]{:S(2)}) async-start(bf16[96,64,4]{0,2,1:T(4,128)(2,1)} %copy.136), calls=%async_computation.2 | async-start | bytes 131072 | tf_op jit(solution)/shard_map/all_to_all | solution.py:71
  77.5 551.1 %all-reduce.3.cloned.1.call-start = ((), (), s32[]{:S(2)}) async-start(), calls=%async_computation.3 | async-start | bytes 2654208 | tf_op jit(solution)/shard_map/psum | solution.py:103
  93.9 12.5 %collective-permute-start = (bf16[2,96,2,1,32]{1,4,3,2,0:T(8,128)(2,1)S(1)}, bf16[2,96,2,1,32]{1,4,3,2,0:T(8,128)(2,1)S(1)}, u32[]{:S(2)}, u32[]{:S(2)}) collective-permute-start(bf16[2,96,2,1,32]{1,4,3,2,0:T(8,128)(2,1)S(1)} %get-tuple-element.205), channel_id=1, source_target_pairs={{0,1},{1,2},{2,3},{3,4},{4,5},{5,6},{6,7},{7,8},{8,9},{9,10},{10,1... | collective-permute-start | bytes 73736 | tf_op jit(solution)/shard_map/ppermute | solution.py:18
  104.4 5.4 collective-permute-start.1
  109.9 3.8 collective-permute-start.2
  112.1 5.4 collective-permute-start.3
  118.8 1.1 copy-start.2
  146.5 1.1 copy-start.3
  147.5 5.3 copy-start.6
  147.6 5.6 copy-start.5
  147.6 5.8 copy-start.4
Sparse Core Ops, SparseCore 0:
  147.7 480.8 all-reduce.2
where the time goes:
time: 641 us; the launch traced here: 638 us
  waiting for transfers between devices  521 us (81%)
  starting transfers between devices  44.8 us (7%)
  matrix products  38.7 us (6%)
  between operations  14.9 us (2%)
  local copies, waits for them, and re-layouts  13.5 us (2%)
    psum x1, waiting for transfers between devices, shards(): grad_weight = lax.psum(jnp.stack(grads), ('band', 'sector'))  470 us
    dot_general x27, matrix products, shards(): jnp.dot(conv_weight[tap], patch, preferred_element_type=jnp.float32)  21.2 us
    all_to_all x1, starting transfers between devices, shards(): lax.all_to_all(jnp.stack([ids, tags]), 'band', split_axis=2, concat_axis=...  21.1 us
    all_to_all x1, waiting for transfers between devices, shards(): lax.all_to_all(ray_out, 'band', split_axis=1, concat_axis=2, tiled=True)  15.8 us
    all_to_all x1, waiting for transfers between devices, shards(): lax.all_to_all(normed, 'band', split_axis=2, concat_axis=1, tiled=True)  15.2 us
    all_to_all x1, waiting for transfers between devices, shards(): lax.all_to_all(jnp.stack([ids, tags]), 'band', split_axis=2, concat_axis=...  13 us
  transfers between devices with their start and end apart: 8, of which 7 were waited for; matrix products, arithmetic and copies ran while one was open for 2% of the time, Pallas kernels for 0%

commit v1 on v0

--- a/solution.py
+++ b/solution.py
@@ -1,10 +1,30 @@
 import jax
 import jax.numpy as jnp
 from jax import lax
+from jax.sharding import Mesh
 from jax.sharding import PartitionSpec as P
 
 HEAD_DIM = 16
 INC = 32
+BAND = ("zh", "y", "x")
+SECTOR = ("zl", "c")
+PLANE = ("y", "x", "c")
+RING = ("zh", "zl")
+
+
+def all_sum(terms):
+    plane, ring = lax.axis_size(PLANE), lax.axis_size(RING)
+    shape, size = terms.shape, terms.size
+    row = -(-size // (plane * 16 * 128)) * 16
+    flat = jnp.pad(terms.reshape(-1).astype(jnp.bfloat16), (0, plane * row * 128 - size))
+    got = lax.all_to_all(flat.reshape(plane, row, 128), PLANE, 0, 0, tiled=True)
+    mine = jnp.sum(got.astype(jnp.float32), 0).astype(jnp.bfloat16)
+    got = lax.all_to_all(jnp.broadcast_to(mine[None], (ring,) + mine.shape), RING, 0, 0, tiled=True)
+    mine = jnp.sum(got.astype(jnp.float32), 0).astype(jnp.bfloat16)
+    got = lax.all_to_all(
+        jnp.broadcast_to(mine[None], (plane,) + mine.shape), PLANE, 0, 0, tiled=True
+    )
+    return got.reshape(-1)[:size].reshape(shape).astype(jnp.float32)
 
 
 def extended(cells, sides, width, closed):
@@ -53,8 +73,8 @@
     ids = window_ids.T
     occ_cells = jnp.repeat(occupancy, 128, axis=1)
     tags = jnp.where(occ_cells == 1, ids, -1)
-    rays = lax.all_to_all(normed, "band", split_axis=2, concat_axis=1, tiled=True)
-    meta = lax.all_to_all(jnp.stack([ids, tags]), "band", split_axis=2, concat_axis=1, tiled=True)
+    rays = lax.all_to_all(normed, BAND, split_axis=2, concat_axis=1, tiled=True)
+    meta = lax.all_to_all(jnp.stack([ids, tags]), BAND, split_axis=2, concat_axis=1, tiled=True)
     full_rows, narrow = (rays.shape[1], rays.shape[2])
     qkv = jnp.dot(w_qkv, rays.reshape(chans, -1), preferred_element_type=jnp.float32).astype(
         jnp.bfloat16
@@ -68,7 +88,7 @@
     )[None]
     ray_out = ray_attention(qkv[0], qkv[1], qkv[2], allowed)
     ray_out = ray_out.transpose(0, 3, 2, 1).reshape(chans, full_rows, narrow)
-    attn = lax.all_to_all(ray_out, "band", split_axis=1, concat_axis=2, tiled=True).reshape(
+    attn = lax.all_to_all(ray_out, BAND, split_axis=1, concat_axis=2, tiled=True).reshape(
         chans, -1
     )
     mid = (
@@ -78,8 +98,8 @@
     both = jnp.stack(
         [mid.reshape(chans, rows, azimuths, INC), cotangent.reshape(chans, rows, azimuths, INC)]
     )
-    both = extended(both, (("sector", 3),), 1, True)
-    both = extended(both, (("band", 2),), 1, False)
+    both = extended(both, ((SECTOR, 3),), 1, True)
+    both = extended(both, ((BAND, 2),), 1, False)
     both = jnp.pad(both, ((0, 0), (0, 0), (0, 0), (0, 0), (1, 1)))
     mid_pad = both[0]
     cot_pad = both[1]
@@ -100,22 +120,23 @@
             :, 2 - dr : 2 - dr + rows, 2 - da : 2 - da + azimuths, 2 - di : 2 - di + INC
         ].reshape(chans, -1)
         back = back + jnp.dot(conv_weight[tap].T, cpatch, preferred_element_type=jnp.float32)
-    grad_weight = lax.psum(jnp.stack(grads), ("band", "sector"))
+    grad_weight = all_sum(jnp.stack(grads))
     section_out = out.astype(jnp.bfloat16).reshape(chans, rows, cells)
     grad_mid = back.astype(jnp.bfloat16).reshape(chans, rows, cells)
     return (section_out, grad_weight, grad_mid)
 
 
 def solution(mesh):
+    mesh = Mesh(mesh.devices.reshape(2, 4, 4, 8, 2), BAND + SECTOR)
     in_specs = (
-        P(None, "band", "sector"),
-        P("band", "sector"),
-        P("band", "sector"),
-        P("sector", "band"),
+        P(None, BAND, SECTOR),
+        P(BAND, SECTOR),
+        P(BAND, SECTOR),
+        P(SECTOR, BAND),
         P(),
         P(),
         P(),
-        P(None, "band", "sector"),
+        P(None, BAND, SECTOR),
     )
-    out_specs = (P(None, "band", "sector"), P(), P(None, "band", "sector"))
+    out_specs = (P(None, BAND, SECTOR), P(), P(None, BAND, SECTOR))
     return jax.shard_map(shards, mesh=mesh, in_specs=in_specs, out_specs=out_specs, check_vma=False)

time: 641 us -> 224 us (0.35)
  waiting for transfers between devices: 521 us -> 81.4 us
  starting transfers between devices: 44.8 us -> 84.6 us
  between operations: 14.9 us -> 1.51 us
    psum x1 -> x0, waiting for transfers between devices: 470 us -> none  [shards(): grad_weight = lax.psum(jnp.stack(grads), ('band', 'sector'))]
    all_to_all x3 -> x6, starting transfers between devices: 28.8 us -> 68.6 us  [the longest x1 22.9 us: all_sum(): got = lax.all_to_all(flat.reshape(plane, row, 128), PLANE, 0, 0, tiled=True)]
    all_to_all x3 -> x6, waiting for transfers between devices: 44 us -> 73.9 us  [the longest x1 15.9 us: shards(): lax.all_to_all(ray_out, BAND, split_axis=1, concat_axis=2, tiled=True)]
  transfers between devices with their start and end apart: 8 -> 10, of which waited for: 7 -> 9; matrix products, arithmetic and copies ran while one was open for 2% -> 5% of each run, Pallas kernels for 0% -> 0%
where the time goes in v1:
time: 224 us; the launch traced here: 222 us
  starting transfers between devices  84.6 us (38%)
  waiting for transfers between devices  81.4 us (36%)
  matrix products  34.1 us (15%)
  local copies, waits for them, and re-layouts  14.9 us (7%)
  other arithmetic  5.22 us (2%)
    all_to_all x1, starting transfers between devices, all_sum(): got = lax.all_to_all(flat.reshape(plane, row, 128), PLANE, 0, 0, tiled=True)  22.9 us
    all_to_all x1, starting transfers between devices, shards(): lax.all_to_all(jnp.stack([ids, tags]), BAND, split_axis=2, concat_axis=1,...  21.1 us
    dot_general x27, matrix products, shards(): jnp.dot(conv_weight[tap], patch, preferred_element_type=jnp.float32)  20.6 us
    all_to_all x1, waiting for transfers between devices, shards(): lax.all_to_all(ray_out, BAND, split_axis=1, concat_axis=2, tiled=True)  15.9 us
    all_to_all x1, waiting for transfers between devices, shards(): rays = lax.all_to_all(normed, BAND, split_axis=2, concat_axis=1, tiled=True)  15.2 us
    all_to_all x1, waiting for transfers between devices, shards(): lax.all_to_all(jnp.stack([ids, tags]), BAND, split_axis=2, concat_axis=1,...  13 us
    all_to_all x1, waiting for transfers between devices, all_sum(): lax.all_to_all(jnp.broadcast_to(mine[None], (ring,) + mine.shape), RING,...  12.7 us
    ppermute x2, starting transfers between devices, extended(): lax.ppermute(tail, axis, [(i, (i + 1) % count) for i in range(ends)])  12.7 us
  transfers between devices with their start and end apart: 10, of which 9 were waited for; matrix products, arithmetic and copies ran while one was open for 5% of the time, Pallas kernels for 0%

profile of v1, /device:TPU:1, one launch (start us, length us, event | category | flops | bytes accessed | tf_op | source)
XLA Modules:
  0.0 221.8 jit_solution(2176059497303119408)
XLA Ops:
  0.6 0.7 compare_bitcast_fusion
  1.3 0.7 fusion.243
  2.1 0.7 pad_add_fusion
  2.8 0.8 copy.148
  3.6 21.1 %all-to-all-start.1 = ((s32[2,2,128]{1,0,2:T(2,128)}), s32[2,2,128]{1,0,2:T(2,128)S(1)}, u32[]{:S(2)}, u32[]{:S(2)}) async-start(s32[2,2,128]{1,0,2:T(2,128)} %copy.148), calls=%async_computation.1 | async-start | bytes 262144 | tf_op jit(solution)/shard_map/all_to_all | solution.py:77
  24.7 0.7 add_log_fusion
  25.4 0.8 multiply_reduce_fusion
  26.2 0.8 fusion.105
  27.1 0.8 copy.144
  27.8 13.0 %all-to-all-done.1 = s32[2,2,128]{1,0,2:T(2,128)S(1)} async-done(((s32[2,2,128]{1,0,2:T(2,128)}), s32[2,2,128]{1,0,2:T(2,128)S(1)}, u32[]{:S(2)}, u32[]{:S(2)}) %all-to-all-start.1) | async-done | bytes 2080 | tf_op jit(solution)/shard_map/all_to_all | solution.py:77
  40.8 3.8 %all-to-all-start = ((bf16[96,2,128]{0,1,2:T(2,128)(2,1)}), bf16[96,2,128]{0,1,2:T(2,128)(2,1)S(1)}, u32[]{:S(2)}, u32[]{:S(2)}) async-start(bf16[96,2,128]{0,1,2:T(2,128)(2,1)} %copy.144), calls=%async_computation | async-start | bytes 131072 | tf_op jit(solution)/shard_map/all_to_all | solution.py:76
  44.6 0.5 copy.165
  45.4 15.2 %all-to-all-done = bf16[96,2,128]{0,1,2:T(2,128)(2,1)S(1)} async-done(((bf16[96,2,128]{0,1,2:T(2,128)(2,1)}), bf16[96,2,128]{0,1,2:T(2,128)(2,1)S(1)}, u32[]{:S(2)}, u32[]{:S(2)}) %all-to-all-start) | async-done | bytes 49184 | tf_op jit(solution)/shard_map/all_to_all | solution.py:76
  61.0 0.9 reshape.244
  62.1 0.5 copy.154
  62.6 0.5 copy.153
  63.1 0.5 copy.152
  63.6 2.8 %while.11 = (s32[]{:T(128)}, bf16[6,4,64,16]{2,3,1,0:T(8,128)(2,1)S(1)}, bf16[6,4,64,16]{2,3,1,0:T(8,128)(2,1)S(1)}, bf16[6,4,64,16]{2,3,1,0:T(8,128)(2,1)S(1)},...) while((s32[]{:T(128)}, ...), condition=%wide.region_4.5_spmd.clone, body=%wide.region_1.4_spmd.clone.sunk | while | flops 1187330 | bytes 349285 | solution.py:62
  66.4 0.7 copy.158
  67.1 3.9 %all-to-all-start.2 = ((bf16[96,64,4]{0,2,1:T(4,128)(2,1)}), bf16[96,64,4]{0,2,1:T(4,128)(2,1)S(1)}, u32[]{:S(2)}, u32[]{:S(2)}) async-start(bf16[96,64,4]{0,2,1:T(4,128)(2,1)} %copy.158), calls=%async_computation.2 | async-start | bytes 131072 | tf_op jit(solution)/shard_map/all_to_all | solution.py:91
  71.1 15.9 %all-to-all-done.2 = bf16[96,64,4]{0,2,1:T(4,128)(2,1)S(1)} async-done(((bf16[96,64,4]{0,2,1:T(4,128)(2,1)}), bf16[96,64,4]{0,2,1:T(4,128)(2,1)S(1)}, u32[]{:S(2)}, u32[]{:S(2)}) %all-to-all-start.2) | async-done | bytes 49184 | tf_op jit(solution)/shard_map/all_to_all | solution.py:91
  87.4 10.5 %collective-permute-start = (bf16[2,96,2,1,32]{1,4,3,2,0:T(8,128)(2,1)S(1)}, bf16[2,96,2,1,32]{1,4,3,2,0:T(8,128)(2,1)S(1)}, u32[]{:S(2)}, u32[]{:S(2)}) collective-permute-start(bf16[2,96,2,1,32]{1,4,3,2,0:T(8,128)(2,1)S(1)} %get-tuple-element.192), channel_id=1, source_target_pairs={{0,1},{1,2},{2,3},{3,4},{4,5},{5,6},{6,7},{7,8},{8,9},{9,10},{10,1... | collective-permute-start | bytes 73736 | tf_op jit(solution)/shard_map/ppermute | solution.py:38
  97.9 1.9 collective-permute-start.1
  99.8 3.4 %collective-permute-done.1 = bf16[2,96,2,1,32]{1,4,3,2,0:T(8,128)(2,1)S(1)} collective-permute-done((bf16[2,96,2,1,32]{1,4,3,2,0:T(8,128)(2,1)S(1)}, bf16[2,96,2,1,32]{1,4,3,2,0:T(8,128)(2,1)S(1)}, u32[]{:S(2)}, u32[]{:S(2)}) %collective-permute-start.1) | collective-permute-done | bytes 24608 | tf_op jit(solution)/shard_map/ppermute | solution.py:40
  103.3 2.2 collective-permute-start.2
  105.5 1.3 collective-permute-start.3
  107.1 3.7 %collective-permute-done.3 = bf16[2,96,1,6,32]{1,4,3,2,0:T(8,128)(2,1)S(1)} collective-permute-done((bf16[2,96,1,6,32]{1,4,3,2,0:T(8,128)(2,1)S(1)}, bf16[2,96,1,6,32]{1,4,3,2,0:T(8,128)(2,1)S(1)}, u32[]{:S(2)}, u32[]{:S(2)}) %collective-permute-start.3) | collective-permute-done | bytes 73760 | tf_op jit(solution)/shard_map/ppermute | solution.py:40
  111.4 0.9 fusion.273
  112.2 0.7 fusion.272
  114.3 0.9 convolution_add_fusion.30
  115.4 0.9 convolution_add_fusion.29
  116.5 0.9 convolution_add_fusion.28
  117.6 0.9 convolution_add_fusion.27
  118.7 0.9 convolution_add_fusion.26
  119.8 0.9 convolution_add_fusion.25
  121.5 0.9 convolution_add_fusion.23
  122.6 0.9 convolution_add_fusion.22
  123.7 0.9 convolution_add_fusion.21
  124.8 0.9 convolution_add_fusion.20
  125.9 0.9 convolution_add_fusion.19
  127.0 0.9 convolution_add_fusion.18
  128.1 0.9 convolution_add_fusion.17
  129.5 0.9 fusion.37
  130.6 0.9 fusion.36
  131.7 0.9 fusion.35
  132.8 0.9 fusion.34
  134.0 0.9 fusion.33
  135.1 0.9 fusion.32
  136.2 0.9 fusion.31
  137.3 0.9 fusion.30
  138.4 0.9 fusion.29
  139.8 0.9 convert_element_type.53
  140.8 0.8 pad.9
  141.6 22.9 %all-to-all-start.3 = ((bf16[32,64,128]{2,1,0:T(8,128)(2,1)}), bf16[32,64,128]{2,1,0:T(8,128)(2,1)S(1)}, u32[]{:S(2)}, u32[]{:S(2)}) async-start(bf16[32,64,128]{2,1,0:T(8,128)(2,1)} %bitcast.146), calls=%async_computation.3 | async-start | bytes 1048576 | tf_op jit(solution)/shard_map/all_to_all | solution.py:20
  168.7 7.4 %all-to-all-done.3 = bf16[32,64,128]{2,1,0:T(8,128)(2,1)S(1)} async-done(((bf16[32,64,128]{2,1,0:T(8,128)(2,1)}), bf16[32,64,128]{2,1,0:T(8,128)(2,1)S(1)}, u32[]{:S(2)}, u32[]{:S(2)}) %all-to-all-start.3) | async-done | bytes 524320 | tf_op jit(solution)/shard_map/all_to_all | solution.py:20
  176.2 0.8 broadcast_in_dim.22
  176.9 8.0 %all-to-all-start.4 = ((bf16[16,64,128]{2,1,0:T(8,128)(2,1)}), bf16[16,64,128]{2,1,0:T(8,128)(2,1)S(1)}, u32[]{:S(2)}, u32[]{:S(2)}) async-start(bf16[16,64,128]{2,1,0:T(8,128)(2,1)} %broadcast_in_dim.22), calls=%async_computation.4 | async-start | bytes 524288 | tf_op jit(solution)/shard_map/all_to_all | solution.py:22
  186.0 12.7 %all-to-all-done.4 = bf16[16,64,128]{2,1,0:T(8,128)(2,1)S(1)} async-done(((bf16[16,64,128]{2,1,0:T(8,128)(2,1)}), bf16[16,64,128]{2,1,0:T(8,128)(2,1)S(1)}, u32[]{:S(2)}, u32[]{:S(2)}) %all-to-all-start.4) | async-done | bytes 262176 | tf_op jit(solution)/shard_map/all_to_all | solution.py:22
  198.8 0.9 broadcast_in_dim.23
  199.7 8.9 %all-to-all-start.5 = ((bf16[32,64,128]{2,1,0:T(8,128)(2,1)}), bf16[32,64,128]{2,1,0:T(8,128)(2,1)S(1)}, u32[]{:S(2)}, u32[]{:S(2)}) async-start(bf16[32,64,128]{2,1,0:T(8,128)(2,1)} %broadcast_in_dim.23), calls=%async_computation.5 | async-start | bytes 1048576 | tf_op jit(solution)/shard_map/all_to_all | solution.py:24
  208.8 0.6 reshape.275
  209.9 0.6 reshape.306
  210.5 9.8 %all-to-all-done.5 = bf16[32,64,128]{2,1,0:T(8,128)(2,1)S(1)} async-done(((bf16[32,64,128]{2,1,0:T(8,128)(2,1)}), bf16[32,64,128]{2,1,0:T(8,128)(2,1)S(1)}, u32[]{:S(2)}, u32[]{:S(2)}) %all-to-all-start.5) | async-done | bytes 524320 | tf_op jit(solution)/shard_map/all_to_all | solution.py:24
  220.4 1.4 reshape.307
  (132 shorter events, 17.4 us)
Async XLA Ops:
  0.6 60.0 %copy-start = (bf16[288,96]{1,0:T(8,128)(2,1)S(1)}, bf16[288,96]{1,0:T(8,128)(2,1)}, u32[]{:S(2)}) copy-start(bf16[288,96]{1,0:T(8,128)(2,1)} %param.14) | copy-start | bytes 165892
  3.6 37.2 %all-to-all-start.1 = ((s32[2,2,128]{1,0,2:T(2,128)}), s32[2,2,128]{1,0,2:T(2,128)S(1)}, u32[]{:S(2)}, u32[]{:S(2)}) async-start(s32[2,2,128]{1,0,2:T(2,128)} %copy.148), calls=%async_computation.1 | async-start | bytes 262144 | tf_op jit(solution)/shard_map/all_to_all | solution.py:77
  40.8 19.7 %all-to-all-start = ((bf16[96,2,128]{0,1,2:T(2,128)(2,1)}), bf16[96,2,128]{0,1,2:T(2,128)(2,1)S(1)}, u32[]{:S(2)}, u32[]{:S(2)}) async-start(bf16[96,2,128]{0,1,2:T(2,128)(2,1)} %copy.144), calls=%async_computation | async-start | bytes 131072 | tf_op jit(solution)/shard_map/all_to_all | solution.py:76
  63.6 7.4 %copy-start.1 = (bf16[96,2,128]{2,1,0:T(2,128)(2,1)S(1)}, bf16[96,2,128]{2,1,0:T(2,128)(2,1)}, u32[]{:S(2)}) copy-start(bf16[96,2,128]{2,1,0:T(2,128)(2,1)} %param.17) | copy-start | bytes 147460
  63.6 23.5 %copy-start.11 = (bf16[96,96]{1,0:T(8,128)(2,1)S(1)}, bf16[96,96]{1,0:T(8,128)(2,1)}, u32[]{:S(2)}) copy-start(bf16[96,96]{1,0:T(8,128)(2,1)} %param.15) | copy-start | bytes 55300
  67.1 19.9 %all-to-all-start.2 = ((bf16[96,64,4]{0,2,1:T(4,128)(2,1)}), bf16[96,64,4]{0,2,1:T(4,128)(2,1)S(1)}, u32[]{:S(2)}, u32[]{:S(2)}) async-start(bf16[96,64,4]{0,2,1:T(4,128)(2,1)} %copy.158), calls=%async_computation.2 | async-start | bytes 131072 | tf_op jit(solution)/shard_map/all_to_all | solution.py:91
  87.4 12.5 %collective-permute-start = (bf16[2,96,2,1,32]{1,4,3,2,0:T(8,128)(2,1)S(1)}, bf16[2,96,2,1,32]{1,4,3,2,0:T(8,128)(2,1)S(1)}, u32[]{:S(2)}, u32[]{:S(2)}) collective-permute-start(bf16[2,96,2,1,32]{1,4,3,2,0:T(8,128)(2,1)S(1)} %get-tuple-element.192), channel_id=1, source_target_pairs={{0,1},{1,2},{2,3},{3,4},{4,5},{5,6},{6,7},{7,8},{8,9},{9,10},{10,1... | collective-permute-start | bytes 73736 | tf_op jit(solution)/shard_map/ppermute | solution.py:38
  97.9 5.4 %collective-permute-start.1 = (bf16[2,96,2,1,32]{1,4,3,2,0:T(8,128)(2,1)S(1)}, bf16[2,96,2,1,32]{1,4,3,2,0:T(8,128)(2,1)S(1)}, u32[]{:S(2)}, u32[]{:S(2)}) collective-permute-start(bf16[2,96,2,1,32]{1,4,3,2,0:T(8,128)(2,1)S(1)} %get-tuple-element.193), channel_id=1, source_target_pairs={{1,0},{2,1},{3,2},{4,3},{5,4},{6,5},{7,6},{8,7},{9,8},{10,9},{11,1... | collective-permute-start | bytes 73736 | tf_op jit(solution)/shard_map/ppermute | solution.py:40
  103.3 3.8 %collective-permute-start.2 = (bf16[2,96,1,6,32]{1,4,3,2,0:T(8,128)(2,1)S(1)}, bf16[2,96,1,6,32]{1,4,3,2,0:T(8,128)(2,1)S(1)}, u32[]{:S(2)}, u32[]{:S(2)}) collective-permute-start(bf16[2,96,1,6,32]{1,4,3,2,0:T(8,128)(2,1)S(1)} %get-tuple-element.190), channel_id=1, source_target_pairs={{0,16},{16,32},{32,48},{48,64},{64,80},{80,96},{96,112},{112,128},... | collective-permute-start | bytes 221192 | tf_op jit(solution)/shard_map/ppermute | solution.py:38
  105.5 5.4 %collective-permute-start.3 = (bf16[2,96,1,6,32]{1,4,3,2,0:T(8,128)(2,1)S(1)}, bf16[2,96,1,6,32]{1,4,3,2,0:T(8,128)(2,1)S(1)}, u32[]{:S(2)}, u32[]{:S(2)}) collective-permute-start(bf16[2,96,1,6,32]{1,4,3,2,0:T(8,128)(2,1)S(1)} %get-tuple-element.191), channel_id=1, source_target_pairs={{16,0},{32,16},{48,32},{64,48},{80,64},{96,80},{112,96},{128,112},... | collective-permute-start | bytes 221192 | tf_op jit(solution)/shard_map/ppermute | solution.py:40
  112.2 1.1 copy-start.2
  140.8 23.8 %copy-start.10 = (bf16[96,2,4,32]{0,3,2,1:T(8,128)(2,1)S(1)}, bf16[96,2,4,32]{0,3,2,1:T(8,128)(2,1)}, u32[]{:S(2)}) copy-start(bf16[96,2,4,32]{0,3,2,1:T(8,128)(2,1)} %get-tuple-element.161) | copy-start | bytes 147460
  140.8 24.0 %copy-start.9 = (bf16[96,2,4,32]{0,3,2,1:T(8,128)(2,1)S(1)}, bf16[96,2,4,32]{0,3,2,1:T(8,128)(2,1)}, u32[]{:S(2)}) copy-start(bf16[96,2,4,32]{0,3,2,1:T(8,128)(2,1)} %get-tuple-element.160) | copy-start | bytes 147460
  140.8 24.7 %copy-start.6 = (bf16[96,2,4,32]{0,3,2,1:T(8,128)(2,1)S(1)}, bf16[96,2,4,32]{0,3,2,1:T(8,128)(2,1)}, u32[]{:S(2)}) copy-start(bf16[96,2,4,32]{0,3,2,1:T(8,128)(2,1)} %get-tuple-element.157) | copy-start | bytes 147460
  140.8 24.9 %copy-start.5 = (bf16[96,2,4,32]{0,3,2,1:T(8,128)(2,1)S(1)}, bf16[96,2,4,32]{0,3,2,1:T(8,128)(2,1)}, u32[]{:S(2)}) copy-start(bf16[96,2,4,32]{0,3,2,1:T(8,128)(2,1)} %get-tuple-element.156) | copy-start | bytes 147460
  141.6 23.4 %copy-start.8 = (bf16[96,2,4,32]{0,3,2,1:T(8,128)(2,1)S(1)}, bf16[96,2,4,32]{0,3,2,1:T(8,128)(2,1)}, u32[]{:S(2)}) copy-start(bf16[96,2,4,32]{0,3,2,1:T(8,128)(2,1)} %get-tuple-element.159) | copy-start | bytes 147460
  141.6 23.6 %copy-start.7 = (bf16[96,2,4,32]{0,3,2,1:T(8,128)(2,1)S(1)}, bf16[96,2,4,32]{0,3,2,1:T(8,128)(2,1)}, u32[]{:S(2)}) copy-start(bf16[96,2,4,32]{0,3,2,1:T(8,128)(2,1)} %get-tuple-element.158) | copy-start | bytes 147460
  141.6 24.3 %copy-start.4 = (bf16[96,2,4,32]{0,3,2,1:T(8,128)(2,1)S(1)}, bf16[96,2,4,32]{0,3,2,1:T(8,128)(2,1)}, u32[]{:S(2)}) copy-start(bf16[96,2,4,32]{0,3,2,1:T(8,128)(2,1)} %get-tuple-element.155) | copy-start | bytes 147460
  141.6 24.5 %copy-start.3 = (bf16[96,2,4,32]{0,3,2,1:T(8,128)(2,1)S(1)}, bf16[96,2,4,32]{0,3,2,1:T(8,128)(2,1)}, u32[]{:S(2)}) copy-start(bf16[96,2,4,32]{0,3,2,1:T(8,128)(2,1)} %get-tuple-element.154) | copy-start | bytes 147460
  141.6 34.5 %all-to-all-start.3 = ((bf16[32,64,128]{2,1,0:T(8,128)(2,1)}), bf16[32,64,128]{2,1,0:T(8,128)(2,1)S(1)}, u32[]{:S(2)}, u32[]{:S(2)}) async-start(bf16[32,64,128]{2,1,0:T(8,128)(2,1)} %bitcast.146), calls=%async_computation.3 | async-start | bytes 1048576 | tf_op jit(solution)/shard_map/all_to_all | solution.py:20
  176.9 21.8 %all-to-all-start.4 = ((bf16[16,64,128]{2,1,0:T(8,128)(2,1)}), bf16[16,64,128]{2,1,0:T(8,128)(2,1)S(1)}, u32[]{:S(2)}, u32[]{:S(2)}) async-start(bf16[16,64,128]{2,1,0:T(8,128)(2,1)} %broadcast_in_dim.22), calls=%async_computation.4 | async-start | bytes 524288 | tf_op jit(solution)/shard_map/all_to_all | solution.py:22
  199.7 20.6 %all-to-all-start.5 = ((bf16[32,64,128]{2,1,0:T(8,128)(2,1)}), bf16[32,64,128]{2,1,0:T(8,128)(2,1)S(1)}, u32[]{:S(2)}, u32[]{:S(2)}) async-start(bf16[32,64,128]{2,1,0:T(8,128)(2,1)} %broadcast_in_dim.23), calls=%async_computation.5 | async-start | bytes 1048576 | tf_op jit(solution)/shard_map/all_to_all | solution.py:24

commit v2 on v1

v2 whole, which is shorter than its diff:
```python
import jax
import jax.numpy as jnp
from jax import lax
from jax.experimental import pallas as pl
from jax.experimental.pallas import tpu as pltpu
from jax.sharding import Mesh
from jax.sharding import PartitionSpec as P

BF16 = jnp.bfloat16
F32 = jnp.float32
CHANS = 96
HEADS = 6
HEAD_DIM = 16
INC = 32
LANES = 128
TAPS = 27
BAND = ("zh", "y", "x")
SECTOR = ("zl", "c")
FACE = ("y", "x")
PLANE = ("y", "x", "c")
RING = ("zh", "zl")


def whole(kernel, outs, *args):
    return pl.pallas_call(
        kernel,
        out_shape=outs,
        compiler_params=pltpu.CompilerParams(vmem_limit_bytes=32 * 1024 * 1024),
    )(*args)


def dot(a, b):
    return jnp.dot(a, b, preferred_element_type=F32)


def iota(shape, dim):
    return lax.broadcasted_iota(jnp.int32, shape, dim)


def pack_kernel(feats, counts, ids, occupancy, out):
    lane = iota((LANES, LANES), 1)
    rows = []
    for row in range(2):
        cells = jnp.concatenate(
            [feats[row].astype(F32), jnp.zeros((LANES - CHANS, LANES), F32)], axis=0
        ).T
        count = jnp.broadcast_to(counts[row : row + 1, :].astype(F32), (LANES, LANES)).T
        number = ids[:, row : row + 1]
        tag = jnp.where(occupancy[row : row + 1, :] == 1, number, -1).astype(F32)
        cells = jnp.where(lane == CHANS, count, cells)
        cells = jnp.where(lane == CHANS + 1, number.astype(F32), cells)
        cells = jnp.where(lane == CHANS + 2, tag, cells)
        rows.append(cells.reshape(16, 8, LANES))
    out[...] = jnp.concatenate(rows, axis=1).astype(BF16)


def ray_kernel(own, other, w_qkv, w_out, out):
    n = 256

    def prepared(ref):
        cells = ref[...].astype(F32).reshape(n, LANES)
        turned = cells.T
        scaled = turned[:CHANS] * jnp.log(2.0 + turned[CHANS : CHANS + 1])
        square = jnp.sum(scaled * scaled, axis=0, keepdims=True) * (1.0 / CHANS)
        return cells, turned, scaled, (scaled * lax.rsqrt(square + 1e-05)).astype(BF16)

    cells_a, turned_a, scaled, normed_a = prepared(own)
    cells_b, _, _, normed_b = prepared(other)
    qkv_a = dot(w_qkv[...], normed_a)
    kv_b = dot(w_qkv[CHANS:, :], normed_b)
    query = qkv_a[:CHANS].astype(BF16) * 0.25
    key = jnp.concatenate([qkv_a[CHANS : 2 * CHANS].T, kv_b[:CHANS].T], axis=0).astype(BF16)
    value = jnp.concatenate([qkv_a[2 * CHANS :], kv_b[CHANS:]], axis=1).astype(BF16)

    number = turned_a[CHANS + 1 : CHANS + 2].astype(jnp.int32)
    wanted = (iota((1, n), 1) % 8) * 4 + number
    wanted = (iota((32, n), 0) == wanted).astype(F32).astype(BF16)
    tag = jnp.concatenate(
        [cells_a[:, CHANS + 2 : CHANS + 3], cells_b[:, CHANS + 2 : CHANS + 3]], axis=0
    ).astype(jnp.int32)
    given = jnp.where(tag < 0, -1, (iota((2 * n, 1), 0) % 8) * 4 + tag)
    given = (iota((2 * n, 32), 1) == given).astype(F32).astype(BF16)
    allowed = (dot(given, wanted) > 0.5) | (iota((2 * n, n), 0) == iota((2 * n, n), 1))
    bias = jnp.where(allowed, 0.0, -1e30)

    channel = iota((CHANS, n), 0) // HEAD_DIM
    heads = []
    for head in range(HEADS):
        mine = jnp.where(channel == head, query.astype(F32), 0.0).astype(BF16)
        score = dot(key, mine) + bias
        weight = jnp.exp(score - jnp.max(score, axis=0, keepdims=True))
        total = jnp.sum(weight, axis=0, keepdims=True)
        summed = dot(value[head * HEAD_DIM : (head + 1) * HEAD_DIM], weight.astype(BF16))
        heads.append((summed / total).astype(BF16))
    attn = jnp.concatenate(heads, axis=0)
    mid = scaled + dot(w_out[...], attn)
    mid = jnp.concatenate([mid, jnp.zeros((LANES - CHANS, n), F32)], axis=0).T
    out[...] = mid.astype(BF16).reshape(16, 16, LANES)


def shifted_kernel(cot, turned_weight, patches, back):
    rows = cot[...].reshape(4 * CHANS, 6 * INC)
    source, target = iota((6 * INC, LANES), 0), iota((6 * INC, LANES), 1)
    for da in range(3):
        for di in range(3):
            at = target % INC + 1 - di
            move = (source == target + (2 - da) * INC + 1 - di) & (at >= 0) & (at < INC)
            moved = dot(rows, move.astype(F32).astype(BF16)).astype(BF16)
            for dr in range(3):
                tap = dr * 9 + da * 3 + di
                for row in range(2):
                    at_row = (2 - dr + row) * CHANS
                    patches[pl.ds(tap * CHANS, CHANS), pl.ds(row * LANES, LANES)] = moved[
                        at_row : at_row + CHANS
                    ]
    total = dot(turned_weight[...], patches[...]).astype(BF16)
    back[0] = total[:, :LANES]
    back[1] = total[:, LANES:]


def by_rows(cells):
    cells = cells.astype(F32)
    return [cells[:, r * 8 : r * 8 + 8, :].reshape(-1, LANES) for r in range(cells.shape[1] // 8)]


def tap_kernel(patches, mid, out):
    cells = jnp.concatenate(by_rows(mid[...]), axis=0).astype(BF16)
    lane = iota((CHANS, LANES), 1)
    for group in range(7):
        terms = [
            dot(patches[pl.ds(tap * CHANS, CHANS), :], cells)
            for tap in range(group * 4, min(group * 4 + 4, TAPS))
        ]
        for j in range(3):
            tile = terms[j]
            if len(terms) == 4:
                tile = jnp.where(lane < CHANS, tile, pltpu.roll(terms[3], 96 - 32 * j, 1))
            out[pl.ds((group * 3 + j) * CHANS, CHANS), :] = tile.astype(BF16)
    out[pl.ds(21 * CHANS, 32), :] = jnp.zeros((32, LANES), BF16)


def sum_kernel(terms, out):
    total = jnp.sum(terms[...].astype(F32), axis=0, keepdims=True)
    out[...] = jnp.broadcast_to(total, out.shape).astype(BF16)


def unpack_kernel(tiles, out):
    lane = iota((CHANS, LANES), 1)
    for group in range(7):
        parts = [
            tiles[pl.ds((group * 3 + j) * CHANS, CHANS), :].astype(F32) for j in range(3)
        ]
        for j in range(3):
            out[group * 4 + j] = parts[j][:, :CHANS]
        if group * 4 + 3 < TAPS:
            turned = [pltpu.roll(parts[j], 32 + 32 * j, 1) for j in range(3)]
            last = jnp.where(lane < 32, turned[0], jnp.where(lane < 64, turned[1], turned[2]))
            out[group * 4 + 3] = last[:, :CHANS]


def conv_kernel(middle, before, after, weight, out):
    rows = by_rows(before[...]) + by_rows(middle[...]) + by_rows(after[...])
    inc = iota((6 * INC, LANES), 0) % INC
    moved = []
    for row in rows:
        moved.append(
            [
                jnp.where(inc > 0, pltpu.roll(row, 1, 0), 0.0).astype(BF16),
                row.astype(BF16),
                jnp.where(inc < INC - 1, pltpu.roll(row, 6 * INC - 1, 0), 0.0).astype(BF16),
            ]
        )
    for row in range(2):
        total = jnp.zeros((LANES, CHANS), F32)
        for tap in range(TAPS):
            dr, da, di = tap // 9, tap // 3 % 3, tap % 3
            patch = moved[row + dr][di][da * INC : da * INC + LANES, :CHANS]
            total = total + lax.dot_general(
                patch, weight[tap], (((1,), (1,)), ((), ())), preferred_element_type=F32
            )
        out[row] = total.T.astype(BF16)


def exchange(cells, axis):
    return lax.all_to_all(cells, axis, 0, 0, tiled=True)


def ring(count, closed):
    return [(i, (i + 1) % count) for i in range(count if closed else count - 1)]


def back_ring(count, closed):
    return [(j, i) for i, j in ring(count, closed)]


def shards(feats, counts, occupancy, window_ids, w_qkv, w_out, conv_weight, cotangent):
    struct = jax.ShapeDtypeStruct
    cells = struct((16, 16, LANES), BF16)
    mine = whole(pack_kernel, cells, feats.transpose(1, 0, 2), counts, window_ids, occupancy)
    partner = lax.ppermute(mine, "zh", [(0, 1), (1, 0)])
    own = exchange(mine, FACE)
    other = exchange(partner, FACE)

    bands, sectors = lax.axis_size(BAND), lax.axis_size(SECTOR)
    cot = cotangent.transpose(1, 0, 2)
    cot = jnp.concatenate(
        [
            lax.ppermute(cot[:, :, -INC:], SECTOR, ring(sectors, True)),
            cot,
            lax.ppermute(cot[:, :, :INC], SECTOR, back_ring(sectors, True)),
        ],
        axis=2,
    )
    cot = jnp.concatenate(
        [
            lax.ppermute(cot[1:], BAND, ring(bands, False)),
            cot,
            lax.ppermute(cot[:1], BAND, back_ring(bands, False)),
        ],
        axis=0,
    )
    turned_weight = conv_weight.reshape(TAPS * CHANS, CHANS).T
    patches, back = whole(
        shifted_kernel,
        (struct((TAPS * CHANS, 2 * LANES), BF16), struct((2, CHANS, LANES), BF16)),
        cot,
        turned_weight,
    )

    mid = exchange(whole(ray_kernel, cells, own, other, w_qkv, w_out), FACE)

    plane, along = lax.axis_size(PLANE), lax.axis_size(RING)
    terms = whole(tap_kernel, struct((2048, LANES), BF16), patches, mid)
    terms = exchange(terms.reshape(plane, -1, LANES), PLANE)
    part = terms.shape[1:]
    terms = exchange(whole(sum_kernel, struct((along,) + part, BF16), terms), RING)
    terms = exchange(whole(sum_kernel, struct((plane,) + part, BF16), terms), PLANE)
    grad_weight = whole(
        unpack_kernel, struct((TAPS, CHANS, CHANS), F32), terms.reshape(2048, LANES)
    )

    wide = jnp.concatenate(
        [
            lax.ppermute(mid[-4:], SECTOR, ring(sectors, True)),
            mid,
            lax.ppermute(mid[:4], SECTOR, back_ring(sectors, True)),
        ],
        axis=0,
    )
    before = lax.ppermute(wide[:, 8:], BAND, ring(bands, False))
    after = lax.ppermute(wide[:, :8], BAND, back_ring(bands, False))
    out = whole(conv_kernel, struct((2, CHANS, LANES), BF16), wide, before, after, conv_weight)
    return (out.transpose(1, 0, 2), grad_weight, back.transpose(1, 0, 2))


def solution(mesh):
    mesh = Mesh(mesh.devices.reshape(2, 4, 4, 8, 2), BAND + SECTOR)
    in_specs = (
        P(None, BAND, SECTOR),
        P(BAND, SECTOR),
        P(BAND, SECTOR),
        P(SECTOR, BAND),
        P(),
        P(),
        P(),
        P(None, BAND, SECTOR),
    )
    out_specs = (P(None, BAND, SECTOR), P(), P(None, BAND, SECTOR))
    return jax.shard_map(shards, mesh=mesh, in_specs=in_specs, out_specs=out_specs, check_vma=False)
```

time: 224 us -> 165 us (0.74)
  the two profiles are of different devices: /device:TPU:1 before, /device:TPU:352 now
where the time goes in v2:
time: 165 us; the launch traced here: 164 us
  starting transfers between devices  86 us (52%)
  waiting for transfers between devices  46.4 us (28%)
  blocking collectives  15.2 us (9%)
  Pallas kernels  10 us (6%)
  local copies, waits for them, and re-layouts  5.66 us (3%)
    all_to_all x5, starting transfers between devices, exchange(): return lax.all_to_all(cells, axis, 0, 0, tiled=True)  38.9 us
    all_to_all x5, waiting for transfers between devices, exchange(): return lax.all_to_all(cells, axis, 0, 0, tiled=True)  20.8 us
    ppermute x1, waiting for transfers between devices, shards(): before = lax.ppermute(wide[:, 8:], BAND, ring(bands, False))  17 us
    all_to_all x1, blocking collectives, exchange(): return lax.all_to_all(cells, axis, 0, 0, tiled=True)  15.2 us
    ppermute x1, starting transfers between devices, shards(): lax.ppermute(cot[:1], BAND, back_ring(bands, False))  14.9 us
    ppermute x1, starting transfers between devices, shards(): after = lax.ppermute(wide[:, :8], BAND, back_ring(bands, False))  13.4 us
    pallas_call x8, Pallas kernels, whole(): pl.pallas_call(kernel, out_shape=outs, compiler_params=pltpu.CompilerPara...  10 us
    ppermute x1, waiting for transfers between devices, shards(): partner = lax.ppermute(mine, 'zh', [(0, 1), (1, 0)])  7.52 us
  transfers between devices with their start and end apart: 14, of which 6 were waited for; matrix products, arithmetic and copies ran while one was open for 3% of the time, Pallas kernels for 5%

profile of v2, /device:TPU:352, one launch (start us, length us, event | category | flops | bytes accessed | tf_op | source)
XLA Modules:
  0.0 164.5 jit_solution(5379163627709752994)
XLA Ops:
  0.6 0.0 copy-start
  0.6 0.0 copy-start.2
  0.7 0.0 copy-start.1
  0.7 0.9 copy.27
  1.5 0.1 fusion.3
  1.6 1.9 %collective-permute-start.5 = (bf16[2,96,32]{2,1,0:T(8,128)(2,1)S(1)}, bf16[2,96,32]{2,1,0:T(8,128)(2,1)S(1)}, u32[]{:S(2)}, u32[]{:S(2)}) collective-permute-start(bf16[2,96,32]{2,1,0:T(8,128)(2,1)S(1)} %get-tuple-element.19), channel_id=1, source_target_pairs={{0,1},{1,2},{2,3},{3,4},{4,5},{5,6},{6,7},{7,8},{8,9},{9,10},{10,1... | collective-permute-start | bytes 36872 | tf_op jit(solution)/shard_map/ppermute | solution.py:208
  3.5 3.6 %collective-permute-start.6 = (bf16[2,96,32]{2,1,0:T(8,128)(2,1)S(1)}, bf16[2,96,32]{2,1,0:T(8,128)(2,1)S(1)}, u32[]{:S(2)}, u32[]{:S(2)}) collective-permute-start(bf16[2,96,32]{2,1,0:T(8,128)(2,1)S(1)} %get-tuple-element.20), channel_id=1, source_target_pairs={{1,0},{2,1},{3,2},{4,3},{5,4},{6,5},{7,6},{8,7},{9,8},{10,9},{11,1... | collective-permute-start | bytes 36872 | tf_op jit(solution)/shard_map/ppermute | solution.py:210
  7.2 0.7 copy.20.occupancy
  7.9 0.8 copy.28
  8.7 0.8 copy.19.ids
  9.5 0.0 copy-start.3
  9.5 0.7 copy-done.3
  10.2 0.9 shard_map.103
  11.1 7.0 %all-to-all-start = ((bf16[16,16,128]{2,1,0:T(8,128)(2,1)}), bf16[16,16,128]{2,1,0:T(8,128)(2,1)S(1)}, u32[]{:S(2)}, u32[]{:S(2)}) async-start(bf16[16,16,128]{2,1,0:T(8,128)(2,1)} %shard_map.103), calls=%async_computation | async-start | bytes 131072 | tf_op jit(solution)/shard_map/all_to_all | solution.py:185
  18.1 1.9 %collective-permute-start = (bf16[16,16,128]{2,1,0:T(8,128)(2,1)}, bf16[16,16,128]{2,1,0:T(8,128)(2,1)}, u32[]{:S(2)}, u32[]{:S(2)}) collective-permute-start(bf16[16,16,128]{2,1,0:T(8,128)(2,1)} %shard_map.103), channel_id=1, source_target_pairs={{0,256},{256,0},{1,257},{257,1},{2,258},{258,2},{3,259},{259,3},{4... | collective-permute-start | bytes 196616 | tf_op jit(solution)/shard_map/ppermute | solution.py:200
  20.0 0.0 collective-permute-done.5
  20.1 0.0 collective-permute-done.6
  20.1 0.1 pad_maximum_fusion.1
  20.2 5.6 %all-to-all-done.own = bf16[16,16,128]{2,1,0:T(8,128)(2,1)S(1)} async-done(((bf16[16,16,128]{2,1,0:T(8,128)(2,1)}), bf16[16,16,128]{2,1,0:T(8,128)(2,1)S(1)}, u32[]{:S(2)}, u32[]{:S(2)}) %all-to-all-start) | async-done | bytes 65568 | tf_op jit(solution)/shard_map/all_to_all | solution.py:185
  25.8 7.5 %collective-permute-done = bf16[16,16,128]{2,1,0:T(8,128)(2,1)} collective-permute-done((bf16[16,16,128]{2,1,0:T(8,128)(2,1)}, bf16[16,16,128]{2,1,0:T(8,128)(2,1)}, u32[]{:S(2)}, u32[]{:S(2)}) %collective-permute-start) | collective-permute-done | bytes 65568 | tf_op jit(solution)/shard_map/ppermute | solution.py:200
  33.3 7.2 %all-to-all-start.1 = ((bf16[16,16,128]{2,1,0:T(8,128)(2,1)}), bf16[16,16,128]{2,1,0:T(8,128)(2,1)S(1)}, u32[]{:S(2)}, u32[]{:S(2)}) async-start(bf16[16,16,128]{2,1,0:T(8,128)(2,1)} %collective-permute-done), calls=%async_computation.1 | async-start | bytes 131072 | tf_op jit(solution)/shard_map/all_to_all | solution.py:185
  40.5 3.8 %collective-permute-start.7 = (bf16[1,96,192]{2,1,0:T(8,128)(2,1)S(1)}, bf16[1,96,192]{2,1,0:T(8,128)(2,1)S(1)}, u32[]{:S(2)}, u32[]{:S(2)}) collective-permute-start(bf16[1,96,192]{2,1,0:T(8,128)(2,1)S(1)} %get-tuple-element.13), channel_id=1, source_target_pairs={{0,16},{16,32},{32,48},{48,64},{64,80},{80,96},{96,112},{112,128},... | collective-permute-start | bytes 110600 | tf_op jit(solution)/shard_map/ppermute | solution.py:216
  44.4 14.9 %collective-permute-start.8 = (bf16[1,96,192]{2,1,0:T(8,128)(2,1)S(1)}, bf16[1,96,192]{2,1,0:T(8,128)(2,1)S(1)}, u32[]{:S(2)}, u32[]{:S(2)}) collective-permute-start(bf16[1,96,192]{2,1,0:T(8,128)(2,1)S(1)} %get-tuple-element.14), channel_id=1, source_target_pairs={{16,0},{32,16},{48,32},{64,48},{80,64},{96,80},{112,96},{128,112},... | collective-permute-start | bytes 110600 | tf_op jit(solution)/shard_map/ppermute | solution.py:218
  59.3 0.0 copy-done
  59.4 0.3 copy.22
  59.7 0.0 all-to-all-done.1.other
  59.7 0.0 copy-done.2
  59.7 0.0 copy-done.1
  59.7 3.4 %shard_map.104 = bf16[16,16,128]{2,1,0:T(8,128)(2,1)} custom-call(bf16[16,16,128]{2,1,0:T(8,128)(2,1)S(1)} %all-to-all-done.own, bf16[16,16,128]{2,1,0:T(8,128)(2,1)S(1)} %all-to-all-done.1.other, bf16[288,96]{1,0:T(8,128)(2,1)S(1)} %copy-done.1, bf16[96,96]{1,0:T(8,128)(2,1)S(1)} %copy-done.2), custom_call_target="tpu_custom_call" | custom-call | tf_op jit(solution)/shard_map/pallas_call | solution.py:25
  63.1 3.5 %all-to-all-start.2 = ((bf16[16,16,128]{2,1,0:T(8,128)(2,1)}), bf16[16,16,128]{2,1,0:T(8,128)(2,1)S(1)}, u32[]{:S(2)}, u32[]{:S(2)}) async-start(bf16[16,16,128]{2,1,0:T(8,128)(2,1)} %shard_map.104), calls=%async_computation.2 | async-start | bytes 131072 | tf_op jit(solution)/shard_map/all_to_all | solution.py:185
  66.6 0.0 collective-permute-done.7
  66.6 0.0 collective-permute-done.8
  66.6 0.1 pad_maximum_fusion.cot
  66.7 1.2 shard_map.106
  68.0 6.2 %all-to-all-done.2.mid = bf16[16,16,128]{2,1,0:T(8,128)(2,1)S(1)} async-done(((bf16[16,16,128]{2,1,0:T(8,128)(2,1)}), bf16[16,16,128]{2,1,0:T(8,128)(2,1)S(1)}, u32[]{:S(2)}, u32[]{:S(2)}) %all-to-all-start.2) | async-done | bytes 65568 | tf_op jit(solution)/shard_map/all_to_all | solution.py:185
  74.2 0.5 shard_map.107
  74.8 15.2 %all_to_all.30.terms = bf16[32,64,128]{2,1,0:T(8,128)(2,1)S(1)} all-to-all(bf16[32,64,128]{2,1,0:T(8,128)(2,1)S(1)} %bitcast.14), channel_id=1, replica_groups=mesh['zh'=2,'y'=4,'x'=4,'zl'=8,'c'=2] {'y','x','c'}, dimensions={0} | all-to-all | bytes 1048576 | tf_op jit(solution)/shard_map/all_to_all | solution.py:185
  90.0 0.8 shard_map.108
  90.8 17.3 %all-to-all-start.4 = ((bf16[16,64,128]{2,1,0:T(8,128)(2,1)}), bf16[16,64,128]{2,1,0:T(8,128)(2,1)S(1)}, u32[]{:S(2)}, u32[]{:S(2)}) async-start(bf16[16,64,128]{2,1,0:T(8,128)(2,1)} %shard_map.108), calls=%async_computation.4 | async-start | bytes 524288 | tf_op jit(solution)/shard_map/all_to_all | solution.py:185
  108.0 1.9 %collective-permute-start.1 = (bf16[4,16,128]{2,1,0:T(8,128)(2,1)S(1)}, bf16[4,16,128]{2,1,0:T(8,128)(2,1)S(1)}, u32[]{:S(2)}, u32[]{:S(2)}) collective-permute-start(bf16[4,16,128]{2,1,0:T(8,128)(2,1)S(1)} %get-tuple-element.18), channel_id=1, source_target_pairs={{0,1},{1,2},{2,3},{3,4},{4,5},{5,6},{6,7},{7,8},{8,9},{9,10},{10,1... | collective-permute-start | bytes 49160 | tf_op jit(solution)/shard_map/ppermute | solution.py:244
  110.0 3.6 %collective-permute-start.2 = (bf16[4,16,128]{2,1,0:T(8,128)(2,1)S(1)}, bf16[4,16,128]{2,1,0:T(8,128)(2,1)S(1)}, u32[]{:S(2)}, u32[]{:S(2)}) collective-permute-start(bf16[4,16,128]{2,1,0:T(8,128)(2,1)S(1)} %get-tuple-element.17), channel_id=1, source_target_pairs={{1,0},{2,1},{3,2},{4,3},{5,4},{6,5},{7,6},{8,7},{9,8},{10,9},{11,1... | collective-permute-start | bytes 49160 | tf_op jit(solution)/shard_map/ppermute | solution.py:246
  113.6 9.0 %all-to-all-done.4.terms = bf16[16,64,128]{2,1,0:T(8,128)(2,1)S(1)} async-done(((bf16[16,64,128]{2,1,0:T(8,128)(2,1)}), bf16[16,64,128]{2,1,0:T(8,128)(2,1)S(1)}, u32[]{:S(2)}, u32[]{:S(2)}) %all-to-all-start.4) | async-done | bytes 262176 | tf_op jit(solution)/shard_map/all_to_all | solution.py:185
  122.6 0.9 shard_map.109
  123.5 3.9 %all-to-all-start.5 = ((bf16[32,64,128]{2,1,0:T(8,128)(2,1)}), bf16[32,64,128]{2,1,0:T(8,128)(2,1)S(1)}, u32[]{:S(2)}, u32[]{:S(2)}) async-start(bf16[32,64,128]{2,1,0:T(8,128)(2,1)} %shard_map.109), calls=%async_computation.5 | async-start | bytes 1048576 | tf_op jit(solution)/shard_map/all_to_all | solution.py:185
  127.4 0.0 collective-permute-done.1
  127.4 0.0 collective-permute-done.2
  127.5 13.4 %collective-permute-start.4 = (bf16[24,8,128]{2,1,0:T(8,128)(2,1)S(1)}, bf16[24,8,128]{2,1,0:T(8,128)(2,1)S(1)}, u32[]{:S(2)}, u32[]{:S(2)}) collective-permute-start(bf16[24,8,128]{2,1,0:T(8,128)(2,1)S(1)} %get-tuple-element.15), channel_id=1, source_target_pairs={{16,0},{32,16},{48,32},{64,48},{80,64},{96,80},{112,96},{128,112},... | collective-permute-start | bytes 147464 | tf_op jit(solution)/shard_map/ppermute | solution.py:251
  140.8 1.9 %collective-permute-start.3 = (bf16[24,8,128]{2,1,0:T(8,128)(2,1)S(1)}, bf16[24,8,128]{2,1,0:T(8,128)(2,1)S(1)}, u32[]{:S(2)}, u32[]{:S(2)}) collective-permute-start(bf16[24,8,128]{2,1,0:T(8,128)(2,1)S(1)} %get-tuple-element.16), channel_id=1, source_target_pairs={{0,16},{16,32},{32,48},{48,64},{64,80},{80,96},{96,112},{112,128},... | collective-permute-start | bytes 147464 | tf_op jit(solution)/shard_map/ppermute | solution.py:250
  142.7 0.7 copy.24
  143.4 1.0 collective-permute-done.4.after
  144.4 17.0 %collective-permute-done.3.before = bf16[24,8,128]{2,1,0:T(8,128)(2,1)S(1)} collective-permute-done((bf16[24,8,128]{2,1,0:T(8,128)(2,1)S(1)}, bf16[24,8,128]{2,1,0:T(8,128)(2,1)S(1)}, u32[]{:S(2)}, u32[]{:S(2)}) %collective-permute-start.3) | collective-permute-done | bytes 49184 | tf_op jit(solution)/shard_map/ppermute | solution.py:250
  161.5 1.1 shard_map.105
  162.5 0.7 copy.23
  163.2 0.0 all-to-all-done.5
  163.2 1.3 shard_map.110
  (6 shorter events, 0.0 us)
Async XLA Ops:
  0.6 58.7 %copy-start = (bf16[27,96,96]{2,1,0:T(8,128)(2,1)S(1)}, bf16[27,96,96]{2,1,0:T(8,128)(2,1)}, u32[]{:S(2)}) copy-start(bf16[27,96,96]{2,1,0:T(8,128)(2,1)} %weight.1) | copy-start | bytes 1492996
  0.6 59.0 %copy-start.2 = (bf16[96,96]{1,0:T(8,128)(2,1)S(1)}, bf16[96,96]{1,0:T(8,128)(2,1)}, u32[]{:S(2)}) copy-start(bf16[96,96]{1,0:T(8,128)(2,1)} %w_out.1) | copy-start | bytes 55300
  0.7 59.0 %copy-start.1 = (bf16[288,96]{1,0:T(8,128)(2,1)S(1)}, bf16[288,96]{1,0:T(8,128)(2,1)}, u32[]{:S(2)}) copy-start(bf16[288,96]{1,0:T(8,128)(2,1)} %w_qkv.1) | copy-start | bytes 165892
  1.6 18.4 %collective-permute-start.5 = (bf16[2,96,32]{2,1,0:T(8,128)(2,1)S(1)}, bf16[2,96,32]{2,1,0:T(8,128)(2,1)S(1)}, u32[]{:S(2)}, u32[]{:S(2)}) collective-permute-start(bf16[2,96,32]{2,1,0:T(8,128)(2,1)S(1)} %get-tuple-element.19), channel_id=1, source_target_pairs={{0,1},{1,2},{2,3},{3,4},{4,5},{5,6},{6,7},{7,8},{8,9},{9,10},{10,1... | collective-permute-start | bytes 36872 | tf_op jit(solution)/shard_map/ppermute | solution.py:208
  3.5 16.5 %collective-permute-start.6 = (bf16[2,96,32]{2,1,0:T(8,128)(2,1)S(1)}, bf16[2,96,32]{2,1,0:T(8,128)(2,1)S(1)}, u32[]{:S(2)}, u32[]{:S(2)}) collective-permute-start(bf16[2,96,32]{2,1,0:T(8,128)(2,1)S(1)} %get-tuple-element.20), channel_id=1, source_target_pairs={{1,0},{2,1},{3,2},{4,3},{5,4},{6,5},{7,6},{8,7},{9,8},{10,9},{11,1... | collective-permute-start | bytes 36872 | tf_op jit(solution)/shard_map/ppermute | solution.py:210
  9.5 0.7 copy-start.3
  11.1 14.7 %all-to-all-start = ((bf16[16,16,128]{2,1,0:T(8,128)(2,1)}), bf16[16,16,128]{2,1,0:T(8,128)(2,1)S(1)}, u32[]{:S(2)}, u32[]{:S(2)}) async-start(bf16[16,16,128]{2,1,0:T(8,128)(2,1)} %shard_map.103), calls=%async_computation | async-start | bytes 131072 | tf_op jit(solution)/shard_map/all_to_all | solution.py:185
  18.1 15.2 %collective-permute-start = (bf16[16,16,128]{2,1,0:T(8,128)(2,1)}, bf16[16,16,128]{2,1,0:T(8,128)(2,1)}, u32[]{:S(2)}, u32[]{:S(2)}) collective-permute-start(bf16[16,16,128]{2,1,0:T(8,128)(2,1)} %shard_map.103), channel_id=1, source_target_pairs={{0,256},{256,0},{1,257},{257,1},{2,258},{258,2},{3,259},{259,3},{4... | collective-permute-start | bytes 196616 | tf_op jit(solution)/shard_map/ppermute | solution.py:200
  33.3 26.4 %all-to-all-start.1 = ((bf16[16,16,128]{2,1,0:T(8,128)(2,1)}), bf16[16,16,128]{2,1,0:T(8,128)(2,1)S(1)}, u32[]{:S(2)}, u32[]{:S(2)}) async-start(bf16[16,16,128]{2,1,0:T(8,128)(2,1)} %collective-permute-done), calls=%async_computation.1 | async-start | bytes 131072 | tf_op jit(solution)/shard_map/all_to_all | solution.py:185
  40.5 26.1 %collective-permute-start.7 = (bf16[1,96,192]{2,1,0:T(8,128)(2,1)S(1)}, bf16[1,96,192]{2,1,0:T(8,128)(2,1)S(1)}, u32[]{:S(2)}, u32[]{:S(2)}) collective-permute-start(bf16[1,96,192]{2,1,0:T(8,128)(2,1)S(1)} %get-tuple-element.13), channel_id=1, source_target_pairs={{0,16},{16,32},{32,48},{48,64},{64,80},{80,96},{96,112},{112,128},... | collective-permute-start | bytes 110600 | tf_op jit(solution)/shard_map/ppermute | solution.py:216
  44.4 22.2 %collective-permute-start.8 = (bf16[1,96,192]{2,1,0:T(8,128)(2,1)S(1)}, bf16[1,96,192]{2,1,0:T(8,128)(2,1)S(1)}, u32[]{:S(2)}, u32[]{:S(2)}) collective-permute-start(bf16[1,96,192]{2,1,0:T(8,128)(2,1)S(1)} %get-tuple-element.14), channel_id=1, source_target_pairs={{16,0},{32,16},{48,32},{64,48},{80,64},{96,80},{112,96},{128,112},... | collective-permute-start | bytes 110600 | tf_op jit(solution)/shard_map/ppermute | solution.py:218
  63.1 11.1 %all-to-all-start.2 = ((bf16[16,16,128]{2,1,0:T(8,128)(2,1)}), bf16[16,16,128]{2,1,0:T(8,128)(2,1)S(1)}, u32[]{:S(2)}, u32[]{:S(2)}) async-start(bf16[16,16,128]{2,1,0:T(8,128)(2,1)} %shard_map.104), calls=%async_computation.2 | async-start | bytes 131072 | tf_op jit(solution)/shard_map/all_to_all | solution.py:185
  90.8 31.8 %all-to-all-start.4 = ((bf16[16,64,128]{2,1,0:T(8,128)(2,1)}), bf16[16,64,128]{2,1,0:T(8,128)(2,1)S(1)}, u32[]{:S(2)}, u32[]{:S(2)}) async-start(bf16[16,64,128]{2,1,0:T(8,128)(2,1)} %shard_map.108), calls=%async_computation.4 | async-start | bytes 524288 | tf_op jit(solution)/shard_map/all_to_all | solution.py:185
  108.0 19.4 %collective-permute-start.1 = (bf16[4,16,128]{2,1,0:T(8,128)(2,1)S(1)}, bf16[4,16,128]{2,1,0:T(8,128)(2,1)S(1)}, u32[]{:S(2)}, u32[]{:S(2)}) collective-permute-start(bf16[4,16,128]{2,1,0:T(8,128)(2,1)S(1)} %get-tuple-element.18), channel_id=1, source_target_pairs={{0,1},{1,2},{2,3},{3,4},{4,5},{5,6},{6,7},{7,8},{8,9},{9,10},{10,1... | collective-permute-start | bytes 49160 | tf_op jit(solution)/shard_map/ppermute | solution.py:244
  110.0 17.5 %collective-permute-start.2 = (bf16[4,16,128]{2,1,0:T(8,128)(2,1)S(1)}, bf16[4,16,128]{2,1,0:T(8,128)(2,1)S(1)}, u32[]{:S(2)}, u32[]{:S(2)}) collective-permute-start(bf16[4,16,128]{2,1,0:T(8,128)(2,1)S(1)} %get-tuple-element.17), channel_id=1, source_target_pairs={{1,0},{2,1},{3,2},{4,3},{5,4},{6,5},{7,6},{8,7},{9,8},{10,9},{11,1... | collective-permute-start | bytes 49160 | tf_op jit(solution)/shard_map/ppermute | solution.py:246
  123.5 39.7 %all-to-all-start.5 = ((bf16[32,64,128]{2,1,0:T(8,128)(2,1)}), bf16[32,64,128]{2,1,0:T(8,128)(2,1)S(1)}, u32[]{:S(2)}, u32[]{:S(2)}) async-start(bf16[32,64,128]{2,1,0:T(8,128)(2,1)} %shard_map.109), calls=%async_computation.5 | async-start | bytes 1048576 | tf_op jit(solution)/shard_map/all_to_all | solution.py:185
  127.5 17.0 %collective-permute-start.4 = (bf16[24,8,128]{2,1,0:T(8,128)(2,1)S(1)}, bf16[24,8,128]{2,1,0:T(8,128)(2,1)S(1)}, u32[]{:S(2)}, u32[]{:S(2)}) collective-permute-start(bf16[24,8,128]{2,1,0:T(8,128)(2,1)S(1)} %get-tuple-element.15), channel_id=1, source_target_pairs={{16,0},{32,16},{48,32},{64,48},{80,64},{96,80},{112,96},{128,112},... | collective-permute-start | bytes 147464 | tf_op jit(solution)/shard_map/ppermute | solution.py:251
  140.8 20.6 %collective-permute-start.3 = (bf16[24,8,128]{2,1,0:T(8,128)(2,1)S(1)}, bf16[24,8,128]{2,1,0:T(8,128)(2,1)S(1)}, u32[]{:S(2)}, u32[]{:S(2)}) collective-permute-start(bf16[24,8,128]{2,1,0:T(8,128)(2,1)S(1)} %get-tuple-element.16), channel_id=1, source_target_pairs={{0,16},{16,32},{32,48},{48,64},{64,80},{80,96},{96,112},{112,128},... | collective-permute-start | bytes 147464 | tf_op jit(solution)/shard_map/ppermute | solution.py:250

commit v3 on v2

v3 whole, which is shorter than its diff:
```python
import jax
import jax.numpy as jnp
from jax import lax
from jax.experimental import pallas as pl
from jax.experimental.pallas import tpu as pltpu
from jax.sharding import Mesh
from jax.sharding import PartitionSpec as P

BF16 = jnp.bfloat16
F32 = jnp.float32
CHANS = 96
HEADS = 6
HEAD_DIM = 16
INC = 32
LANES = 128
TAPS = 27
BAND = ("zh", "y", "x")
SECTOR = ("zl", "c")
FACE = ("y", "x")
PLANE = ("y", "x", "c")
RING = ("zh", "zl")


def whole(kernel, outs, *args):
    return pl.pallas_call(
        kernel,
        out_shape=outs,
        compiler_params=pltpu.CompilerParams(vmem_limit_bytes=32 * 1024 * 1024),
    )(*args)


def dot(a, b):
    return jnp.dot(a, b, preferred_element_type=F32)


def iota(shape, dim):
    return lax.broadcasted_iota(jnp.int32, shape, dim)


def pack_kernel(feats_hbm, counts_hbm, ids_hbm, occupancy_hbm, out, feats, counts, ids, occupancy, sems):
    copies = [
        pltpu.make_async_copy(source, target, sems.at[i])
        for i, (source, target) in enumerate(
            [
                (feats_hbm, feats),
                (counts_hbm, counts),
                (ids_hbm, ids),
                (occupancy_hbm, occupancy),
            ]
        )
    ]
    for copy in copies:
        copy.start()
    for copy in copies:
        copy.wait()
    lane = iota((LANES, LANES), 1)
    both = feats[...].astype(F32)
    rows = []
    for row in range(2):
        number = ids[row : row + 1, :]
        tag = jnp.where(occupancy[:, row : row + 1] == 1, number, -1)
        more = [v.astype(F32) for v in (counts[row : row + 1, :], number, tag)]
        more.append(jnp.zeros((LANES - CHANS - 3, LANES), F32))
        cells = jnp.concatenate([both[:, row, :]] + more, axis=0)
        rows.append(cells.T.reshape(16, 8, LANES))
    out[...] = jnp.concatenate(rows, axis=1).astype(BF16)


def ray_kernel(place_of, loads, w_qkv_hbm, w_out_hbm, turned_weight, out, w_qkv, w_out, patches, sems):
    n, wide = 256, 384
    fetches = [
        pltpu.make_async_copy(w_qkv_hbm, w_qkv, sems.at[0]),
        pltpu.make_async_copy(w_out_hbm, w_out, sems.at[1]),
    ]
    for fetch in fetches:
        fetch.start()
    every = loads[...].astype(F32)
    own = every[:, :16].reshape(n, LANES)
    other = every[:, 16:32].reshape(n, LANES)
    low = place_of[0, 0] == 0
    edge = jnp.where(low, other[:8], other[n - 8 :])
    asked = jnp.concatenate([own, edge, jnp.zeros((wide - n - 8, LANES), F32)], axis=0)

    def prepared(cells):
        turned = cells.T
        scaled = turned[:CHANS] * jnp.log(2.0 + turned[CHANS : CHANS + 1])
        square = jnp.sum(scaled * scaled, axis=0, keepdims=True) * (1.0 / CHANS)
        return turned, scaled, (scaled * lax.rsqrt(square + 1e-05)).astype(BF16)

    turned, scaled, normed_a = prepared(asked)
    _, _, normed_b = prepared(other)
    for fetch in fetches:
        fetch.wait()
    query = dot(w_qkv[:CHANS, :], normed_a).astype(BF16).astype(F32) * 0.25
    kv = dot(w_qkv[CHANS:, :], jnp.concatenate([normed_a[:, :n], normed_b], axis=1))
    key = kv[:CHANS].T.astype(BF16)
    value = kv[CHANS:].astype(BF16)

    number = turned[CHANS + 1 : CHANS + 2].astype(jnp.int32)
    wanted = (iota((1, wide), 1) % 8) * 4 + number
    wanted = (iota((32, wide), 0) == wanted).astype(F32).astype(BF16)
    tag = jnp.concatenate(
        [own[:, CHANS + 2 : CHANS + 3], other[:, CHANS + 2 : CHANS + 3]], axis=0
    ).astype(jnp.int32)
    given = jnp.where(tag < 0, -1, (iota((2 * n, 1), 0) % 8) * 4 + tag)
    given = (iota((2 * n, 32), 1) == given).astype(F32).astype(BF16)
    place = iota((1, wide), 1)
    place = jnp.where((place < n) | low, place, place + n - 8)
    allowed = (dot(given, wanted) > 0.5) | (iota((2 * n, wide), 0) == place)
    bias = jnp.where(allowed, 0.0, -1e30)

    cell = iota((16, 8, LANES), 1)
    for da in range(3):
        shifted = [[], [], []]
        for row in range(2):
            at, edge_at = 32 + da * 16 + row * 8, 80 + da * 4 + row * 2
            block = every[:, at : at + 8]
            flat = block.reshape(LANES, LANES)
            upper = pltpu.roll(flat, LANES - 1, 0).reshape(16, 8, LANES)
            lower = pltpu.roll(flat, 1, 0).reshape(16, 8, LANES)
            shifted[0].append(jnp.where(cell < 7, upper, every[:, edge_at + 1 : edge_at + 2]))
            shifted[1].append(block)
            shifted[2].append(jnp.where(cell > 0, lower, every[:, edge_at : edge_at + 1]))
        for di in range(3):
            cells = jnp.concatenate(shifted[di], axis=1).reshape(n, LANES)
            patches[pl.ds((da * 3 + di) * CHANS, CHANS), :] = cells.T[:CHANS].astype(BF16)

    channel = iota((CHANS, wide), 0) // HEAD_DIM
    heads = []
    for head in range(HEADS):
        mine = jnp.where(channel == head, query, 0.0).astype(BF16)
        score = dot(key, mine) + bias
        weight = jnp.exp(score - jnp.max(score, axis=0, keepdims=True))
        total = jnp.sum(weight, axis=0, keepdims=True)
        summed = dot(value[head * HEAD_DIM : (head + 1) * HEAD_DIM], weight.astype(BF16))
        heads.append((summed / total).astype(BF16))
    attn = jnp.concatenate(heads, axis=0)
    mid = scaled + dot(w_out[...], attn)
    mid = jnp.concatenate([mid, jnp.zeros((LANES - CHANS, wide), F32)], axis=0).T
    edge, none = mid[n : n + 8], jnp.zeros((8, LANES), F32)
    mid = jnp.concatenate(
        [jnp.where(low, none, edge), mid[:n], jnp.where(low, edge, none)], axis=0
    )
    pairs = mid.reshape(17, 16, LANES)
    pairs = jnp.concatenate([pairs[:16], pairs[1:]], axis=1).astype(BF16)

    near = [mid[8 * dr : 8 * dr + n].astype(BF16) for dr in range(3)]
    lane = iota((CHANS, LANES), 1)
    for group in range(7):
        parts = [
            dot(patches[pl.ds(tap % 9 * CHANS, CHANS), :], near[tap // 9])
            for tap in range(group * 4, min(group * 4 + 4, TAPS))
        ]
        for j in range(3):
            tile = parts[j]
            if len(parts) == 4:
                tile = jnp.where(lane < CHANS, tile, pltpu.roll(parts[3], 96 - 32 * j, 1))
            tile = tile.astype(BF16)
            for q in range(3):
                at = (group * 3 + j) * CHANS + 32 * q
                out[at // 64, pl.ds(at % 64, 32), :] = tile[32 * q : 32 * q + 32]
    out[31, pl.ds(32, 32), :] = jnp.zeros((32, LANES), BF16)

    lane = iota((CHANS, n), 1)
    up, level, down = (dot(turned_weight[dr], patches[...]) for dr in range(3))
    back = level + jnp.where(lane < n - 8, pltpu.roll(up, n - 8, 1), 0.0)
    back = back + jnp.where(lane >= 8, pltpu.roll(down, 8, 1), 0.0)
    back = jnp.concatenate([back, jnp.zeros((LANES - CHANS, n), F32)], axis=0).T
    back = back.astype(BF16).reshape(16, 16, LANES)
    for face in range(16):
        for core in range(2):
            out[2 * face + core, pl.ds(64, 32), :] = pairs[face]
            out[2 * face + core, pl.ds(96, 16), :] = back[face]


def moves():
    source, target = iota((6 * INC, LANES), 0), iota((6 * INC, LANES), 1)
    for da in range(3):
        for di in range(3):
            at = target % INC + 1 - di
            move = (source == target + (2 - da) * INC + 1 - di) & (at >= 0) & (at < INC)
            yield da, di, move.astype(F32).astype(BF16)


def load_kernel(mine, partner, left, middle, right, out):
    inc = iota((6 * INC, LANES), 0) % INC
    rows = []
    for row in range(2):
        parts = []
        for piece in (left, middle, right):
            cells = piece[row].astype(F32)
            more = jnp.zeros((LANES - CHANS, cells.shape[1]), F32)
            parts.append(jnp.concatenate([cells, more], axis=0).T)
        cells = jnp.concatenate(parts, axis=0)
        lower = jnp.where(inc > 0, pltpu.roll(cells, 1, 0), 0.0)
        upper = jnp.where(inc < INC - 1, pltpu.roll(cells, 6 * INC - 1, 0), 0.0)
        rows.append((cells, lower, upper))
    blocks, edges = [], []
    for da in range(3):
        at = (2 - da) * INC
        for row in range(2):
            cells, lower, upper = (v[at : at + LANES].reshape(16, 8, LANES) for v in rows[row])
            blocks.append(cells)
            edges += [lower[:, :1], upper[:, 7:]]
    edges.append(jnp.zeros((16, 4, LANES), F32))
    out[:, pl.ds(0, 16), :] = mine[...]
    out[:, pl.ds(16, 16), :] = partner[...]
    out[:, pl.ds(32, 48), :] = jnp.concatenate(blocks, axis=1).astype(BF16)
    out[:, pl.ds(80, 16), :] = jnp.concatenate(edges, axis=1).astype(BF16)


def by_rows(cells):
    cells = cells.astype(F32)
    return [cells[:, r * 8 : r * 8 + 8, :].reshape(-1, LANES) for r in range(cells.shape[1] // 8)]


def sum_kernel(terms, out):
    total = jnp.sum(terms[:, pl.ds(0, 64), :].astype(F32), axis=0, keepdims=True)
    out[...] = jnp.broadcast_to(total, out.shape).astype(BF16)


def unpack_kernel(tiles, out):
    lane = iota((CHANS, LANES), 1)
    for group in range(7):
        parts = [
            tiles[pl.ds((group * 3 + j) * CHANS, CHANS), :].astype(F32) for j in range(3)
        ]
        for j in range(3):
            out[group * 4 + j] = parts[j][:, :CHANS]
        if group * 4 + 3 < TAPS:
            turned = [pltpu.roll(parts[j], 32 + 32 * j, 1) for j in range(3)]
            last = jnp.where(lane < 32, turned[0], jnp.where(lane < 64, turned[1], turned[2]))
            out[group * 4 + 3] = last[:, :CHANS]


def conv_kernel(place_of, blocks, halo, far, weight, turned_weight, out, back, patches):
    low, first = place_of[0, 0] == 0, place_of[0, 1] == 0
    got = blocks[:, pl.ds(64, 48), :].astype(F32).reshape(16, 2, 48, LANES)
    mine = jnp.where(first, got[:, 0], got[:, 1])
    beside = jnp.where(first, got[:4, 1, :32], got[12:, 0, :32])
    edge = halo[...].astype(F32)
    left, right = jnp.where(first, edge, beside), jnp.where(first, beside, edge)

    for da, di, move in moves():
        patches[pl.ds((da * 3 + di) * CHANS, CHANS), :] = dot(far[0], move).astype(BF16)
    more = [dot(turned_weight[dr], patches[...]) for dr in (2, 0)]
    more = [jnp.where(low, 0.0, more[0]), jnp.where(low, more[1], 0.0)]
    for row, cells in enumerate(by_rows(mine[:, 32:])):
        back[row] = (cells.T[:CHANS] + more[row]).astype(BF16)

    rows = by_rows(jnp.concatenate([left, mine[:, :32], right], axis=0))
    inc = iota((6 * INC, LANES), 0) % INC
    moved = []
    for row in rows:
        moved.append(
            [
                jnp.where(inc > 0, pltpu.roll(row, 1, 0), 0.0).astype(BF16),
                row.astype(BF16),
                jnp.where(inc < INC - 1, pltpu.roll(row, 6 * INC - 1, 0), 0.0).astype(BF16),
            ]
        )
    for row in range(2):
        total = jnp.zeros((LANES, CHANS), F32)
        for tap in range(TAPS):
            dr, da, di = tap // 9, tap // 3 % 3, tap % 3
            patch = moved[row + dr][di][da * INC : da * INC + LANES, :CHANS]
            total = total + lax.dot_general(
                patch, weight[tap], (((1,), (1,)), ((), ())), preferred_element_type=F32
            )
        out[row] = total.T.astype(BF16)


def exchange(cells, axis):
    return lax.all_to_all(cells, axis, 0, 0, tiled=True)


def ring(count, closed):
    return [(i, (i + 1) % count) for i in range(count if closed else count - 1)]


def back_ring(count, closed):
    return [(j, i) for i, j in ring(count, closed)]


def shards(feats, counts, occupancy, window_ids, w_qkv, w_out, conv_weight, cotangent):
    struct = jax.ShapeDtypeStruct
    sectors = lax.axis_size(SECTOR)
    mine = pl.pallas_call(
        pack_kernel,
        out_shape=struct((16, 16, LANES), BF16),
        in_specs=[pl.BlockSpec(memory_space=pl.ANY)] * 4,
        scratch_shapes=[
            pltpu.VMEM((CHANS, 2, LANES), BF16),
            pltpu.VMEM((2, LANES), jnp.int32),
            pltpu.VMEM((2, LANES), jnp.int32),
            pltpu.VMEM((1, 2), jnp.int32),
            pltpu.SemaphoreType.DMA((4,)),
        ],
    )(feats, counts, window_ids.T, occupancy.T)
    partner = lax.ppermute(mine, "zh", [(0, 1), (1, 0)])
    cotangent, mine = lax.optimization_barrier((cotangent, mine))
    cot = cotangent.transpose(1, 0, 2)
    left = lax.ppermute(cot[:, :, -INC:], SECTOR, ring(sectors, True))
    right = lax.ppermute(cot[:, :, :INC], SECTOR, back_ring(sectors, True))
    loads = whole(load_kernel, struct((16, 96, LANES), BF16), mine, partner, left, cot, right)
    loads = exchange(loads, FACE)
    turned_weight = conv_weight.reshape(3, 9 * CHANS, CHANS).transpose(0, 2, 1)

    side, core = lax.axis_index("zh"), lax.axis_index("c")
    place_of = jnp.stack([side, core]).astype(jnp.int32).reshape(1, 2)
    smem, vmem = pl.BlockSpec(memory_space=pltpu.SMEM), pl.BlockSpec(memory_space=pltpu.VMEM)
    hbm = pl.BlockSpec(memory_space=pl.ANY)
    params = pltpu.CompilerParams(vmem_limit_bytes=32 * 1024 * 1024)
    plane, along, face = lax.axis_size(PLANE), lax.axis_size(RING), lax.axis_size(FACE)
    blocks = pl.pallas_call(
        ray_kernel,
        out_shape=struct((plane, 112, LANES), BF16),
        in_specs=[smem, vmem, hbm, hbm, vmem],
        scratch_shapes=[
            pltpu.VMEM((3 * CHANS, CHANS), BF16),
            pltpu.VMEM((CHANS, CHANS), BF16),
            pltpu.VMEM((9 * CHANS, 2 * LANES), BF16),
            pltpu.SemaphoreType.DMA((2,)),
        ],
        compiler_params=params,
    )(place_of, loads, w_qkv, w_out, turned_weight)
    blocks = exchange(blocks, PLANE)

    terms = whole(sum_kernel, struct((along, 64, LANES), BF16), blocks)
    terms, blocks, cot, left, right = lax.optimization_barrier((terms, blocks, cot, left, right))
    terms = whole(sum_kernel, struct((plane, 64, LANES), BF16), exchange(terms, RING))

    edge = lax.dynamic_slice(
        blocks.reshape(face, 2, 112, LANES), (12 * core, core, 64, 0), (4, 1, 32, LANES)
    ).reshape(4, 32, LANES)
    odd = [(i, (i + 1) % sectors) for i in range(1, sectors, 2)]
    halo = lax.ppermute(edge, SECTOR, odd + [(j, i) for i, j in odd])
    far = jnp.concatenate([left, cot, right], axis=2)
    far = jnp.where(side == 0, far[1:], far[:1])
    far = lax.ppermute(far, BAND, [(face - 1, face), (face, face - 1)])
    out, back = pl.pallas_call(
        conv_kernel,
        out_shape=(struct((2, CHANS, LANES), BF16),) * 2,
        in_specs=[smem] + [vmem] * 5,
        scratch_shapes=[pltpu.VMEM((9 * CHANS, LANES), BF16)],
        compiler_params=params,
    )(place_of, blocks, halo, far, conv_weight, turned_weight)
    out, back = out.transpose(1, 0, 2), back.transpose(1, 0, 2)

    terms, out, back = lax.optimization_barrier((terms, out, back))
    grad_weight = whole(
        unpack_kernel,
        struct((TAPS, CHANS, CHANS), F32),
        exchange(terms, PLANE).reshape(2048, LANES),
    )
    return (out, grad_weight, back)


def solution(mesh):
    mesh = Mesh(mesh.devices.reshape(2, 4, 4, 8, 2), BAND + SECTOR)
    in_specs = (
        P(None, BAND, SECTOR),
        P(BAND, SECTOR),
        P(BAND, SECTOR),
        P(SECTOR, BAND),
        P(),
        P(),
        P(),
        P(None, BAND, SECTOR),
    )
    out_specs = (P(None, BAND, SECTOR), P(), P(None, BAND, SECTOR))
    return jax.shard_map(shards, mesh=mesh, in_specs=in_specs, out_specs=out_specs, check_vma=False)
```

time: 165 us -> 133 us (0.81)
  the two profiles are of different devices: /device:TPU:352 before, /device:TPU:1 now
where the time goes in v3:
time: 133 us; the launch traced here: 132 us
  starting transfers between devices  59.3 us (45%)
  waiting for transfers between devices  30.1 us (23%)
  blocking collectives  26.1 us (20%)
  Pallas kernels  12.1 us (9%)
  local copies, waits for them, and re-layouts  3.39 us (3%)
    all_to_all x3, starting transfers between devices, exchange(): return lax.all_to_all(cells, axis, 0, 0, tiled=True)  32.9 us
    all_to_all x1, blocking collectives, exchange(): return lax.all_to_all(cells, axis, 0, 0, tiled=True)  26.1 us
    all_to_all x3, waiting for transfers between devices, exchange(): return lax.all_to_all(cells, axis, 0, 0, tiled=True)  18.1 us
    ppermute x1, starting transfers between devices, shards(): partner = lax.ppermute(mine, 'zh', [(0, 1), (1, 0)])  16.3 us
    ppermute x1, waiting for transfers between devices, shards(): halo = lax.ppermute(edge, SECTOR, odd + [(j, i) for i, j in odd])  8.56 us
    pallas_call x1, Pallas kernels, shards(): pl.pallas_call(ray_kernel, out_shape=struct((plane, 112, LANES), BF16), i...  4.75 us
    ppermute x1, starting transfers between devices, shards(): halo = lax.ppermute(edge, SECTOR, odd + [(j, i) for i, j in odd])  4.11 us
    pallas_call x4, Pallas kernels, whole(): pl.pallas_call(kernel, out_shape=outs, compiler_params=pltpu.CompilerPara...  3.84 us
  transfers between devices with their start and end apart: 8, of which 4 were waited for; matrix products, arithmetic and copies ran while one was open for 2% of the time, Pallas kernels for 1%

profile of v3, /device:TPU:1, one launch (start us, length us, event | category | flops | bytes accessed | tf_op | source)
XLA Modules:
  0.0 132.0 jit_solution(14616790751116529658)
XLA Ops:
  0.6 0.0 copy-start
  0.6 1.7 %shard_map.103.mine = bf16[16,16,128]{2,1,0:T(8,128)(2,1)} custom-call(bf16[96,2,128]{2,1,0:T(2,128)(2,1)} %feats_hbm.1, s32[2,128]{1,0:T(2,128)} %counts_hbm.1, s32[2,128]{1,0:T(2,128)} %bitcast.29, s32[1,2]{1,0:T(1,128)} %bitcast.30), custom_call_target="tpu_custom_call" | custom-call | tf_op jit(solution)/shard_map/pallas_call | solution.py:288
  2.4 16.3 %collective-permute-start = (bf16[16,16,128]{2,1,0:T(8,128)(2,1)}, bf16[16,16,128]{2,1,0:T(8,128)(2,1)S(1)}, u32[]{:S(2)}, u32[]{:S(2)}) collective-permute-start(bf16[16,16,128]{2,1,0:T(8,128)(2,1)} %shard_map.103.mine), channel_id=1, source_target_pairs={{0,256},{256,0},{1,257},{257,1},{2,258},{258,2},{3,259},{259,3},{4... | collective-permute-start | bytes 196616 | tf_op jit(solution)/shard_map/ppermute | solution.py:300
  18.6 0.8 copy.22
  19.4 0.1 fusion
  19.5 3.5 %collective-permute-start.1 = (bf16[2,96,32]{2,1,0:T(8,128)(2,1)S(1)}, bf16[2,96,32]{2,1,0:T(8,128)(2,1)S(1)}, u32[]{:S(2)}, u32[]{:S(2)}) collective-permute-start(bf16[2,96,32]{2,1,0:T(8,128)(2,1)S(1)} %get-tuple-element.34), channel_id=1, source_target_pairs={{0,1},{1,2},{2,3},{3,4},{4,5},{5,6},{6,7},{7,8},{8,9},{9,10},{10,1... | collective-permute-start | bytes 36872 | tf_op jit(solution)/shard_map/ppermute | solution.py:303
  23.0 1.9 %collective-permute-start.2 = (bf16[2,96,32]{2,1,0:T(8,128)(2,1)S(1)}, bf16[2,96,32]{2,1,0:T(8,128)(2,1)S(1)}, u32[]{:S(2)}, u32[]{:S(2)}) collective-permute-start(bf16[2,96,32]{2,1,0:T(8,128)(2,1)S(1)} %get-tuple-element.33), channel_id=1, source_target_pairs={{1,0},{2,1},{3,2},{4,3},{5,4},{6,5},{7,6},{8,7},{9,8},{10,9},{11,1... | collective-permute-start | bytes 36872 | tf_op jit(solution)/shard_map/ppermute | solution.py:304
  25.0 0.0 collective-permute-done.1.left
  25.0 3.5 %collective-permute-done.2.right = bf16[2,96,32]{2,1,0:T(8,128)(2,1)S(1)} collective-permute-done((bf16[2,96,32]{2,1,0:T(8,128)(2,1)S(1)}, bf16[2,96,32]{2,1,0:T(8,128)(2,1)S(1)}, u32[]{:S(2)}, u32[]{:S(2)}) %collective-permute-start.2) | collective-permute-done | bytes 12320 | tf_op jit(solution)/shard_map/ppermute | solution.py:304
  28.4 0.0 collective-permute-done.partner
  28.4 0.0 copy-start.1
  28.4 0.8 copy-done.1
  29.3 0.0 copy-start.2
  29.3 0.0 copy-start.3
  29.3 0.9 shard_map.104
  30.2 6.8 %all-to-all-start = ((bf16[16,96,128]{2,1,0:T(8,128)(2,1)}), bf16[16,96,128]{2,1,0:T(8,128)(2,1)S(1)}, u32[]{:S(2)}, u32[]{:S(2)}) async-start(bf16[16,96,128]{2,1,0:T(8,128)(2,1)} %shard_map.104), calls=%async_computation | async-start | bytes 786432 | tf_op jit(solution)/shard_map/all_to_all | solution.py:274
  37.0 0.0 copy-done
  37.0 0.3 copy.16
  37.3 0.1 add_bitcast_fusion.place_of
  37.4 7.8 %all-to-all-done.loads = bf16[16,96,128]{2,1,0:T(8,128)(2,1)S(1)} async-done(((bf16[16,96,128]{2,1,0:T(8,128)(2,1)}), bf16[16,96,128]{2,1,0:T(8,128)(2,1)S(1)}, u32[]{:S(2)}, u32[]{:S(2)}) %all-to-all-start) | async-done | bytes 393248 | tf_op jit(solution)/shard_map/all_to_all | solution.py:274
  45.2 0.0 copy-done.2
  45.2 0.0 copy-done.3
  45.2 4.7 %shard_map.105 = bf16[32,112,128]{2,1,0:T(8,128)(2,1)S(1)} custom-call(s32[1,2]{1,0:T(1,128)S(1)} %add_bitcast_fusion.place_of, bf16[16,96,128]{2,1,0:T(8,128)(2,1)S(1)} %all-to-all-done.loads, bf16[288,96]{1,0:T(8,128)(2,1)S(1)} %copy-done.2, bf16[96,96]{1,0:T(8,128)(2,1)S(1)} %copy-done.3, bf16[3,96,864]{2,1,0:T(8,128)(2,1)S(1)} %bitcast.20), custom_call_target="tpu_custom_call" | custom-call | tf_op jit(solution)/shard_map/pallas_call | solution.py:315
  50.0 26.1 %all_to_all.20.terms.blocks = bf16[32,112,128]{2,1,0:T(8,128)(2,1)S(1)} all-to-all(bf16[32,112,128]{2,1,0:T(8,128)(2,1)S(1)} %shard_map.105), channel_id=1, replica_groups=mesh['zh'=2,'y'=4,'x'=4,'zl'=8,'c'=2] {'y','x','c'}, dimensions={0} | all-to-all | bytes 1835008 | tf_op jit(solution)/shard_map/all_to_all | solution.py:274
  76.1 0.8 shard_map.106
  76.9 8.0 %all-to-all-start.2 = ((bf16[16,64,128]{2,1,0:T(8,128)(2,1)}), bf16[16,64,128]{2,1,0:T(8,128)(2,1)S(1)}, u32[]{:S(2)}, u32[]{:S(2)}) async-start(bf16[16,64,128]{2,1,0:T(8,128)(2,1)} %shard_map.106), calls=%async_computation.2 | async-start | bytes 524288 | tf_op jit(solution)/shard_map/all_to_all | solution.py:274
  84.9 0.1 pad_maximum_fusion
  85.1 0.7 collective-permute-start.4
  85.8 4.1 %collective-permute-start.3 = (bf16[4,32,128]{2,1,0:T(8,128)(2,1)S(1)}, bf16[4,32,128]{2,1,0:T(8,128)(2,1)S(1)}, u32[]{:S(2)}, u32[]{:S(2)}) collective-permute-start(bf16[4,32,128]{2,1,0:T(8,128)(2,1)S(1)} %dynamic-slice_bitcast_fusion), channel_id=1, source_target_pairs={{1,2},{3,4},{5,6},{7,8},{9,10},{11,12},{13,14},{15,0},{2,1},{4,3},... | collective-permute-start | bytes 98312 | tf_op jit(solution)/shard_map/ppermute | solution.py:337
  89.9 8.6 %collective-permute-done.3.halo = bf16[4,32,128]{2,1,0:T(8,128)(2,1)S(1)} collective-permute-done((bf16[4,32,128]{2,1,0:T(8,128)(2,1)S(1)}, bf16[4,32,128]{2,1,0:T(8,128)(2,1)S(1)}, u32[]{:S(2)}, u32[]{:S(2)}) %collective-permute-start.3) | collective-permute-done | bytes 32800 | tf_op jit(solution)/shard_map/ppermute | solution.py:337
  98.4 0.0 collective-permute-done.4.far
  98.4 1.8 %shard_map.108 = (bf16[2,96,128]{2,1,0:T(8,128)(2,1)S(1)}, bf16[2,96,128]{2,1,0:T(8,128)(2,1)S(1)}) custom-call(s32[1,2]{1,0:T(1,128)S(1)} %add_bitcast_fusion.place_of, bf16[32,112,128]{2,1,0:T(8,128)(2,1)S(1)} %all_to_all.20.terms.blocks, bf16[4,32,128]{2,1,0:T(8,128)(2,1)S(1)} %collective-permute-done.3.halo, ...), custom_call_target="tpu_custom_call" | custom-call | tf_op jit(solution)/shard_map/pallas_call | solution.py:341
  100.3 0.0 all-to-all-done.2.terms
  100.3 0.9 shard_map.107
  101.1 18.1 %all-to-all-start.3 = ((bf16[32,64,128]{2,1,0:T(8,128)(2,1)}), bf16[32,64,128]{2,1,0:T(8,128)(2,1)S(1)}, u32[]{:S(2)}, u32[]{:S(2)}) async-start(bf16[32,64,128]{2,1,0:T(8,128)(2,1)} %shard_map.107), calls=%async_computation.3 | async-start | bytes 1048576 | tf_op jit(solution)/shard_map/all_to_all | solution.py:274
  119.2 0.7 copy.18
  119.9 0.7 copy.19
  120.5 10.2 %all-to-all-done.3 = bf16[32,64,128]{2,1,0:T(8,128)(2,1)S(1)} async-done(((bf16[32,64,128]{2,1,0:T(8,128)(2,1)}), bf16[32,64,128]{2,1,0:T(8,128)(2,1)S(1)}, u32[]{:S(2)}, u32[]{:S(2)}) %all-to-all-start.3) | async-done | bytes 524320 | tf_op jit(solution)/shard_map/all_to_all | solution.py:274
  130.8 1.3 shard_map.109
  (2 shorter events, 0.0 us)
Async XLA Ops:
  0.6 36.3 %copy-start = (bf16[27,96,96]{2,1,0:T(8,128)(2,1)S(1)}, bf16[27,96,96]{2,1,0:T(8,128)(2,1)}, u32[]{:S(2)}) copy-start(bf16[27,96,96]{2,1,0:T(8,128)(2,1)} %weight.1) | copy-start | bytes 1492996
  2.4 26.1 %collective-permute-start = (bf16[16,16,128]{2,1,0:T(8,128)(2,1)}, bf16[16,16,128]{2,1,0:T(8,128)(2,1)S(1)}, u32[]{:S(2)}, u32[]{:S(2)}) collective-permute-start(bf16[16,16,128]{2,1,0:T(8,128)(2,1)} %shard_map.103.mine), channel_id=1, source_target_pairs={{0,256},{256,0},{1,257},{257,1},{2,258},{258,2},{3,259},{259,3},{4... | collective-permute-start | bytes 196616 | tf_op jit(solution)/shard_map/ppermute | solution.py:300
  19.5 5.4 %collective-permute-start.1 = (bf16[2,96,32]{2,1,0:T(8,128)(2,1)S(1)}, bf16[2,96,32]{2,1,0:T(8,128)(2,1)S(1)}, u32[]{:S(2)}, u32[]{:S(2)}) collective-permute-start(bf16[2,96,32]{2,1,0:T(8,128)(2,1)S(1)} %get-tuple-element.34), channel_id=1, source_target_pairs={{0,1},{1,2},{2,3},{3,4},{4,5},{5,6},{6,7},{7,8},{8,9},{9,10},{10,1... | collective-permute-start | bytes 36872 | tf_op jit(solution)/shard_map/ppermute | solution.py:303
  23.0 5.4 %collective-permute-start.2 = (bf16[2,96,32]{2,1,0:T(8,128)(2,1)S(1)}, bf16[2,96,32]{2,1,0:T(8,128)(2,1)S(1)}, u32[]{:S(2)}, u32[]{:S(2)}) collective-permute-start(bf16[2,96,32]{2,1,0:T(8,128)(2,1)S(1)} %get-tuple-element.33), channel_id=1, source_target_pairs={{1,0},{2,1},{3,2},{4,3},{5,4},{6,5},{7,6},{8,7},{9,8},{10,9},{11,1... | collective-permute-start | bytes 36872 | tf_op jit(solution)/shard_map/ppermute | solution.py:304
  28.4 0.8 copy-start.1
  29.3 15.9 %copy-start.2 = (bf16[288,96]{1,0:T(8,128)(2,1)S(1)}, bf16[288,96]{1,0:T(8,128)(2,1)}, u32[]{:S(2)}) copy-start(bf16[288,96]{1,0:T(8,128)(2,1)} %w_qkv_hbm.1) | copy-start | bytes 165892
  29.3 15.9 %copy-start.3 = (bf16[96,96]{1,0:T(8,128)(2,1)S(1)}, bf16[96,96]{1,0:T(8,128)(2,1)}, u32[]{:S(2)}) copy-start(bf16[96,96]{1,0:T(8,128)(2,1)} %w_out_hbm.1) | copy-start | bytes 55300
  30.2 15.0 %all-to-all-start = ((bf16[16,96,128]{2,1,0:T(8,128)(2,1)}), bf16[16,96,128]{2,1,0:T(8,128)(2,1)S(1)}, u32[]{:S(2)}, u32[]{:S(2)}) async-start(bf16[16,96,128]{2,1,0:T(8,128)(2,1)} %shard_map.104), calls=%async_computation | async-start | bytes 786432 | tf_op jit(solution)/shard_map/all_to_all | solution.py:274
  76.9 23.4 %all-to-all-start.2 = ((bf16[16,64,128]{2,1,0:T(8,128)(2,1)}), bf16[16,64,128]{2,1,0:T(8,128)(2,1)S(1)}, u32[]{:S(2)}, u32[]{:S(2)}) async-start(bf16[16,64,128]{2,1,0:T(8,128)(2,1)} %shard_map.106), calls=%async_computation.2 | async-start | bytes 524288 | tf_op jit(solution)/shard_map/all_to_all | solution.py:274
  85.1 13.4 %collective-permute-start.4 = (bf16[1,96,192]{2,1,0:T(8,128)(2,1)S(1)}, bf16[1,96,192]{2,1,0:T(8,128)(2,1)S(1)}, u32[]{:S(2)}, u32[]{:S(2)}) collective-permute-start(bf16[1,96,192]{2,1,0:T(8,128)(2,1)S(1)} %slice_select_fusion), channel_id=1, source_target_pairs={{240,256},{256,240},{241,257},{257,241},{242,258},{258,242},{243,2... | collective-permute-start | bytes 110600 | tf_op jit(solution)/shard_map/ppermute | solution.py:340
  85.8 12.7 %collective-permute-start.3 = (bf16[4,32,128]{2,1,0:T(8,128)(2,1)S(1)}, bf16[4,32,128]{2,1,0:T(8,128)(2,1)S(1)}, u32[]{:S(2)}, u32[]{:S(2)}) collective-permute-start(bf16[4,32,128]{2,1,0:T(8,128)(2,1)S(1)} %dynamic-slice_bitcast_fusion), channel_id=1, source_target_pairs={{1,2},{3,4},{5,6},{7,8},{9,10},{11,12},{13,14},{15,0},{2,1},{4,3},... | collective-permute-start | bytes 98312 | tf_op jit(solution)/shard_map/ppermute | solution.py:337
  101.1 29.6 %all-to-all-start.3 = ((bf16[32,64,128]{2,1,0:T(8,128)(2,1)}), bf16[32,64,128]{2,1,0:T(8,128)(2,1)S(1)}, u32[]{:S(2)}, u32[]{:S(2)}) async-start(bf16[32,64,128]{2,1,0:T(8,128)(2,1)} %shard_map.107), calls=%async_computation.3 | async-start | bytes 1048576 | tf_op jit(solution)/shard_map/all_to_all | solution.py:274

commit v4 on v3

--- a/solution.py
+++ b/solution.py
@@ -37,36 +37,49 @@
     return lax.broadcasted_iota(jnp.int32, shape, dim)
 
 
-def pack_kernel(feats_hbm, counts_hbm, ids_hbm, occupancy_hbm, out, feats, counts, ids, occupancy, sems):
-    copies = [
-        pltpu.make_async_copy(source, target, sems.at[i])
-        for i, (source, target) in enumerate(
-            [
-                (feats_hbm, feats),
-                (counts_hbm, counts),
-                (ids_hbm, ids),
-                (occupancy_hbm, occupancy),
-            ]
-        )
+def lower_half():
+    return lax.axis_index("zh") == 0
+
+
+def first_core():
+    return lax.axis_index("c") == 0
+
+
+def pack_kernel(
+    feats_hbm, counts_hbm, ids_hbm, occupancy_hbm, cot_hbm,
+    out, turned, to_core, to_chip, feats, counts, ids, occupancy, cot, sems,
+):
+    pairs = [
+        (feats_hbm, feats),
+        (counts_hbm, counts),
+        (ids_hbm, ids),
+        (occupancy_hbm, occupancy),
+        (cot_hbm, cot),
     ]
+    copies = [pltpu.make_async_copy(*pair, sems.at[i]) for i, pair in enumerate(pairs)]
     for copy in copies:
         copy.start()
     for copy in copies:
         copy.wait()
-    lane = iota((LANES, LANES), 1)
-    both = feats[...].astype(F32)
-    rows = []
+    both, each = feats[...].astype(F32), cot[...].astype(F32)
+    more = []
     for row in range(2):
+        out[pl.ds(row * CHANS, CHANS), :] = both[:, row, :].astype(BF16)
+        cells = each[:, row, :].astype(BF16)
+        turned[row] = cells
+        head, tail = each[:, row, :INC], each[:, row, LANES - INC :]
+        to_core[row] = jnp.where(first_core(), tail, head).astype(BF16)
+        to_chip[row] = jnp.where(first_core(), head, tail).astype(BF16)
         number = ids[row : row + 1, :]
         tag = jnp.where(occupancy[:, row : row + 1] == 1, number, -1)
-        more = [v.astype(F32) for v in (counts[row : row + 1, :], number, tag)]
-        more.append(jnp.zeros((LANES - CHANS - 3, LANES), F32))
-        cells = jnp.concatenate([both[:, row, :]] + more, axis=0)
-        rows.append(cells.T.reshape(16, 8, LANES))
-    out[...] = jnp.concatenate(rows, axis=1).astype(BF16)
-
-
-def ray_kernel(place_of, loads, w_qkv_hbm, w_out_hbm, turned_weight, out, w_qkv, w_out, patches, sems):
+        more += [v.astype(F32) for v in (counts[row : row + 1, :], number, tag)]
+        more.append(jnp.zeros((5, LANES), F32))
+    out[pl.ds(2 * CHANS, 16), :] = jnp.concatenate(more, axis=0).astype(BF16)
+    edge = jnp.where(lower_half(), each[:, 1, :], each[:, 0, :])
+    out[pl.ds(2 * CHANS + 16, CHANS), :] = edge.astype(BF16)
+
+
+def ray_kernel(loads, w_qkv_hbm, w_out_hbm, turned_weight, out, w_qkv, w_out, patches, sems):
     n, wide = 256, 384
     fetches = [
         pltpu.make_async_copy(w_qkv_hbm, w_qkv, sems.at[0]),
@@ -77,7 +90,7 @@
     every = loads[...].astype(F32)
     own = every[:, :16].reshape(n, LANES)
     other = every[:, 16:32].reshape(n, LANES)
-    low = place_of[0, 0] == 0
+    low = lower_half()
     edge = jnp.where(low, other[:8], other[n - 8 :])
     asked = jnp.concatenate([own, edge, jnp.zeros((wide - n - 8, LANES), F32)], axis=0)
 
@@ -182,13 +195,20 @@
             yield da, di, move.astype(F32).astype(BF16)
 
 
-def load_kernel(mine, partner, left, middle, right, out):
+def load_kernel(mine_hbm, partner_hbm, middle, from_core, from_chip, out, mine, partner, sems):
+    copies = [
+        pltpu.make_async_copy(mine_hbm, mine, sems.at[0]),
+        pltpu.make_async_copy(partner_hbm, partner, sems.at[1]),
+    ]
+    for copy in copies:
+        copy.start()
     inc = iota((6 * INC, LANES), 0) % INC
     rows = []
     for row in range(2):
         parts = []
-        for piece in (left, middle, right):
-            cells = piece[row].astype(F32)
+        core, chip = from_core[row].astype(F32), from_chip[row].astype(F32)
+        left, right = jnp.where(first_core(), chip, core), jnp.where(first_core(), core, chip)
+        for cells in (left, middle[row].astype(F32), right):
             more = jnp.zeros((LANES - CHANS, cells.shape[1]), F32)
             parts.append(jnp.concatenate([cells, more], axis=0).T)
         cells = jnp.concatenate(parts, axis=0)
@@ -203,8 +223,18 @@
             blocks.append(cells)
             edges += [lower[:, :1], upper[:, 7:]]
     edges.append(jnp.zeros((16, 4, LANES), F32))
-    out[:, pl.ds(0, 16), :] = mine[...]
-    out[:, pl.ds(16, 16), :] = partner[...]
+    for copy in copies:
+        copy.wait()
+    for half, packed in enumerate((mine, partner)):
+        voxels = []
+        for row in range(2):
+            parts = [
+                packed[pl.ds(row * CHANS, CHANS), :].astype(F32),
+                packed[pl.ds(2 * CHANS, 16), :].astype(F32)[row * 8 : row * 8 + 8],
+                jnp.zeros((LANES - CHANS - 8, LANES), F32),
+            ]
+            voxels.append(jnp.concatenate(parts, axis=0).T.reshape(16, 8, LANES))
+        out[:, pl.ds(half * 16, 16), :] = jnp.concatenate(voxels, axis=1).astype(BF16)
     out[:, pl.ds(32, 48), :] = jnp.concatenate(blocks, axis=1).astype(BF16)
     out[:, pl.ds(80, 16), :] = jnp.concatenate(edges, axis=1).astype(BF16)
 
@@ -233,16 +263,22 @@
             out[group * 4 + 3] = last[:, :CHANS]
 
 
-def conv_kernel(place_of, blocks, halo, far, weight, turned_weight, out, back, patches):
-    low, first = place_of[0, 0] == 0, place_of[0, 1] == 0
+def conv_kernel(blocks, halo, far, from_core, weight, turned_weight, out, back, patches):
+    low, first = lower_half(), first_core()
     got = blocks[:, pl.ds(64, 48), :].astype(F32).reshape(16, 2, 48, LANES)
     mine = jnp.where(first, got[:, 0], got[:, 1])
     beside = jnp.where(first, got[:4, 1, :32], got[12:, 0, :32])
-    edge = halo[...].astype(F32)
+    edge = halo[pl.ds(0, LANES), :].astype(F32).reshape(4, 32, LANES)
     left, right = jnp.where(first, edge, beside), jnp.where(first, beside, edge)
 
+    core, chip = from_core[...].astype(F32), halo[pl.ds(LANES, CHANS), :].astype(F32)
+    before, after = jnp.where(first, chip, core), jnp.where(first, core, chip)
+    beyond = [before[:, LANES - INC :], far[...].astype(F32), after[:, :INC]]
+    at = lax.axis_index("y") * lax.axis_size("x") + lax.axis_index("x")
+    reached = at == jnp.where(low, 15, 0)
+    beyond = jnp.where(reached, jnp.concatenate(beyond, axis=1), 0.0).astype(BF16)
     for da, di, move in moves():
-        patches[pl.ds((da * 3 + di) * CHANS, CHANS), :] = dot(far[0], move).astype(BF16)
+        patches[pl.ds((da * 3 + di) * CHANS, CHANS), :] = dot(beyond, move).astype(BF16)
     more = [dot(turned_weight[dr], patches[...]) for dr in (2, 0)]
     more = [jnp.where(low, 0.0, more[0]), jnp.where(low, more[1], 0.0)]
     for row, cells in enumerate(by_rows(mine[:, 32:])):
@@ -274,48 +310,51 @@
     return lax.all_to_all(cells, axis, 0, 0, tiled=True)
 
 
-def ring(count, closed):
-    return [(i, (i + 1) % count) for i in range(count if closed else count - 1)]
-
-
-def back_ring(count, closed):
-    return [(j, i) for i, j in ring(count, closed)]
-
-
 def shards(feats, counts, occupancy, window_ids, w_qkv, w_out, conv_weight, cotangent):
     struct = jax.ShapeDtypeStruct
     sectors = lax.axis_size(SECTOR)
-    mine = pl.pallas_call(
+    core = lax.axis_index("c")
+    plane, along, face = lax.axis_size(PLANE), lax.axis_size(RING), lax.axis_size(FACE)
+    vmem, hbm = pl.BlockSpec(memory_space=pltpu.VMEM), pl.BlockSpec(memory_space=pl.ANY)
+    params = pltpu.CompilerParams(vmem_limit_bytes=32 * 1024 * 1024)
+    chips = [(i, (i + 1) % sectors) for i in range(1, sectors, 2)]
+    chips += [(j, i) for i, j in chips]
+    swap = [(0, 1), (1, 0)]
+    packed, edge = (3 * CHANS + 16, LANES), struct((2, CHANS, INC), BF16)
+    mine, cot, to_core, to_chip = pl.pallas_call(
         pack_kernel,
-        out_shape=struct((16, 16, LANES), BF16),
-        in_specs=[pl.BlockSpec(memory_space=pl.ANY)] * 4,
+        out_shape=(struct(packed, BF16), struct((2, CHANS, LANES), BF16), edge, edge),
+        in_specs=[hbm] * 5,
         scratch_shapes=[
             pltpu.VMEM((CHANS, 2, LANES), BF16),
             pltpu.VMEM((2, LANES), jnp.int32),
             pltpu.VMEM((2, LANES), jnp.int32),
             pltpu.VMEM((1, 2), jnp.int32),
-            pltpu.SemaphoreType.DMA((4,)),
+            pltpu.VMEM((CHANS, 2, LANES), BF16),
+            pltpu.SemaphoreType.DMA((5,)),
         ],
-    )(feats, counts, window_ids.T, occupancy.T)
-    partner = lax.ppermute(mine, "zh", [(0, 1), (1, 0)])
-    cotangent, mine = lax.optimization_barrier((cotangent, mine))
-    cot = cotangent.transpose(1, 0, 2)
-    left = lax.ppermute(cot[:, :, -INC:], SECTOR, ring(sectors, True))
-    right = lax.ppermute(cot[:, :, :INC], SECTOR, back_ring(sectors, True))
-    loads = whole(load_kernel, struct((16, 96, LANES), BF16), mine, partner, left, cot, right)
+    )(feats, counts, window_ids.T, occupancy.T, cotangent)
+    partner = lax.ppermute(mine, "zh", swap)
+    from_core = lax.ppermute(to_core, "c", swap)
+    from_chip = lax.ppermute(to_chip, SECTOR, chips)
+    loads = pl.pallas_call(
+        load_kernel,
+        out_shape=struct((16, 96, LANES), BF16),
+        in_specs=[hbm, hbm, vmem, vmem, vmem],
+        scratch_shapes=[
+            pltpu.VMEM(packed, BF16),
+            pltpu.VMEM(packed, BF16),
+            pltpu.SemaphoreType.DMA((2,)),
+        ],
+        compiler_params=params,
+    )(mine, partner, cot, from_core, from_chip)
     loads = exchange(loads, FACE)
     turned_weight = conv_weight.reshape(3, 9 * CHANS, CHANS).transpose(0, 2, 1)
 
-    side, core = lax.axis_index("zh"), lax.axis_index("c")
-    place_of = jnp.stack([side, core]).astype(jnp.int32).reshape(1, 2)
-    smem, vmem = pl.BlockSpec(memory_space=pltpu.SMEM), pl.BlockSpec(memory_space=pltpu.VMEM)
-    hbm = pl.BlockSpec(memory_space=pl.ANY)
-    params = pltpu.CompilerParams(vmem_limit_bytes=32 * 1024 * 1024)
-    plane, along, face = lax.axis_size(PLANE), lax.axis_size(RING), lax.axis_size(FACE)
     blocks = pl.pallas_call(
         ray_kernel,
         out_shape=struct((plane, 112, LANES), BF16),
-        in_specs=[smem, vmem, hbm, hbm, vmem],
+        in_specs=[vmem, hbm, hbm, vmem],
         scratch_shapes=[
             pltpu.VMEM((3 * CHANS, CHANS), BF16),
             pltpu.VMEM((CHANS, CHANS), BF16),
@@ -323,28 +362,26 @@
             pltpu.SemaphoreType.DMA((2,)),
         ],
         compiler_params=params,
-    )(place_of, loads, w_qkv, w_out, turned_weight)
+    )(loads, w_qkv, w_out, turned_weight)
     blocks = exchange(blocks, PLANE)
 
     terms = whole(sum_kernel, struct((along, 64, LANES), BF16), blocks)
-    terms, blocks, cot, left, right = lax.optimization_barrier((terms, blocks, cot, left, right))
+    terms, blocks, partner = lax.optimization_barrier((terms, blocks, partner))
     terms = whole(sum_kernel, struct((plane, 64, LANES), BF16), exchange(terms, RING))
 
+    far = lax.ppermute(partner[2 * CHANS + 16 :], FACE, [(0, face - 1), (face - 1, 0)])
+    from_core = lax.ppermute(far, "c", swap)
     edge = lax.dynamic_slice(
         blocks.reshape(face, 2, 112, LANES), (12 * core, core, 64, 0), (4, 1, 32, LANES)
-    ).reshape(4, 32, LANES)
-    odd = [(i, (i + 1) % sectors) for i in range(1, sectors, 2)]
-    halo = lax.ppermute(edge, SECTOR, odd + [(j, i) for i, j in odd])
-    far = jnp.concatenate([left, cot, right], axis=2)
-    far = jnp.where(side == 0, far[1:], far[:1])
-    far = lax.ppermute(far, BAND, [(face - 1, face), (face, face - 1)])
+    ).reshape(LANES, LANES)
+    halo = lax.ppermute(jnp.concatenate([edge, far], axis=0), SECTOR, chips)
     out, back = pl.pallas_call(
         conv_kernel,
         out_shape=(struct((2, CHANS, LANES), BF16),) * 2,
-        in_specs=[smem] + [vmem] * 5,
+        in_specs=[vmem] * 6,
         scratch_shapes=[pltpu.VMEM((9 * CHANS, LANES), BF16)],
         compiler_params=params,
-    )(place_of, blocks, halo, far, conv_weight, turned_weight)
+    )(blocks, halo, far, from_core, conv_weight, turned_weight)
     out, back = out.transpose(1, 0, 2), back.transpose(1, 0, 2)
 
     terms, out, back = lax.optimization_barrier((terms, out, back))

time: 133 us -> 124 us (0.932)
  starting transfers between devices: 59.3 us -> 53.8 us
  waiting for transfers between devices: 30.1 us -> 27.3 us
    all_to_all x3, starting transfers between devices: 32.9 us -> 16.1 us  [exchange(): return lax.all_to_all(cells, axis, 0, 0, tiled=True)]
    ppermute x5 -> x6, starting transfers between devices: 26.5 us -> 37.6 us  [the longest x1 16.3 us: shards(): partner = lax.ppermute(mine, 'zh', swap)]
    ppermute x5 -> x6, waiting for transfers between devices: 12 us -> 9.02 us  [the longest x1 4.35 us: shards(): lax.ppermute(partner[2 * CHANS + 16:], FACE, [(0, face - 1), (face - 1, 0)])]
    pallas_call x1 -> x2, Pallas kernels: 1.71 us -> 3.27 us  [the longest x1 2.1 us: shards(): pl.pallas_call(pack_kernel, out_shape=(struct(packed, BF16), struct((2, C...]
    pallas_call x4 -> x3, Pallas kernels: 3.84 us -> 2.93 us  [whole(): pl.pallas_call(kernel, out_shape=outs, compiler_params=pltpu.CompilerPara...]
    unnamed x10 -> x12, local copies, waits for them, and re-layouts: 2.17 us -> 3.01 us
  transfers between devices with their start and end apart: 8 -> 9, of which waited for: 4 -> 5; matrix products, arithmetic and copies ran while one was open for 2% -> 1% of each run, Pallas kernels for 1% -> 1%
where the time goes in v4:
time: 124 us; the launch traced here: 123 us
  starting transfers between devices  53.8 us (43%)
  waiting for transfers between devices  27.3 us (22%)
  blocking collectives  26 us (21%)
  Pallas kernels  11.9 us (10%)
  local copies, waits for them, and re-layouts  3.36 us (3%)
    all_to_all x1, blocking collectives, exchange(): return lax.all_to_all(cells, axis, 0, 0, tiled=True)  26 us
    all_to_all x3, waiting for transfers between devices, exchange(): return lax.all_to_all(cells, axis, 0, 0, tiled=True)  18.3 us
    ppermute x1, starting transfers between devices, shards(): partner = lax.ppermute(mine, 'zh', swap)  16.3 us
    all_to_all x3, starting transfers between devices, exchange(): return lax.all_to_all(cells, axis, 0, 0, tiled=True)  16.1 us
    ppermute x1, starting transfers between devices, shards(): from_core = lax.ppermute(far, 'c', swap)  7.21 us
    ppermute x1, starting transfers between devices, shards(): halo = lax.ppermute(jnp.concatenate([edge, far], axis=0), SECTOR, chips)  4.94 us
    ppermute x1, waiting for transfers between devices, shards(): lax.ppermute(partner[2 * CHANS + 16:], FACE, [(0, face - 1), (face - 1, 0)])  4.35 us
    pallas_call x1, Pallas kernels, shards(): pl.pallas_call(ray_kernel, out_shape=struct((plane, 112, LANES), BF16), i...  4.19 us
  transfers between devices with their start and end apart: 9, of which 5 were waited for; matrix products, arithmetic and copies ran while one was open for 1% of the time, Pallas kernels for 1%

profile of v4, /device:TPU:1, one launch (start us, length us, event | category | flops | bytes accessed | tf_op | source)
XLA Modules:
  0.0 123.0 jit_solution(10236798291996536363)
XLA Ops:
  0.6 0.0 copy-start
  0.6 2.1 %shard_map.103 = (bf16[304,128]{1,0:T(8,128)(2,1)}, bf16[2,96,128]{2,1,0:T(8,128)(2,1)}, bf16[2,96,32]{2,1,0:T(8,128)(2,1)}, bf16[2,96,32]{2,1,0:T(8,128)(2,1)}) custom-call(bf16[96,2,128]{2,1,0:T(2,128)(2,1)} %feats_hbm.1, s32[2,128]{1,0:T(2,128)} %counts_hbm.1, s32[2,128]{1,0:T(2,128)} %bitcast.19, s32[1,2]{1,0:T(1,128)} %bitcast.20, ...), custom_call_target="tpu_custom_call" | custom-call | tf_op jit(solution)/shard_map/pallas_call | solution.py:324
  2.7 16.3 %collective-permute-start = (bf16[304,128]{1,0:T(8,128)(2,1)}, bf16[304,128]{1,0:T(8,128)(2,1)S(1)}, u32[]{:S(2)}, u32[]{:S(2)}) collective-permute-start(bf16[304,128]{1,0:T(8,128)(2,1)} %get-tuple-element.15.mine_hbm), channel_id=1, source_target_pairs={{0,256},{256,0},{1,257},{257,1},{2,258},{258,2},{3,259},{259,3},{4... | collective-permute-start | bytes 233480 | tf_op jit(solution)/shard_map/ppermute | solution.py:337
  19.0 2.9 %collective-permute-start.1 = (bf16[2,96,32]{2,1,0:T(8,128)(2,1)}, bf16[2,96,32]{2,1,0:T(8,128)(2,1)S(1)}, u32[]{:S(2)}, u32[]{:S(2)}) collective-permute-start(bf16[2,96,32]{2,1,0:T(8,128)(2,1)} %get-tuple-element.17), channel_id=1, source_target_pairs={{0,1},{1,0},{2,3},{3,2},{4,5},{5,4},{6,7},{7,6},{8,9},{9,8},{10,11... | collective-permute-start | bytes 36872 | tf_op jit(solution)/shard_map/ppermute | solution.py:338
  21.9 2.5 %collective-permute-start.2 = (bf16[2,96,32]{2,1,0:T(8,128)(2,1)}, bf16[2,96,32]{2,1,0:T(8,128)(2,1)S(1)}, u32[]{:S(2)}, u32[]{:S(2)}) collective-permute-start(bf16[2,96,32]{2,1,0:T(8,128)(2,1)} %get-tuple-element.18), channel_id=1, source_target_pairs={{1,2},{3,4},{5,6},{7,8},{9,10},{11,12},{13,14},{15,0},{2,1},{4,3},... | collective-permute-start | bytes 36872 | tf_op jit(solution)/shard_map/ppermute | solution.py:339
  24.4 0.0 collective-permute-done.1.from_core
  24.5 3.8 %collective-permute-done.2.from_chip = bf16[2,96,32]{2,1,0:T(8,128)(2,1)S(1)} collective-permute-done((bf16[2,96,32]{2,1,0:T(8,128)(2,1)}, bf16[2,96,32]{2,1,0:T(8,128)(2,1)S(1)}, u32[]{:S(2)}, u32[]{:S(2)}) %collective-permute-start.2) | collective-permute-done | bytes 12320 | tf_op jit(solution)/shard_map/ppermute | solution.py:339
  28.3 0.0 collective-permute-done.partner_hbm
  28.3 0.0 copy-start.1
  28.3 0.9 copy-done.1
  29.2 0.0 copy-start.3
  29.2 0.8 copy-done.3
  30.0 0.0 copy-start.2
  30.0 0.0 copy-start.4
  30.0 1.2 shard_map.104
  31.2 6.8 %all-to-all-start = ((bf16[16,96,128]{2,1,0:T(8,128)(2,1)}), bf16[16,96,128]{2,1,0:T(8,128)(2,1)S(1)}, u32[]{:S(2)}, u32[]{:S(2)}) async-start(bf16[16,96,128]{2,1,0:T(8,128)(2,1)} %shard_map.104), calls=%async_computation | async-start | bytes 786432 | tf_op jit(solution)/shard_map/all_to_all | solution.py:310
  38.0 0.0 copy-done
  38.0 0.3 copy.14
  38.3 7.9 %all-to-all-done.loads = bf16[16,96,128]{2,1,0:T(8,128)(2,1)S(1)} async-done(((bf16[16,96,128]{2,1,0:T(8,128)(2,1)}), bf16[16,96,128]{2,1,0:T(8,128)(2,1)S(1)}, u32[]{:S(2)}, u32[]{:S(2)}) %all-to-all-start) | async-done | bytes 393248 | tf_op jit(solution)/shard_map/all_to_all | solution.py:310
  46.2 0.0 copy-done.2
  46.2 0.0 copy-done.4
  46.2 4.2 %shard_map.105 = bf16[32,112,128]{2,1,0:T(8,128)(2,1)S(1)} custom-call(bf16[16,96,128]{2,1,0:T(8,128)(2,1)S(1)} %all-to-all-done.loads, bf16[288,96]{1,0:T(8,128)(2,1)S(1)} %copy-done.2, bf16[96,96]{1,0:T(8,128)(2,1)S(1)} %copy-done.4, bf16[3,96,864]{2,1,0:T(8,128)(2,1)S(1)} %bitcast.12), custom_call_target="tpu_custom_call" | custom-call | tf_op jit(solution)/shard_map/pallas_call | solution.py:354
  50.4 26.0 %all_to_all.20.terms.blocks = bf16[32,112,128]{2,1,0:T(8,128)(2,1)S(1)} all-to-all(bf16[32,112,128]{2,1,0:T(8,128)(2,1)S(1)} %shard_map.105), channel_id=1, replica_groups=mesh['zh'=2,'y'=4,'x'=4,'zl'=8,'c'=2] {'y','x','c'}, dimensions={0} | all-to-all | bytes 1835008 | tf_op jit(solution)/shard_map/all_to_all | solution.py:310
  76.4 0.8 shard_map.106
  77.2 3.5 %all-to-all-start.2 = ((bf16[16,64,128]{2,1,0:T(8,128)(2,1)}), bf16[16,64,128]{2,1,0:T(8,128)(2,1)S(1)}, u32[]{:S(2)}, u32[]{:S(2)}) async-start(bf16[16,64,128]{2,1,0:T(8,128)(2,1)} %shard_map.106), calls=%async_computation.2 | async-start | bytes 524288 | tf_op jit(solution)/shard_map/all_to_all | solution.py:310
  80.7 3.8 %collective-permute-start.3 = (bf16[96,128]{1,0:T(8,128)(2,1)S(1)}, bf16[96,128]{1,0:T(8,128)(2,1)S(1)}, u32[]{:S(2)}, u32[]{:S(2)}) collective-permute-start(bf16[96,128]{1,0:T(8,128)(2,1)S(1)} %slice.3), channel_id=1, source_target_pairs={{0,240},{240,0},{1,241},{241,1},{2,242},{242,2},{3,243},{243,3},{4... | collective-permute-start | bytes 73736 | tf_op jit(solution)/shard_map/ppermute | solution.py:372
  84.6 4.3 %collective-permute-done.3.far = bf16[96,128]{1,0:T(8,128)(2,1)S(1)} collective-permute-done((bf16[96,128]{1,0:T(8,128)(2,1)S(1)}, bf16[96,128]{1,0:T(8,128)(2,1)S(1)}, u32[]{:S(2)}, u32[]{:S(2)}) %collective-permute-start.3) | collective-permute-done | bytes 24608 | tf_op jit(solution)/shard_map/ppermute | solution.py:372
  88.9 4.9 %collective-permute-start.4 = (bf16[224,128]{1,0:T(8,128)(2,1)S(1)}, bf16[224,128]{1,0:T(8,128)(2,1)S(1)}, u32[]{:S(2)}, u32[]{:S(2)}) collective-permute-start(bf16[224,128]{1,0:T(8,128)(2,1)S(1)} %pad_maximum_fusion), channel_id=1, source_target_pairs={{1,2},{3,4},{5,6},{7,8},{9,10},{11,12},{13,14},{15,0},{2,1},{4,3},... | collective-permute-start | bytes 172040 | tf_op jit(solution)/shard_map/ppermute | solution.py:377
  93.9 7.2 %collective-permute-start.5 = (bf16[96,128]{1,0:T(8,128)(2,1)S(1)}, bf16[96,128]{1,0:T(8,128)(2,1)S(1)}, u32[]{:S(2)}, u32[]{:S(2)}) collective-permute-start(bf16[96,128]{1,0:T(8,128)(2,1)S(1)} %collective-permute-done.3.far), channel_id=1, source_target_pairs={{0,1},{1,0},{2,3},{3,2},{4,5},{5,4},{6,7},{7,6},{8,9},{9,8},{10,11... | collective-permute-start | bytes 73736 | tf_op jit(solution)/shard_map/ppermute | solution.py:373
  101.1 0.8 collective-permute-done.5.from_core
  101.9 0.0 collective-permute-done.4.halo
  101.9 1.5 %shard_map.108 = (bf16[2,96,128]{2,1,0:T(8,128)(2,1)S(1)}, bf16[2,96,128]{2,1,0:T(8,128)(2,1)S(1)}) custom-call(bf16[32,112,128]{2,1,0:T(8,128)(2,1)S(1)} %all_to_all.20.terms.blocks, bf16[224,128]{1,0:T(8,128)(2,1)S(1)} %collective-permute-done.4.halo, bf16[96,128]{1,0:T(8,128)(2,1)S(1)} %collective-permute-done.3.far, ...), custom_call_target="tpu_custom_call" | custom-call | tf_op jit(solution)/shard_map/pallas_call | solution.py:378
  103.4 0.0 all-to-all-done.2.terms
  103.4 0.9 shard_map.107
  104.3 5.8 %all-to-all-start.3 = ((bf16[32,64,128]{2,1,0:T(8,128)(2,1)}), bf16[32,64,128]{2,1,0:T(8,128)(2,1)S(1)}, u32[]{:S(2)}, u32[]{:S(2)}) async-start(bf16[32,64,128]{2,1,0:T(8,128)(2,1)} %shard_map.107), calls=%async_computation.3 | async-start | bytes 1048576 | tf_op jit(solution)/shard_map/all_to_all | solution.py:310
  110.1 0.7 copy.16
  110.8 0.7 copy.17
  111.4 10.3 %all-to-all-done.3 = bf16[32,64,128]{2,1,0:T(8,128)(2,1)S(1)} async-done(((bf16[32,64,128]{2,1,0:T(8,128)(2,1)}), bf16[32,64,128]{2,1,0:T(8,128)(2,1)S(1)}, u32[]{:S(2)}, u32[]{:S(2)}) %all-to-all-start.3) | async-done | bytes 524320 | tf_op jit(solution)/shard_map/all_to_all | solution.py:310
  121.8 1.3 %shard_map.109 = f32[27,96,96]{2,1,0:T(8,128)} custom-call(bf16[2048,128]{1,0:T(8,128)(2,1)S(1)} %bitcast.15), custom_call_target="tpu_custom_call" | custom-call | tf_op jit(solution)/shard_map/pallas_call | solution.py:25
  (3 shorter events, 0.0 us)
Async XLA Ops:
  0.6 37.3 %copy-start = (bf16[27,96,96]{2,1,0:T(8,128)(2,1)S(1)}, bf16[27,96,96]{2,1,0:T(8,128)(2,1)}, u32[]{:S(2)}) copy-start(bf16[27,96,96]{2,1,0:T(8,128)(2,1)} %weight.1) | copy-start | bytes 1492996
  2.7 25.6 %collective-permute-start = (bf16[304,128]{1,0:T(8,128)(2,1)}, bf16[304,128]{1,0:T(8,128)(2,1)S(1)}, u32[]{:S(2)}, u32[]{:S(2)}) collective-permute-start(bf16[304,128]{1,0:T(8,128)(2,1)} %get-tuple-element.15.mine_hbm), channel_id=1, source_target_pairs={{0,256},{256,0},{1,257},{257,1},{2,258},{258,2},{3,259},{259,3},{4... | collective-permute-start | bytes 233480 | tf_op jit(solution)/shard_map/ppermute | solution.py:337
  19.0 5.4 %collective-permute-start.1 = (bf16[2,96,32]{2,1,0:T(8,128)(2,1)}, bf16[2,96,32]{2,1,0:T(8,128)(2,1)S(1)}, u32[]{:S(2)}, u32[]{:S(2)}) collective-permute-start(bf16[2,96,32]{2,1,0:T(8,128)(2,1)} %get-tuple-element.17), channel_id=1, source_target_pairs={{0,1},{1,0},{2,3},{3,2},{4,5},{5,4},{6,7},{7,6},{8,9},{9,8},{10,11... | collective-permute-start | bytes 36872 | tf_op jit(solution)/shard_map/ppermute | solution.py:338
  21.9 6.4 %collective-permute-start.2 = (bf16[2,96,32]{2,1,0:T(8,128)(2,1)}, bf16[2,96,32]{2,1,0:T(8,128)(2,1)S(1)}, u32[]{:S(2)}, u32[]{:S(2)}) collective-permute-start(bf16[2,96,32]{2,1,0:T(8,128)(2,1)} %get-tuple-element.18), channel_id=1, source_target_pairs={{1,2},{3,4},{5,6},{7,8},{9,10},{11,12},{13,14},{15,0},{2,1},{4,3},... | collective-permute-start | bytes 36872 | tf_op jit(solution)/shard_map/ppermute | solution.py:339
  28.3 0.9 copy-start.1
  29.2 0.8 copy-start.3
  30.0 16.2 %copy-start.2 = (bf16[288,96]{1,0:T(8,128)(2,1)S(1)}, bf16[288,96]{1,0:T(8,128)(2,1)}, u32[]{:S(2)}) copy-start(bf16[288,96]{1,0:T(8,128)(2,1)} %w_qkv_hbm.1) | copy-start | bytes 165892
  30.0 16.2 %copy-start.4 = (bf16[96,96]{1,0:T(8,128)(2,1)S(1)}, bf16[96,96]{1,0:T(8,128)(2,1)}, u32[]{:S(2)}) copy-start(bf16[96,96]{1,0:T(8,128)(2,1)} %w_out_hbm.1) | copy-start | bytes 55300
  31.2 15.0 %all-to-all-start = ((bf16[16,96,128]{2,1,0:T(8,128)(2,1)}), bf16[16,96,128]{2,1,0:T(8,128)(2,1)S(1)}, u32[]{:S(2)}, u32[]{:S(2)}) async-start(bf16[16,96,128]{2,1,0:T(8,128)(2,1)} %shard_map.104), calls=%async_computation | async-start | bytes 786432 | tf_op jit(solution)/shard_map/all_to_all | solution.py:310
  77.2 26.3 %all-to-all-start.2 = ((bf16[16,64,128]{2,1,0:T(8,128)(2,1)}), bf16[16,64,128]{2,1,0:T(8,128)(2,1)S(1)}, u32[]{:S(2)}, u32[]{:S(2)}) async-start(bf16[16,64,128]{2,1,0:T(8,128)(2,1)} %shard_map.106), calls=%async_computation.2 | async-start | bytes 524288 | tf_op jit(solution)/shard_map/all_to_all | solution.py:310
  80.7 8.2 %collective-permute-start.3 = (bf16[96,128]{1,0:T(8,128)(2,1)S(1)}, bf16[96,128]{1,0:T(8,128)(2,1)S(1)}, u32[]{:S(2)}, u32[]{:S(2)}) collective-permute-start(bf16[96,128]{1,0:T(8,128)(2,1)S(1)} %slice.3), channel_id=1, source_target_pairs={{0,240},{240,0},{1,241},{241,1},{2,242},{242,2},{3,243},{243,3},{4... | collective-permute-start | bytes 73736 | tf_op jit(solution)/shard_map/ppermute | solution.py:372
  88.9 13.0 %collective-permute-start.4 = (bf16[224,128]{1,0:T(8,128)(2,1)S(1)}, bf16[224,128]{1,0:T(8,128)(2,1)S(1)}, u32[]{:S(2)}, u32[]{:S(2)}) collective-permute-start(bf16[224,128]{1,0:T(8,128)(2,1)S(1)} %pad_maximum_fusion), channel_id=1, source_target_pairs={{1,2},{3,4},{5,6},{7,8},{9,10},{11,12},{13,14},{15,0},{2,1},{4,3},... | collective-permute-start | bytes 172040 | tf_op jit(solution)/shard_map/ppermute | solution.py:377
  93.9 8.0 %collective-permute-start.5 = (bf16[96,128]{1,0:T(8,128)(2,1)S(1)}, bf16[96,128]{1,0:T(8,128)(2,1)S(1)}, u32[]{:S(2)}, u32[]{:S(2)}) collective-permute-start(bf16[96,128]{1,0:T(8,128)(2,1)S(1)} %collective-permute-done.3.far), channel_id=1, source_target_pairs={{0,1},{1,0},{2,3},{3,2},{4,5},{5,4},{6,7},{7,6},{8,9},{9,8},{10,11... | collective-permute-start | bytes 73736 | tf_op jit(solution)/shard_map/ppermute | solution.py:373
  104.3 17.5 %all-to-all-start.3 = ((bf16[32,64,128]{2,1,0:T(8,128)(2,1)}), bf16[32,64,128]{2,1,0:T(8,128)(2,1)S(1)}, u32[]{:S(2)}, u32[]{:S(2)}) async-start(bf16[32,64,128]{2,1,0:T(8,128)(2,1)} %shard_map.107), calls=%async_computation.3 | async-start | bytes 1048576 | tf_op jit(solution)/shard_map/all_to_all | solution.py:310

commit v5 on v4

--- a/solution.py
+++ b/solution.py
@@ -79,7 +79,7 @@
     out[pl.ds(2 * CHANS + 16, CHANS), :] = edge.astype(BF16)
 
 
-def ray_kernel(loads, w_qkv_hbm, w_out_hbm, turned_weight, out, w_qkv, w_out, patches, sems):
+def ray_kernel(loads, w_qkv_hbm, w_out_hbm, turned_weight, out, send, w_qkv, w_out, patches, terms, sems):
     n, wide = 256, 384
     fetches = [
         pltpu.make_async_copy(w_qkv_hbm, w_qkv, sems.at[0]),
@@ -171,19 +171,26 @@
             tile = tile.astype(BF16)
             for q in range(3):
                 at = (group * 3 + j) * CHANS + 32 * q
-                out[at // 64, pl.ds(at % 64, 32), :] = tile[32 * q : 32 * q + 32]
-    out[31, pl.ds(32, 32), :] = jnp.zeros((32, LANES), BF16)
+                core, face = at // 64 % 2, at // 128
+                terms[core, face, pl.ds(at % 64, 32), :] = tile[32 * q : 32 * q + 32]
+    terms[1, 15, pl.ds(32, 32), :] = jnp.zeros((32, LANES), BF16)
+    core = lax.axis_index("c")
+    out[:, pl.ds(0, 64), :] = terms[core]
+    send[...] = terms[1 - core]
 
     lane = iota((CHANS, n), 1)
     up, level, down = (dot(turned_weight[dr], patches[...]) for dr in range(3))
     back = level + jnp.where(lane < n - 8, pltpu.roll(up, n - 8, 1), 0.0)
     back = back + jnp.where(lane >= 8, pltpu.roll(down, 8, 1), 0.0)
     back = jnp.concatenate([back, jnp.zeros((LANES - CHANS, n), F32)], axis=0).T
-    back = back.astype(BF16).reshape(16, 16, LANES)
-    for face in range(16):
-        for core in range(2):
-            out[2 * face + core, pl.ds(64, 32), :] = pairs[face]
-            out[2 * face + core, pl.ds(96, 16), :] = back[face]
+    out[:, pl.ds(64, 32), :] = pairs
+    out[:, pl.ds(96, 16), :] = back.astype(BF16).reshape(16, 16, LANES)
+
+
+def join_kernel(blocks, got, out):
+    total = blocks[:, pl.ds(0, 64), :].astype(F32) + got[...].astype(F32)
+    out[:, pl.ds(0, 64), :] = total.astype(BF16)
+    out[:, pl.ds(64, 48), :] = blocks[:, pl.ds(64, 48), :]
 
 
 def moves():
@@ -195,13 +202,30 @@
             yield da, di, move.astype(F32).astype(BF16)
 
 
-def load_kernel(mine_hbm, partner_hbm, middle, from_core, from_chip, out, mine, partner, sems):
-    copies = [
-        pltpu.make_async_copy(mine_hbm, mine, sems.at[0]),
-        pltpu.make_async_copy(partner_hbm, partner, sems.at[1]),
-    ]
-    for copy in copies:
-        copy.start()
+def as_voxels(packed):
+    voxels = []
+    for row in range(2):
+        parts = [
+            packed[pl.ds(row * CHANS, CHANS), :].astype(F32),
+            packed[pl.ds(2 * CHANS, 16), :].astype(F32)[row * 8 : row * 8 + 8],
+            jnp.zeros((LANES - CHANS - 8, LANES), F32),
+        ]
+        voxels.append(jnp.concatenate(parts, axis=0).T.reshape(16, 8, LANES))
+    return jnp.concatenate(voxels, axis=1).astype(BF16)
+
+
+def partner_kernel(partner_hbm, loads_hbm, out_hbm, partner, voxels, sem):
+    del loads_hbm
+    fetch = pltpu.make_async_copy(partner_hbm, partner, sem)
+    fetch.start()
+    fetch.wait()
+    voxels[...] = as_voxels(partner)
+    put = pltpu.make_async_copy(voxels, out_hbm.at[:, pl.ds(16, 16), :], sem)
+    put.start()
+    put.wait()
+
+
+def load_kernel(mine, middle, from_core, from_chip, out):
     inc = iota((6 * INC, LANES), 0) % INC
     rows = []
     for row in range(2):
@@ -223,18 +247,8 @@
             blocks.append(cells)
             edges += [lower[:, :1], upper[:, 7:]]
     edges.append(jnp.zeros((16, 4, LANES), F32))
-    for copy in copies:
-        copy.wait()
-    for half, packed in enumerate((mine, partner)):
-        voxels = []
-        for row in range(2):
-            parts = [
-                packed[pl.ds(row * CHANS, CHANS), :].astype(F32),
-                packed[pl.ds(2 * CHANS, 16), :].astype(F32)[row * 8 : row * 8 + 8],
-                jnp.zeros((LANES - CHANS - 8, LANES), F32),
-            ]
-            voxels.append(jnp.concatenate(parts, axis=0).T.reshape(16, 8, LANES))
-        out[:, pl.ds(half * 16, 16), :] = jnp.concatenate(voxels, axis=1).astype(BF16)
+    out[:, pl.ds(0, 16), :] = as_voxels(mine)
+    out[:, pl.ds(16, 16), :] = jnp.zeros((16, 16, LANES), BF16)
     out[:, pl.ds(32, 48), :] = jnp.concatenate(blocks, axis=1).astype(BF16)
     out[:, pl.ds(80, 16), :] = jnp.concatenate(edges, axis=1).astype(BF16)
 
@@ -263,16 +277,13 @@
             out[group * 4 + 3] = last[:, :CHANS]
 
 
-def conv_kernel(blocks, halo, far, from_core, weight, turned_weight, out, back, patches):
+def conv_kernel(blocks, from_chip, far, from_core, weight, turned_weight, out, back, patches):
     low, first = lower_half(), first_core()
-    got = blocks[:, pl.ds(64, 48), :].astype(F32).reshape(16, 2, 48, LANES)
-    mine = jnp.where(first, got[:, 0], got[:, 1])
-    beside = jnp.where(first, got[:4, 1, :32], got[12:, 0, :32])
-    edge = halo[pl.ds(0, LANES), :].astype(F32).reshape(4, 32, LANES)
-    left, right = jnp.where(first, edge, beside), jnp.where(first, beside, edge)
-
-    core, chip = from_core[...].astype(F32), halo[pl.ds(LANES, CHANS), :].astype(F32)
-    before, after = jnp.where(first, chip, core), jnp.where(first, core, chip)
+    mine = blocks[:, pl.ds(64, 48), :].astype(F32)
+    core, chip = from_core[...].astype(F32), from_chip[...].astype(F32)
+    left, right = jnp.where(first, chip, core), jnp.where(first, core, chip)
+    before, after = left[LANES:], right[LANES:]
+    left, right = left[:LANES].reshape(4, 32, LANES), right[:LANES].reshape(4, 32, LANES)
     beyond = [before[:, LANES - INC :], far[...].astype(F32), after[:, :INC]]
     at = lax.axis_index("y") * lax.axis_size("x") + lax.axis_index("x")
     reached = at == jnp.where(low, 15, 0)
@@ -337,54 +348,61 @@
     partner = lax.ppermute(mine, "zh", swap)
     from_core = lax.ppermute(to_core, "c", swap)
     from_chip = lax.ppermute(to_chip, SECTOR, chips)
+    loads = whole(load_kernel, struct((16, 96, LANES), BF16), mine, cot, from_core, from_chip)
     loads = pl.pallas_call(
-        load_kernel,
+        partner_kernel,
         out_shape=struct((16, 96, LANES), BF16),
-        in_specs=[hbm, hbm, vmem, vmem, vmem],
+        in_specs=[hbm, hbm],
+        out_specs=hbm,
         scratch_shapes=[
             pltpu.VMEM(packed, BF16),
-            pltpu.VMEM(packed, BF16),
-            pltpu.SemaphoreType.DMA((2,)),
+            pltpu.VMEM((16, 16, LANES), BF16),
+            pltpu.SemaphoreType.DMA,
         ],
+        input_output_aliases={1: 0},
         compiler_params=params,
-    )(mine, partner, cot, from_core, from_chip)
+    )(partner, loads)
     loads = exchange(loads, FACE)
     turned_weight = conv_weight.reshape(3, 9 * CHANS, CHANS).transpose(0, 2, 1)
 
-    blocks = pl.pallas_call(
+    blocks, send = pl.pallas_call(
         ray_kernel,
-        out_shape=struct((plane, 112, LANES), BF16),
+        out_shape=(struct((face, 112, LANES), BF16), struct((face, 64, LANES), BF16)),
         in_specs=[vmem, hbm, hbm, vmem],
         scratch_shapes=[
             pltpu.VMEM((3 * CHANS, CHANS), BF16),
             pltpu.VMEM((CHANS, CHANS), BF16),
             pltpu.VMEM((9 * CHANS, 2 * LANES), BF16),
+            pltpu.VMEM((2, face, 64, LANES), BF16),
             pltpu.SemaphoreType.DMA((2,)),
         ],
         compiler_params=params,
     )(loads, w_qkv, w_out, turned_weight)
-    blocks = exchange(blocks, PLANE)
+    got = lax.ppermute(send, "c", swap)
+    blocks = exchange(whole(join_kernel, struct((face, 112, LANES), BF16), blocks, got), FACE)
 
     terms = whole(sum_kernel, struct((along, 64, LANES), BF16), blocks)
     terms, blocks, partner = lax.optimization_barrier((terms, blocks, partner))
     terms = whole(sum_kernel, struct((plane, 64, LANES), BF16), exchange(terms, RING))
 
     far = lax.ppermute(partner[2 * CHANS + 16 :], FACE, [(0, face - 1), (face - 1, 0)])
-    from_core = lax.ppermute(far, "c", swap)
-    edge = lax.dynamic_slice(
-        blocks.reshape(face, 2, 112, LANES), (12 * core, core, 64, 0), (4, 1, 32, LANES)
-    ).reshape(LANES, LANES)
-    halo = lax.ppermute(jnp.concatenate([edge, far], axis=0), SECTOR, chips)
+
+    def edge_of(start):
+        piece = lax.dynamic_slice(blocks, (start, 64, 0), (4, 32, LANES))
+        return jnp.concatenate([piece.reshape(LANES, LANES), far], axis=0)
+
+    from_chip = lax.ppermute(edge_of(12 * core), SECTOR, chips)
+    from_core = lax.ppermute(edge_of(12 * (1 - core)), "c", swap)
     out, back = pl.pallas_call(
         conv_kernel,
         out_shape=(struct((2, CHANS, LANES), BF16),) * 2,
         in_specs=[vmem] * 6,
         scratch_shapes=[pltpu.VMEM((9 * CHANS, LANES), BF16)],
         compiler_params=params,
-    )(blocks, halo, far, from_core, conv_weight, turned_weight)
+        cost_estimate=pl.CostEstimate(flops=10**11, bytes_accessed=2**21, transcendentals=0),
+    )(blocks, from_chip, far, from_core, conv_weight, turned_weight)
     out, back = out.transpose(1, 0, 2), back.transpose(1, 0, 2)
 
-    terms, out, back = lax.optimization_barrier((terms, out, back))
     grad_weight = whole(
         unpack_kernel,
         struct((TAPS, CHANS, CHANS), F32),

time: 124 us -> 120 us (0.968)
  blocking collectives: 26 us -> 12.6 us
  starting transfers between devices: 53.8 us -> 63.7 us
    all_to_all x1, blocking collectives: 26 us -> 12.6 us  [exchange(): return lax.all_to_all(cells, axis, 0, 0, tiled=True)]
    all_to_all x3, starting transfers between devices: 16.1 us -> 21.5 us  [exchange(): return lax.all_to_all(cells, axis, 0, 0, tiled=True)]
    ppermute x2 -> x3, starting transfers between devices: 12.2 us -> 17.5 us  [the longest x1 9.17 us: shards(): got = lax.ppermute(send, 'c', swap)]
    all_to_all x3, waiting for transfers between devices: 18.3 us -> 16.8 us  [exchange(): return lax.all_to_all(cells, axis, 0, 0, tiled=True)]
    pallas_call x3 -> x5, Pallas kernels: 2.93 us -> 3.87 us  [whole(): pl.pallas_call(kernel, out_shape=outs, compiler_params=pltpu.CompilerPara...]
  transfers between devices with their start and end apart: 9 -> 10, of which waited for: 5 -> 5; matrix products, arithmetic and copies ran while one was open for 1% -> 1% of each run, Pallas kernels for 1% -> 3%
where the time goes in v5:
time: 120 us
  starting transfers between devices  63.7 us (53%)
  waiting for transfers between devices  26.6 us (22%)
  blocking collectives  12.6 us (10%)
  Pallas kernels  12.5 us (10%)
  local copies, waits for them, and re-layouts  3.36 us (3%)
    all_to_all x3, starting transfers between devices, exchange(): return lax.all_to_all(cells, axis, 0, 0, tiled=True)  21.5 us
    all_to_all x3, waiting for transfers between devices, exchange(): return lax.all_to_all(cells, axis, 0, 0, tiled=True)  16.8 us
    ppermute x1, starting transfers between devices, shards(): partner = lax.ppermute(mine, 'zh', swap)  16.3 us
    all_to_all x1, blocking collectives, exchange(): return lax.all_to_all(cells, axis, 0, 0, tiled=True)  12.6 us
    ppermute x1, starting transfers between devices, shards(): got = lax.ppermute(send, 'c', swap)  9.17 us
    ppermute x1, starting transfers between devices, shards(): from_core = lax.ppermute(edge_of(12 * (1 - core)), 'c', swap)  4.9 us
    ppermute x1, waiting for transfers between devices, shards(): lax.ppermute(partner[2 * CHANS + 16:], FACE, [(0, face - 1), (face - 1, 0)])  4.81 us
    pallas_call x1, Pallas kernels, shards(): pl.pallas_call(ray_kernel, out_shape=(struct((face, 112, LANES), BF16), s...  4.28 us
  transfers between devices with their start and end apart: 10, of which 5 were waited for; matrix products, arithmetic and copies ran while one was open for 1% of the time, Pallas kernels for 3%

profile of v5, /device:TPU:1, one launch (start us, length us, event | category | flops | bytes accessed | tf_op | source)
XLA Modules:
  0.0 119.6 jit_solution(4279973912110633037)
XLA Ops:
  0.6 0.0 copy-start
  0.6 2.1 %shard_map.103 = (bf16[304,128]{1,0:T(8,128)(2,1)}, bf16[2,96,128]{2,1,0:T(8,128)(2,1)}, bf16[2,96,32]{2,1,0:T(8,128)(2,1)}, bf16[2,96,32]{2,1,0:T(8,128)(2,1)}) custom-call(bf16[96,2,128]{2,1,0:T(2,128)(2,1)} %feats_hbm.1, s32[2,128]{1,0:T(2,128)} %counts_hbm.1, s32[2,128]{1,0:T(2,128)} %bitcast.17, s32[1,2]{1,0:T(1,128)} %bitcast.18, ...), custom_call_target="tpu_custom_call" | custom-call | tf_op jit(solution)/shard_map/pallas_call | solution.py:335
  2.7 16.3 %collective-permute-start = (bf16[304,128]{1,0:T(8,128)(2,1)}, bf16[304,128]{1,0:T(8,128)(2,1)S(1)}, u32[]{:S(2)}, u32[]{:S(2)}) collective-permute-start(bf16[304,128]{1,0:T(8,128)(2,1)} %get-tuple-element.14.mine), channel_id=1, source_target_pairs={{0,256},{256,0},{1,257},{257,1},{2,258},{258,2},{3,259},{259,3},{4... | collective-permute-start | bytes 233480 | tf_op jit(solution)/shard_map/ppermute | solution.py:348
  19.0 2.9 %collective-permute-start.1 = (bf16[2,96,32]{2,1,0:T(8,128)(2,1)}, bf16[2,96,32]{2,1,0:T(8,128)(2,1)S(1)}, u32[]{:S(2)}, u32[]{:S(2)}) collective-permute-start(bf16[2,96,32]{2,1,0:T(8,128)(2,1)} %get-tuple-element.16), channel_id=1, source_target_pairs={{0,1},{1,0},{2,3},{3,2},{4,5},{5,4},{6,7},{7,6},{8,9},{9,8},{10,11... | collective-permute-start | bytes 36872 | tf_op jit(solution)/shard_map/ppermute | solution.py:349
  21.9 2.5 %collective-permute-start.2 = (bf16[2,96,32]{2,1,0:T(8,128)(2,1)}, bf16[2,96,32]{2,1,0:T(8,128)(2,1)S(1)}, u32[]{:S(2)}, u32[]{:S(2)}) collective-permute-start(bf16[2,96,32]{2,1,0:T(8,128)(2,1)} %get-tuple-element.17), channel_id=1, source_target_pairs={{1,2},{3,4},{5,6},{7,8},{9,10},{11,12},{13,14},{15,0},{2,1},{4,3},... | collective-permute-start | bytes 36872 | tf_op jit(solution)/shard_map/ppermute | solution.py:350
  24.4 0.0 collective-permute-done.1.from_core
  24.4 3.8 %collective-permute-done.2.from_chip = bf16[2,96,32]{2,1,0:T(8,128)(2,1)S(1)} collective-permute-done((bf16[2,96,32]{2,1,0:T(8,128)(2,1)}, bf16[2,96,32]{2,1,0:T(8,128)(2,1)S(1)}, u32[]{:S(2)}, u32[]{:S(2)}) %collective-permute-start.2) | collective-permute-done | bytes 12320 | tf_op jit(solution)/shard_map/ppermute | solution.py:350
  28.3 0.0 copy-start.1
  28.3 0.9 copy-done.1
  29.2 0.0 copy-start.3
  29.2 0.8 copy-done.3
  30.0 0.9 shard_map.104.loads_hbm
  30.9 0.0 copy-start.2
  30.9 0.0 copy-start.4
  30.9 0.0 collective-permute-done.partner_hbm
  30.9 0.8 shard_map.105
  31.7 6.8 %all-to-all-start = ((bf16[16,96,128]{2,1,0:T(8,128)(2,1)}), bf16[16,96,128]{2,1,0:T(8,128)(2,1)S(1)}, u32[]{:S(2)}, u32[]{:S(2)}) async-start(bf16[16,96,128]{2,1,0:T(8,128)(2,1)} %shard_map.105), calls=%async_computation | async-start | bytes 786432 | tf_op jit(solution)/shard_map/all_to_all | solution.py:321
  38.5 0.0 copy-done
  38.5 0.3 copy.14
  38.9 7.9 %all-to-all-done.loads = bf16[16,96,128]{2,1,0:T(8,128)(2,1)S(1)} async-done(((bf16[16,96,128]{2,1,0:T(8,128)(2,1)}), bf16[16,96,128]{2,1,0:T(8,128)(2,1)S(1)}, u32[]{:S(2)}, u32[]{:S(2)}) %all-to-all-start) | async-done | bytes 393248 | tf_op jit(solution)/shard_map/all_to_all | solution.py:321
  46.8 0.0 copy-done.2
  46.8 0.0 copy-done.4
  46.8 4.3 %shard_map.106 = (bf16[16,112,128]{2,1,0:T(8,128)(2,1)S(1)}, bf16[16,64,128]{2,1,0:T(8,128)(2,1)S(1)}) custom-call(bf16[16,96,128]{2,1,0:T(8,128)(2,1)S(1)} %all-to-all-done.loads, bf16[288,96]{1,0:T(8,128)(2,1)S(1)} %copy-done.2, bf16[96,96]{1,0:T(8,128)(2,1)S(1)} %copy-done.4, bf16[3,96,864]{2,1,0:T(8,128)(2,1)S(1)} %bitcast.10), custom_call_target="tpu_custom_call" | custom-call | tf_op jit(solution)/shard_map/pallas_call | solution.py:368
  51.1 9.2 %collective-permute-start.3 = (bf16[16,64,128]{2,1,0:T(8,128)(2,1)S(1)}, bf16[16,64,128]{2,1,0:T(8,128)(2,1)S(1)}, u32[]{:S(2)}, u32[]{:S(2)}) collective-permute-start(bf16[16,64,128]{2,1,0:T(8,128)(2,1)S(1)} %get-tuple-element.19), channel_id=1, source_target_pairs={{0,1},{1,0},{2,3},{3,2},{4,5},{5,4},{6,7},{7,6},{8,9},{9,8},{10,11... | collective-permute-start | bytes 786440 | tf_op jit(solution)/shard_map/ppermute | solution.py:381
  60.2 1.1 collective-permute-done.3.got
  61.4 0.1 shard_map.107
  61.4 12.6 %all_to_all.20.terms.blocks = bf16[16,112,128]{2,1,0:T(8,128)(2,1)S(1)} all-to-all(bf16[16,112,128]{2,1,0:T(8,128)(2,1)S(1)} %shard_map.107), channel_id=1, replica_groups=mesh['zh'=2,'y'=4,'x'=4,'zl'=8,'c'=2] {'y','x'}, dimensions={0} | all-to-all | bytes 917504 | tf_op jit(solution)/shard_map/all_to_all | solution.py:321
  74.0 0.8 shard_map.108
  74.8 4.1 %all-to-all-start.2 = ((bf16[16,64,128]{2,1,0:T(8,128)(2,1)}), bf16[16,64,128]{2,1,0:T(8,128)(2,1)S(1)}, u32[]{:S(2)}, u32[]{:S(2)}) async-start(bf16[16,64,128]{2,1,0:T(8,128)(2,1)} %shard_map.108), calls=%async_computation.2 | async-start | bytes 524288 | tf_op jit(solution)/shard_map/all_to_all | solution.py:321
  78.9 3.0 %collective-permute-start.4 = (bf16[96,128]{1,0:T(8,128)(2,1)S(1)}, bf16[96,128]{1,0:T(8,128)(2,1)S(1)}, u32[]{:S(2)}, u32[]{:S(2)}) collective-permute-start(bf16[96,128]{1,0:T(8,128)(2,1)S(1)} %slice.3), channel_id=1, source_target_pairs={{0,240},{240,0},{1,241},{241,1},{2,242},{242,2},{3,243},{243,3},{4... | collective-permute-start | bytes 73736 | tf_op jit(solution)/shard_map/ppermute | solution.py:388
  81.9 4.8 %collective-permute-done.4.far = bf16[96,128]{1,0:T(8,128)(2,1)S(1)} collective-permute-done((bf16[96,128]{1,0:T(8,128)(2,1)S(1)}, bf16[96,128]{1,0:T(8,128)(2,1)S(1)}, u32[]{:S(2)}, u32[]{:S(2)}) %collective-permute-start.4) | collective-permute-done | bytes 24608 | tf_op jit(solution)/shard_map/ppermute | solution.py:388
  86.8 4.9 %collective-permute-start.6 = (bf16[224,128]{1,0:T(8,128)(2,1)S(1)}, bf16[224,128]{1,0:T(8,128)(2,1)S(1)}, u32[]{:S(2)}, u32[]{:S(2)}) collective-permute-start(bf16[224,128]{1,0:T(8,128)(2,1)S(1)} %get-tuple-element.33), channel_id=1, source_target_pairs={{0,1},{1,0},{2,3},{3,2},{4,5},{5,4},{6,7},{7,6},{8,9},{9,8},{10,11... | collective-permute-start | bytes 172040 | tf_op jit(solution)/shard_map/ppermute | solution.py:395
  91.7 3.4 %collective-permute-start.5 = (bf16[224,128]{1,0:T(8,128)(2,1)S(1)}, bf16[224,128]{1,0:T(8,128)(2,1)S(1)}, u32[]{:S(2)}, u32[]{:S(2)}) collective-permute-start(bf16[224,128]{1,0:T(8,128)(2,1)S(1)} %get-tuple-element.34), channel_id=1, source_target_pairs={{1,2},{3,4},{5,6},{7,8},{9,10},{11,12},{13,14},{15,0},{2,1},{4,3},... | collective-permute-start | bytes 172040 | tf_op jit(solution)/shard_map/ppermute | solution.py:394
  95.1 0.0 all-to-all-done.2.terms
  95.1 0.9 shard_map.110
  96.0 10.6 %all-to-all-start.3 = ((bf16[32,64,128]{2,1,0:T(8,128)(2,1)}), bf16[32,64,128]{2,1,0:T(8,128)(2,1)S(1)}, u32[]{:S(2)}, u32[]{:S(2)}) async-start(bf16[32,64,128]{2,1,0:T(8,128)(2,1)} %shard_map.110), calls=%async_computation.3 | async-start | bytes 1048576 | tf_op jit(solution)/shard_map/all_to_all | solution.py:321
  106.7 0.0 collective-permute-done.6.from_core
  106.7 0.0 collective-permute-done.5.from_chip
  106.7 1.4 %shard_map.109 = (bf16[2,96,128]{2,1,0:T(8,128)(2,1)S(1)}, bf16[2,96,128]{2,1,0:T(8,128)(2,1)S(1)}) custom-call(bf16[16,112,128]{2,1,0:T(8,128)(2,1)S(1)} %all_to_all.20.terms.blocks, bf16[224,128]{1,0:T(8,128)(2,1)S(1)} %collective-permute-done.5.from_chip, bf16[96,128]{1,0:T(8,128)(2,1)S(1)} %collective-permute-done.4.far, ...), custom_call_target="tpu_custom_call" | custom-call | flops 99999997952 | bytes 2097152 | tf_op jit(solution)/shard_map/pallas_call | solution.py:396
  108.1 0.7 copy.15
  108.8 0.7 copy.16
  109.4 8.9 %all-to-all-done.3 = bf16[32,64,128]{2,1,0:T(8,128)(2,1)S(1)} async-done(((bf16[32,64,128]{2,1,0:T(8,128)(2,1)}), bf16[32,64,128]{2,1,0:T(8,128)(2,1)S(1)}, u32[]{:S(2)}, u32[]{:S(2)}) %all-to-all-start.3) | async-done | bytes 524320 | tf_op jit(solution)/shard_map/all_to_all | solution.py:321
  118.3 1.3 %shard_map.111 = f32[27,96,96]{2,1,0:T(8,128)} custom-call(bf16[2048,128]{1,0:T(8,128)(2,1)S(1)} %bitcast.9), custom_call_target="tpu_custom_call" | custom-call | tf_op jit(solution)/shard_map/pallas_call | solution.py:25
  (3 shorter events, 0.0 us)
Async XLA Ops:
  0.6 37.9 %copy-start = (bf16[27,96,96]{2,1,0:T(8,128)(2,1)S(1)}, bf16[27,96,96]{2,1,0:T(8,128)(2,1)}, u32[]{:S(2)}) copy-start(bf16[27,96,96]{2,1,0:T(8,128)(2,1)} %weight.1) | copy-start | bytes 1492996
  2.7 28.2 %collective-permute-start = (bf16[304,128]{1,0:T(8,128)(2,1)}, bf16[304,128]{1,0:T(8,128)(2,1)S(1)}, u32[]{:S(2)}, u32[]{:S(2)}) collective-permute-start(bf16[304,128]{1,0:T(8,128)(2,1)} %get-tuple-element.14.mine), channel_id=1, source_target_pairs={{0,256},{256,0},{1,257},{257,1},{2,258},{258,2},{3,259},{259,3},{4... | collective-permute-start | bytes 233480 | tf_op jit(solution)/shard_map/ppermute | solution.py:348
  19.0 5.4 %collective-permute-start.1 = (bf16[2,96,32]{2,1,0:T(8,128)(2,1)}, bf16[2,96,32]{2,1,0:T(8,128)(2,1)S(1)}, u32[]{:S(2)}, u32[]{:S(2)}) collective-permute-start(bf16[2,96,32]{2,1,0:T(8,128)(2,1)} %get-tuple-element.16), channel_id=1, source_target_pairs={{0,1},{1,0},{2,3},{3,2},{4,5},{5,4},{6,7},{7,6},{8,9},{9,8},{10,11... | collective-permute-start | bytes 36872 | tf_op jit(solution)/shard_map/ppermute | solution.py:349
  21.9 6.4 %collective-permute-start.2 = (bf16[2,96,32]{2,1,0:T(8,128)(2,1)}, bf16[2,96,32]{2,1,0:T(8,128)(2,1)S(1)}, u32[]{:S(2)}, u32[]{:S(2)}) collective-permute-start(bf16[2,96,32]{2,1,0:T(8,128)(2,1)} %get-tuple-element.17), channel_id=1, source_target_pairs={{1,2},{3,4},{5,6},{7,8},{9,10},{11,12},{13,14},{15,0},{2,1},{4,3},... | collective-permute-start | bytes 36872 | tf_op jit(solution)/shard_map/ppermute | solution.py:350
  28.3 0.9 copy-start.1
  29.2 0.8 copy-start.3
  30.9 15.9 %copy-start.2 = (bf16[288,96]{1,0:T(8,128)(2,1)S(1)}, bf16[288,96]{1,0:T(8,128)(2,1)}, u32[]{:S(2)}) copy-start(bf16[288,96]{1,0:T(8,128)(2,1)} %w_qkv_hbm.1) | copy-start | bytes 165892
  30.9 15.9 %copy-start.4 = (bf16[96,96]{1,0:T(8,128)(2,1)S(1)}, bf16[96,96]{1,0:T(8,128)(2,1)}, u32[]{:S(2)}) copy-start(bf16[96,96]{1,0:T(8,128)(2,1)} %w_out_hbm.1) | copy-start | bytes 55300
  31.7 15.0 %all-to-all-start = ((bf16[16,96,128]{2,1,0:T(8,128)(2,1)}), bf16[16,96,128]{2,1,0:T(8,128)(2,1)S(1)}, u32[]{:S(2)}, u32[]{:S(2)}) async-start(bf16[16,96,128]{2,1,0:T(8,128)(2,1)} %shard_map.105), calls=%async_computation | async-start | bytes 786432 | tf_op jit(solution)/shard_map/all_to_all | solution.py:321
  51.1 10.3 %collective-permute-start.3 = (bf16[16,64,128]{2,1,0:T(8,128)(2,1)S(1)}, bf16[16,64,128]{2,1,0:T(8,128)(2,1)S(1)}, u32[]{:S(2)}, u32[]{:S(2)}) collective-permute-start(bf16[16,64,128]{2,1,0:T(8,128)(2,1)S(1)} %get-tuple-element.19), channel_id=1, source_target_pairs={{0,1},{1,0},{2,3},{3,2},{4,5},{5,4},{6,7},{7,6},{8,9},{9,8},{10,11... | collective-permute-start | bytes 786440 | tf_op jit(solution)/shard_map/ppermute | solution.py:381
  74.8 20.4 %all-to-all-start.2 = ((bf16[16,64,128]{2,1,0:T(8,128)(2,1)}), bf16[16,64,128]{2,1,0:T(8,128)(2,1)S(1)}, u32[]{:S(2)}, u32[]{:S(2)}) async-start(bf16[16,64,128]{2,1,0:T(8,128)(2,1)} %shard_map.108), calls=%async_computation.2 | async-start | bytes 524288 | tf_op jit(solution)/shard_map/all_to_all | solution.py:321
  78.9 7.9 %collective-permute-start.4 = (bf16[96,128]{1,0:T(8,128)(2,1)S(1)}, bf16[96,128]{1,0:T(8,128)(2,1)S(1)}, u32[]{:S(2)}, u32[]{:S(2)}) collective-permute-start(bf16[96,128]{1,0:T(8,128)(2,1)S(1)} %slice.3), channel_id=1, source_target_pairs={{0,240},{240,0},{1,241},{241,1},{2,242},{242,2},{3,243},{243,3},{4... | collective-permute-start | bytes 73736 | tf_op jit(solution)/shard_map/ppermute | solution.py:388
  86.8 19.9 %collective-permute-start.6 = (bf16[224,128]{1,0:T(8,128)(2,1)S(1)}, bf16[224,128]{1,0:T(8,128)(2,1)S(1)}, u32[]{:S(2)}, u32[]{:S(2)}) collective-permute-start(bf16[224,128]{1,0:T(8,128)(2,1)S(1)} %get-tuple-element.33), channel_id=1, source_target_pairs={{0,1},{1,0},{2,3},{3,2},{4,5},{5,4},{6,7},{7,6},{8,9},{9,8},{10,11... | collective-permute-start | bytes 172040 | tf_op jit(solution)/shard_map/ppermute | solution.py:395
  91.7 15.0 %collective-permute-start.5 = (bf16[224,128]{1,0:T(8,128)(2,1)S(1)}, bf16[224,128]{1,0:T(8,128)(2,1)S(1)}, u32[]{:S(2)}, u32[]{:S(2)}) collective-permute-start(bf16[224,128]{1,0:T(8,128)(2,1)S(1)} %get-tuple-element.34), channel_id=1, source_target_pairs={{1,2},{3,4},{5,6},{7,8},{9,10},{11,12},{13,14},{15,0},{2,1},{4,3},... | collective-permute-start | bytes 172040 | tf_op jit(solution)/shard_map/ppermute | solution.py:394
  96.0 22.3 %all-to-all-start.3 = ((bf16[32,64,128]{2,1,0:T(8,128)(2,1)}), bf16[32,64,128]{2,1,0:T(8,128)(2,1)S(1)}, u32[]{:S(2)}, u32[]{:S(2)}) async-start(bf16[32,64,128]{2,1,0:T(8,128)(2,1)} %shard_map.110), calls=%async_computation.3 | async-start | bytes 1048576 | tf_op jit(solution)/shard_map/all_to_all | solution.py:321

commit v6 on v5

--- a/solution.py
+++ b/solution.py
@@ -277,7 +277,7 @@
             out[group * 4 + 3] = last[:, :CHANS]
 
 
-def conv_kernel(blocks, from_chip, far, from_core, weight, turned_weight, out, back, patches):
+def conv_kernel(blocks, from_core, far, from_chip, weight, turned_weight, out, back, patches):
     low, first = lower_half(), first_core()
     mine = blocks[:, pl.ds(64, 48), :].astype(F32)
     core, chip = from_core[...].astype(F32), from_chip[...].astype(F32)
@@ -391,8 +391,8 @@
         piece = lax.dynamic_slice(blocks, (start, 64, 0), (4, 32, LANES))
         return jnp.concatenate([piece.reshape(LANES, LANES), far], axis=0)
 
+    from_core = lax.ppermute(edge_of(12 * (1 - core)), "c", swap)
     from_chip = lax.ppermute(edge_of(12 * core), SECTOR, chips)
-    from_core = lax.ppermute(edge_of(12 * (1 - core)), "c", swap)
     out, back = pl.pallas_call(
         conv_kernel,
         out_shape=(struct((2, CHANS, LANES), BF16),) * 2,
@@ -400,7 +400,7 @@
         scratch_shapes=[pltpu.VMEM((9 * CHANS, LANES), BF16)],
         compiler_params=params,
         cost_estimate=pl.CostEstimate(flops=10**11, bytes_accessed=2**21, transcendentals=0),
-    )(blocks, from_chip, far, from_core, conv_weight, turned_weight)
+    )(blocks, from_core, far, from_chip, conv_weight, turned_weight)
     out, back = out.transpose(1, 0, 2), back.transpose(1, 0, 2)
 
     grad_weight = whole(

time: 120 us -> 118 us (0.983)
  starting transfers between devices: 63.7 us -> 61.4 us
    all_to_all x3, starting transfers between devices: 21.5 us -> 15 us  [exchange(): return lax.all_to_all(cells, axis, 0, 0, tiled=True)]
    ppermute x1, starting transfers between devices: 3.44 us -> 6.42 us  [shards(): from_chip = lax.ppermute(edge_of(12 * core), SECTOR, chips)]
where the time goes in v6:
time: 118 us; the launch traced here: 117 us
  starting transfers between devices  61.4 us (52%)
  waiting for transfers between devices  26.5 us (22%)
  blocking collectives  12.6 us (11%)
  Pallas kernels  12.5 us (11%)
  local copies, waits for them, and re-layouts  3.36 us (3%)
    all_to_all x3, waiting for transfers between devices, exchange(): return lax.all_to_all(cells, axis, 0, 0, tiled=True)  16.7 us
    ppermute x1, starting transfers between devices, shards(): partner = lax.ppermute(mine, 'zh', swap)  16.3 us
    all_to_all x3, starting transfers between devices, exchange(): return lax.all_to_all(cells, axis, 0, 0, tiled=True)  15 us
    all_to_all x1, blocking collectives, exchange(): return lax.all_to_all(cells, axis, 0, 0, tiled=True)  12.6 us
    ppermute x1, starting transfers between devices, shards(): got = lax.ppermute(send, 'c', swap)  9.17 us
    ppermute x1, starting transfers between devices, shards(): from_chip = lax.ppermute(edge_of(12 * core), SECTOR, chips)  6.42 us
    ppermute x1, starting transfers between devices, shards(): from_core = lax.ppermute(edge_of(12 * (1 - core)), 'c', swap)  6.04 us
    ppermute x1, waiting for transfers between devices, shards(): lax.ppermute(partner[2 * CHANS + 16:], FACE, [(0, face - 1), (face - 1, 0)])  4.81 us
  transfers between devices with their start and end apart: 10, of which 5 were waited for; matrix products, arithmetic and copies ran while one was open for 1% of the time, Pallas kernels for 3%

profile of v6, /device:TPU:1, one launch (start us, length us, event | category | flops | bytes accessed | tf_op | source)
XLA Modules:
  0.0 117.1 jit_solution(12899837647042041640)
XLA Ops:
  0.6 0.0 copy-start
  0.6 2.1 %shard_map.103 = (bf16[304,128]{1,0:T(8,128)(2,1)}, bf16[2,96,128]{2,1,0:T(8,128)(2,1)}, bf16[2,96,32]{2,1,0:T(8,128)(2,1)}, bf16[2,96,32]{2,1,0:T(8,128)(2,1)}) custom-call(bf16[96,2,128]{2,1,0:T(2,128)(2,1)} %feats_hbm.1, s32[2,128]{1,0:T(2,128)} %counts_hbm.1, s32[2,128]{1,0:T(2,128)} %bitcast.17, s32[1,2]{1,0:T(1,128)} %bitcast.18, ...), custom_call_target="tpu_custom_call" | custom-call | tf_op jit(solution)/shard_map/pallas_call | solution.py:335
  2.7 16.3 %collective-permute-start = (bf16[304,128]{1,0:T(8,128)(2,1)}, bf16[304,128]{1,0:T(8,128)(2,1)S(1)}, u32[]{:S(2)}, u32[]{:S(2)}) collective-permute-start(bf16[304,128]{1,0:T(8,128)(2,1)} %get-tuple-element.14.mine), channel_id=1, source_target_pairs={{0,256},{256,0},{1,257},{257,1},{2,258},{258,2},{3,259},{259,3},{4... | collective-permute-start | bytes 233480 | tf_op jit(solution)/shard_map/ppermute | solution.py:348
  19.0 2.9 %collective-permute-start.1 = (bf16[2,96,32]{2,1,0:T(8,128)(2,1)}, bf16[2,96,32]{2,1,0:T(8,128)(2,1)S(1)}, u32[]{:S(2)}, u32[]{:S(2)}) collective-permute-start(bf16[2,96,32]{2,1,0:T(8,128)(2,1)} %get-tuple-element.16), channel_id=1, source_target_pairs={{0,1},{1,0},{2,3},{3,2},{4,5},{5,4},{6,7},{7,6},{8,9},{9,8},{10,11... | collective-permute-start | bytes 36872 | tf_op jit(solution)/shard_map/ppermute | solution.py:349
  21.9 2.5 %collective-permute-start.2 = (bf16[2,96,32]{2,1,0:T(8,128)(2,1)}, bf16[2,96,32]{2,1,0:T(8,128)(2,1)S(1)}, u32[]{:S(2)}, u32[]{:S(2)}) collective-permute-start(bf16[2,96,32]{2,1,0:T(8,128)(2,1)} %get-tuple-element.17), channel_id=1, source_target_pairs={{1,2},{3,4},{5,6},{7,8},{9,10},{11,12},{13,14},{15,0},{2,1},{4,3},... | collective-permute-start | bytes 36872 | tf_op jit(solution)/shard_map/ppermute | solution.py:350
  24.4 0.0 collective-permute-done.1.from_core
  24.4 3.8 %collective-permute-done.2.from_chip = bf16[2,96,32]{2,1,0:T(8,128)(2,1)S(1)} collective-permute-done((bf16[2,96,32]{2,1,0:T(8,128)(2,1)}, bf16[2,96,32]{2,1,0:T(8,128)(2,1)S(1)}, u32[]{:S(2)}, u32[]{:S(2)}) %collective-permute-start.2) | collective-permute-done | bytes 12320 | tf_op jit(solution)/shard_map/ppermute | solution.py:350
  28.3 0.0 copy-start.1
  28.3 0.9 copy-done.1
  29.2 0.0 copy-start.3
  29.2 0.8 copy-done.3
  30.0 0.9 shard_map.104.loads_hbm
  30.9 0.0 copy-start.2
  30.9 0.0 copy-start.4
  30.9 0.0 collective-permute-done.partner_hbm
  30.9 0.8 shard_map.105
  31.7 6.8 %all-to-all-start = ((bf16[16,96,128]{2,1,0:T(8,128)(2,1)}), bf16[16,96,128]{2,1,0:T(8,128)(2,1)S(1)}, u32[]{:S(2)}, u32[]{:S(2)}) async-start(bf16[16,96,128]{2,1,0:T(8,128)(2,1)} %shard_map.105), calls=%async_computation | async-start | bytes 786432 | tf_op jit(solution)/shard_map/all_to_all | solution.py:321
  38.5 0.0 copy-done
  38.5 0.3 copy.14
  38.9 7.9 %all-to-all-done.loads = bf16[16,96,128]{2,1,0:T(8,128)(2,1)S(1)} async-done(((bf16[16,96,128]{2,1,0:T(8,128)(2,1)}), bf16[16,96,128]{2,1,0:T(8,128)(2,1)S(1)}, u32[]{:S(2)}, u32[]{:S(2)}) %all-to-all-start) | async-done | bytes 393248 | tf_op jit(solution)/shard_map/all_to_all | solution.py:321
  46.8 0.0 copy-done.2
  46.8 0.0 copy-done.4
  46.8 4.3 %shard_map.106 = (bf16[16,112,128]{2,1,0:T(8,128)(2,1)S(1)}, bf16[16,64,128]{2,1,0:T(8,128)(2,1)S(1)}) custom-call(bf16[16,96,128]{2,1,0:T(8,128)(2,1)S(1)} %all-to-all-done.loads, bf16[288,96]{1,0:T(8,128)(2,1)S(1)} %copy-done.2, bf16[96,96]{1,0:T(8,128)(2,1)S(1)} %copy-done.4, bf16[3,96,864]{2,1,0:T(8,128)(2,1)S(1)} %bitcast.10), custom_call_target="tpu_custom_call" | custom-call | tf_op jit(solution)/shard_map/pallas_call | solution.py:368
  51.1 9.2 %collective-permute-start.3 = (bf16[16,64,128]{2,1,0:T(8,128)(2,1)S(1)}, bf16[16,64,128]{2,1,0:T(8,128)(2,1)S(1)}, u32[]{:S(2)}, u32[]{:S(2)}) collective-permute-start(bf16[16,64,128]{2,1,0:T(8,128)(2,1)S(1)} %get-tuple-element.19), channel_id=1, source_target_pairs={{0,1},{1,0},{2,3},{3,2},{4,5},{5,4},{6,7},{7,6},{8,9},{9,8},{10,11... | collective-permute-start | bytes 786440 | tf_op jit(solution)/shard_map/ppermute | solution.py:381
  60.2 1.1 collective-permute-done.3.got
  61.4 0.1 shard_map.107
  61.4 12.6 %all_to_all.20.terms.blocks = bf16[16,112,128]{2,1,0:T(8,128)(2,1)S(1)} all-to-all(bf16[16,112,128]{2,1,0:T(8,128)(2,1)S(1)} %shard_map.107), channel_id=1, replica_groups=mesh['zh'=2,'y'=4,'x'=4,'zl'=8,'c'=2] {'y','x'}, dimensions={0} | all-to-all | bytes 917504 | tf_op jit(solution)/shard_map/all_to_all | solution.py:321
  74.0 0.8 shard_map.108
  74.8 4.1 %all-to-all-start.2 = ((bf16[16,64,128]{2,1,0:T(8,128)(2,1)}), bf16[16,64,128]{2,1,0:T(8,128)(2,1)S(1)}, u32[]{:S(2)}, u32[]{:S(2)}) async-start(bf16[16,64,128]{2,1,0:T(8,128)(2,1)} %shard_map.108), calls=%async_computation.2 | async-start | bytes 524288 | tf_op jit(solution)/shard_map/all_to_all | solution.py:321
  78.9 3.0 %collective-permute-start.4 = (bf16[96,128]{1,0:T(8,128)(2,1)S(1)}, bf16[96,128]{1,0:T(8,128)(2,1)S(1)}, u32[]{:S(2)}, u32[]{:S(2)}) collective-permute-start(bf16[96,128]{1,0:T(8,128)(2,1)S(1)} %slice.3), channel_id=1, source_target_pairs={{0,240},{240,0},{1,241},{241,1},{2,242},{242,2},{3,243},{243,3},{4... | collective-permute-start | bytes 73736 | tf_op jit(solution)/shard_map/ppermute | solution.py:388
  81.9 4.8 %collective-permute-done.4.far = bf16[96,128]{1,0:T(8,128)(2,1)S(1)} collective-permute-done((bf16[96,128]{1,0:T(8,128)(2,1)S(1)}, bf16[96,128]{1,0:T(8,128)(2,1)S(1)}, u32[]{:S(2)}, u32[]{:S(2)}) %collective-permute-start.4) | collective-permute-done | bytes 24608 | tf_op jit(solution)/shard_map/ppermute | solution.py:388
  86.8 6.4 %collective-permute-start.6 = (bf16[224,128]{1,0:T(8,128)(2,1)S(1)}, bf16[224,128]{1,0:T(8,128)(2,1)S(1)}, u32[]{:S(2)}, u32[]{:S(2)}) collective-permute-start(bf16[224,128]{1,0:T(8,128)(2,1)S(1)} %get-tuple-element.33), channel_id=1, source_target_pairs={{1,2},{3,4},{5,6},{7,8},{9,10},{11,12},{13,14},{15,0},{2,1},{4,3},... | collective-permute-start | bytes 172040 | tf_op jit(solution)/shard_map/ppermute | solution.py:395
  93.2 6.0 %collective-permute-start.5 = (bf16[224,128]{1,0:T(8,128)(2,1)S(1)}, bf16[224,128]{1,0:T(8,128)(2,1)S(1)}, u32[]{:S(2)}, u32[]{:S(2)}) collective-permute-start(bf16[224,128]{1,0:T(8,128)(2,1)S(1)} %get-tuple-element.34), channel_id=1, source_target_pairs={{0,1},{1,0},{2,3},{3,2},{4,5},{5,4},{6,7},{7,6},{8,9},{9,8},{10,11... | collective-permute-start | bytes 172040 | tf_op jit(solution)/shard_map/ppermute | solution.py:394
  99.2 0.0 all-to-all-done.2.terms
  99.2 0.9 shard_map.110
  100.1 4.2 %all-to-all-start.3 = ((bf16[32,64,128]{2,1,0:T(8,128)(2,1)}), bf16[32,64,128]{2,1,0:T(8,128)(2,1)S(1)}, u32[]{:S(2)}, u32[]{:S(2)}) async-start(bf16[32,64,128]{2,1,0:T(8,128)(2,1)} %shard_map.110), calls=%async_computation.3 | async-start | bytes 1048576 | tf_op jit(solution)/shard_map/all_to_all | solution.py:321
  104.3 0.0 collective-permute-done.6.from_chip
  104.3 0.0 collective-permute-done.5.from_core
  104.3 1.4 %shard_map.109 = (bf16[2,96,128]{2,1,0:T(8,128)(2,1)S(1)}, bf16[2,96,128]{2,1,0:T(8,128)(2,1)S(1)}) custom-call(bf16[16,112,128]{2,1,0:T(8,128)(2,1)S(1)} %all_to_all.20.terms.blocks, bf16[224,128]{1,0:T(8,128)(2,1)S(1)} %collective-permute-done.5.from_core, bf16[96,128]{1,0:T(8,128)(2,1)S(1)} %collective-permute-done.4.far, ...), custom_call_target="tpu_custom_call" | custom-call | flops 99999997952 | bytes 2097152 | tf_op jit(solution)/shard_map/pallas_call | solution.py:396
  105.8 0.7 copy.15
  106.4 0.7 copy.16
  107.1 8.8 %all-to-all-done.3 = bf16[32,64,128]{2,1,0:T(8,128)(2,1)S(1)} async-done(((bf16[32,64,128]{2,1,0:T(8,128)(2,1)}), bf16[32,64,128]{2,1,0:T(8,128)(2,1)S(1)}, u32[]{:S(2)}, u32[]{:S(2)}) %all-to-all-start.3) | async-done | bytes 524320 | tf_op jit(solution)/shard_map/all_to_all | solution.py:321
  115.8 1.3 %shard_map.111 = f32[27,96,96]{2,1,0:T(8,128)} custom-call(bf16[2048,128]{1,0:T(8,128)(2,1)S(1)} %bitcast.9), custom_call_target="tpu_custom_call" | custom-call | tf_op jit(solution)/shard_map/pallas_call | solution.py:25
  (3 shorter events, 0.0 us)
Async XLA Ops:
  0.6 37.9 %copy-start = (bf16[27,96,96]{2,1,0:T(8,128)(2,1)S(1)}, bf16[27,96,96]{2,1,0:T(8,128)(2,1)}, u32[]{:S(2)}) copy-start(bf16[27,96,96]{2,1,0:T(8,128)(2,1)} %weight.1) | copy-start | bytes 1492996
  2.7 28.2 %collective-permute-start = (bf16[304,128]{1,0:T(8,128)(2,1)}, bf16[304,128]{1,0:T(8,128)(2,1)S(1)}, u32[]{:S(2)}, u32[]{:S(2)}) collective-permute-start(bf16[304,128]{1,0:T(8,128)(2,1)} %get-tuple-element.14.mine), channel_id=1, source_target_pairs={{0,256},{256,0},{1,257},{257,1},{2,258},{258,2},{3,259},{259,3},{4... | collective-permute-start | bytes 233480 | tf_op jit(solution)/shard_map/ppermute | solution.py:348
  19.0 5.4 %collective-permute-start.1 = (bf16[2,96,32]{2,1,0:T(8,128)(2,1)}, bf16[2,96,32]{2,1,0:T(8,128)(2,1)S(1)}, u32[]{:S(2)}, u32[]{:S(2)}) collective-permute-start(bf16[2,96,32]{2,1,0:T(8,128)(2,1)} %get-tuple-element.16), channel_id=1, source_target_pairs={{0,1},{1,0},{2,3},{3,2},{4,5},{5,4},{6,7},{7,6},{8,9},{9,8},{10,11... | collective-permute-start | bytes 36872 | tf_op jit(solution)/shard_map/ppermute | solution.py:349
  21.9 6.4 %collective-permute-start.2 = (bf16[2,96,32]{2,1,0:T(8,128)(2,1)}, bf16[2,96,32]{2,1,0:T(8,128)(2,1)S(1)}, u32[]{:S(2)}, u32[]{:S(2)}) collective-permute-start(bf16[2,96,32]{2,1,0:T(8,128)(2,1)} %get-tuple-element.17), channel_id=1, source_target_pairs={{1,2},{3,4},{5,6},{7,8},{9,10},{11,12},{13,14},{15,0},{2,1},{4,3},... | collective-permute-start | bytes 36872 | tf_op jit(solution)/shard_map/ppermute | solution.py:350
  28.3 0.9 copy-start.1
  29.2 0.8 copy-start.3
  30.9 15.9 %copy-start.2 = (bf16[288,96]{1,0:T(8,128)(2,1)S(1)}, bf16[288,96]{1,0:T(8,128)(2,1)}, u32[]{:S(2)}) copy-start(bf16[288,96]{1,0:T(8,128)(2,1)} %w_qkv_hbm.1) | copy-start | bytes 165892
  30.9 15.9 %copy-start.4 = (bf16[96,96]{1,0:T(8,128)(2,1)S(1)}, bf16[96,96]{1,0:T(8,128)(2,1)}, u32[]{:S(2)}) copy-start(bf16[96,96]{1,0:T(8,128)(2,1)} %w_out_hbm.1) | copy-start | bytes 55300
  31.7 15.0 %all-to-all-start = ((bf16[16,96,128]{2,1,0:T(8,128)(2,1)}), bf16[16,96,128]{2,1,0:T(8,128)(2,1)S(1)}, u32[]{:S(2)}, u32[]{:S(2)}) async-start(bf16[16,96,128]{2,1,0:T(8,128)(2,1)} %shard_map.105), calls=%async_computation | async-start | bytes 786432 | tf_op jit(solution)/shard_map/all_to_all | solution.py:321
  51.1 10.3 %collective-permute-start.3 = (bf16[16,64,128]{2,1,0:T(8,128)(2,1)S(1)}, bf16[16,64,128]{2,1,0:T(8,128)(2,1)S(1)}, u32[]{:S(2)}, u32[]{:S(2)}) collective-permute-start(bf16[16,64,128]{2,1,0:T(8,128)(2,1)S(1)} %get-tuple-element.19), channel_id=1, source_target_pairs={{0,1},{1,0},{2,3},{3,2},{4,5},{5,4},{6,7},{7,6},{8,9},{9,8},{10,11... | collective-permute-start | bytes 786440 | tf_op jit(solution)/shard_map/ppermute | solution.py:381
  74.8 24.5 %all-to-all-start.2 = ((bf16[16,64,128]{2,1,0:T(8,128)(2,1)}), bf16[16,64,128]{2,1,0:T(8,128)(2,1)S(1)}, u32[]{:S(2)}, u32[]{:S(2)}) async-start(bf16[16,64,128]{2,1,0:T(8,128)(2,1)} %shard_map.108), calls=%async_computation.2 | async-start | bytes 524288 | tf_op jit(solution)/shard_map/all_to_all | solution.py:321
  78.9 7.9 %collective-permute-start.4 = (bf16[96,128]{1,0:T(8,128)(2,1)S(1)}, bf16[96,128]{1,0:T(8,128)(2,1)S(1)}, u32[]{:S(2)}, u32[]{:S(2)}) collective-permute-start(bf16[96,128]{1,0:T(8,128)(2,1)S(1)} %slice.3), channel_id=1, source_target_pairs={{0,240},{240,0},{1,241},{241,1},{2,242},{242,2},{3,243},{243,3},{4... | collective-permute-start | bytes 73736 | tf_op jit(solution)/shard_map/ppermute | solution.py:388
  86.8 17.5 %collective-permute-start.6 = (bf16[224,128]{1,0:T(8,128)(2,1)S(1)}, bf16[224,128]{1,0:T(8,128)(2,1)S(1)}, u32[]{:S(2)}, u32[]{:S(2)}) collective-permute-start(bf16[224,128]{1,0:T(8,128)(2,1)S(1)} %get-tuple-element.33), channel_id=1, source_target_pairs={{1,2},{3,4},{5,6},{7,8},{9,10},{11,12},{13,14},{15,0},{2,1},{4,3},... | collective-permute-start | bytes 172040 | tf_op jit(solution)/shard_map/ppermute | solution.py:395
  93.2 11.1 %collective-permute-start.5 = (bf16[224,128]{1,0:T(8,128)(2,1)S(1)}, bf16[224,128]{1,0:T(8,128)(2,1)S(1)}, u32[]{:S(2)}, u32[]{:S(2)}) collective-permute-start(bf16[224,128]{1,0:T(8,128)(2,1)S(1)} %get-tuple-element.34), channel_id=1, source_target_pairs={{0,1},{1,0},{2,3},{3,2},{4,5},{5,4},{6,7},{7,6},{8,9},{9,8},{10,11... | collective-permute-start | bytes 172040 | tf_op jit(solution)/shard_map/ppermute | solution.py:394
  100.1 15.7 %all-to-all-start.3 = ((bf16[32,64,128]{2,1,0:T(8,128)(2,1)}), bf16[32,64,128]{2,1,0:T(8,128)(2,1)S(1)}, u32[]{:S(2)}, u32[]{:S(2)}) async-start(bf16[32,64,128]{2,1,0:T(8,128)(2,1)} %shard_map.110), calls=%async_computation.3 | async-start | bytes 1048576 | tf_op jit(solution)/shard_map/all_to_all | solution.py:321
